TPU v7x, 256 devices: a whole 4x4x8 slice. The times are simulated.
256 devices in a mesh: tile: 64 (over x, y, z_lo, core), lev: 4 (over z_hi).
Axes of the slice: x: 4, y: 4, z: 8 (z_hi: 4, z_lo: 2; z = z_hi * 2 + z_lo), core: 2. Of those that a mesh axis runs over, the one named last changes fastest.
Arguments:
- tracer: float32 [2, 72, 128, 512], P(None, 'lev', 'tile'), may hold values from -6 to 6
- u_courant: float32 [72, 128, 512], P('lev', 'tile'), may hold values from -0.45 to 0.45
- v_courant: float32 [72, 128, 512], P('lev', 'tile'), may hold values from -0.45 to 0.45
- surface_flux: float32 [2, 128, 512], P(None, 'tile'), may hold values from -6 to 6
- mixing: float32 [72, 72], replicated, may hold values from 0 to 1
- kernel: float32 [72, 262144], P('lev', 'tile'), may hold values from 0.1 to 1
- column: int32 [262144], P('tile'), may hold values from 0 to 1023
- owner_tile: int32 [262144], P('tile'), may hold values from 0 to 63, as said below
- offset: int32 [262144], P('tile'), may hold values from 0 to 23
- counts: int32 [64], P('tile'), may hold values from 2048 to 4096, as said below
Outputs:
- transported: float32 [2, 72, 128, 512], P(None, 'lev', 'tile')
- evolved: float32 [2, 262144], P(None, 'tile')
Inputs may be any that keep to these rules, and one draw needn't show every extreme that they name: `owner_tile`: among the rows of one device, no owner tile is named by more than 192 rows; one owner tile, the same for every device, is named by exactly 192 rows of each device. Rows at position counts[t] and beyond in tile t's block of soundings are unused.
All inputs are finite; a program needn't handle non-finite values.
Results may differ from a plain program's by a relative error of at most 0.0003.
Values sent between devices are 32-bit elements; how exact they have to be, the bound alone decides.
No kernel may reach another device: no remote copies, remote signals or barrier semaphores. Data moves between devices by JAX's collectives and lax.ppermute only.
A program may use at most 64 MiB of HBM per device.

v0:
```python
import jax
import jax.numpy as jnp
from jax import lax
from jax.sharding import PartitionSpec as P

NSUB = 2


def from_behind(block, axis, distance):
    devices = range(lax.axis_size(axis))
    route = [((i - distance) % len(devices), i) for i in devices]
    return lax.ppermute(block, axis, route)


def padded(shard, sides, width):
    for axis, dim in sides:
        size, length = (lax.axis_size(axis), shard.shape[dim])
        up = [(i, (i + 1) % size) for i in range(size)]
        down = [(j, i) for i, j in up]
        last = lax.slice_in_dim(shard, length - width, length, axis=dim)
        initial = lax.slice_in_dim(shard, 0, width, axis=dim)
        before = lax.ppermute(last, axis, up)
        after = lax.ppermute(initial, axis, down)
        shard = jnp.concatenate([before, shard, after], axis=dim)
    return shard


def substep(extended, wind_u, wind_v):
    centre = extended[:, :, 1:-1]
    west_cells = extended[:, :, :-2]
    east_cells = extended[:, :, 2:]
    wind_west = wind_u[:, 1:-1]
    wind_east = wind_u[:, 2:]
    wind_lat = wind_v[:, 1:-1]
    flux_west = wind_west * jnp.where(wind_west > 0, west_cells, centre)
    flux_east = wind_east * jnp.where(wind_east > 0, centre, east_cells)
    south_cells = jnp.concatenate([jnp.zeros_like(centre[..., :1]), centre[..., :-1]], axis=-1)
    lat_ids = lax.broadcasted_iota(jnp.int32, wind_lat.shape, 2)
    open_face = jnp.where(lat_ids > 0, wind_lat, jnp.zeros_like(wind_lat))
    flux_south = open_face * jnp.where(wind_lat > 0, south_cells, centre)
    flux_north = jnp.concatenate(
        [flux_south[..., 1:], jnp.zeros_like(flux_south[..., :1])], axis=-1
    )
    return centre - (flux_east - flux_west) - (flux_north - flux_south)


def body(
    tracer, u_courant, v_courant, surface_flux, mixing, kernel, column, owner_tile, offset, counts
):
    scen_count, level_here, lon_here, lat_count = tracer.shape
    lev_id = lax.axis_index("lev")
    on_ground = (lev_id == 0).astype(jnp.float32)
    advected = tracer.at[:, 0].add(on_ground * surface_flux)
    east_column = from_behind(u_courant[:, :1], "tile", -1)
    wind_u_ext = jnp.concatenate([u_courant[:, :1], u_courant, east_column], axis=1)
    wind_v_ext = jnp.concatenate([v_courant[:, :1], v_courant, v_courant[:, :1]], axis=1)
    for sub_step in range(NSUB):
        extended = padded(advected, (("tile", 2),), 1)
        advected = substep(extended, wind_u_ext, wind_v_ext)
    my_rows = lax.dynamic_slice_in_dim(mixing, lev_id * level_here, level_here, 0)
    transported = jnp.einsum(
        "kl,slxy->skxy",
        my_rows,
        lax.all_gather(advected, "lev", axis=1, tiled=True),
        precision=lax.Precision.HIGHEST,
    )
    snd_here = column.shape[0]
    tile_count = lax.axis_size("tile")
    slot_cap = 3 * snd_here // tile_count
    buffer_len = tile_count * slot_cap
    positions = jnp.arange(snd_here, dtype=jnp.int32)
    in_use = positions < counts[0]
    onehot = (owner_tile[:, None] == jnp.arange(tile_count, dtype=jnp.int32)[None, :]).astype(
        jnp.int32
    )
    rank_ids = jnp.sum(jnp.cumsum(onehot, axis=0) * onehot, axis=1) - 1
    slot_ids = jnp.where(in_use, owner_tile * slot_cap + rank_ids, buffer_len)
    level_ids = lev_id * level_here + jnp.arange(level_here, dtype=jnp.int32)
    weighted = jnp.where(level_ids[:, None] >= offset[None, :], kernel, jnp.zeros_like(kernel))
    denominator = jnp.sum(weighted, axis=0)
    source_ids = (
        jnp.full((buffer_len,), snd_here, jnp.int32).at[slot_ids].set(positions, mode="drop")
    )
    filled = source_ids < snd_here
    safe_ids = jnp.minimum(source_ids, snd_here - 1)
    weight_rows = jnp.take(weighted.T, safe_ids, axis=0)
    send_weights = jnp.where(filled[:, None], weight_rows, jnp.zeros_like(weight_rows))
    column_rows = jnp.take(column, safe_ids, axis=0).astype(jnp.float32)
    send_columns = jnp.where(filled, column_rows, jnp.zeros_like(column_rows))[:, None]
    got_weights, got_columns = (
        lax.all_to_all(send_weights, "tile", split_axis=0, concat_axis=0, tiled=True),
        lax.all_to_all(send_columns, "tile", split_axis=0, concat_axis=0, tiled=True),
    )
    column_ids = got_columns[:, 0].astype(jnp.int32)
    field_rows = transported.reshape(scen_count * level_here, lon_here * lat_count).T
    picked = jnp.take(field_rows, column_ids, axis=0).reshape(buffer_len, scen_count, level_here)
    partial_sums = jnp.sum(picked * got_weights[:, None, :], axis=2)
    returned_sums = lax.all_to_all(partial_sums, "tile", split_axis=0, concat_axis=0, tiled=True)
    own_sums = jnp.take(returned_sums, jnp.minimum(slot_ids, buffer_len - 1), axis=0).T
    numerator, total_weight = lax.psum((own_sums, denominator), "lev")
    evolved = jnp.where(
        in_use[None, :], numerator / total_weight[None, :], jnp.zeros_like(numerator)
    )
    return (transported, evolved)


def solution(mesh):
    in_specs = (
        P(None, "lev", "tile", None),
        P("lev", "tile", None),
        P("lev", "tile", None),
        P(None, "tile", None),
        P(),
        P("lev", "tile"),
        P("tile"),
        P("tile"),
        P("tile"),
        P("tile"),
    )
    out_specs = (P(None, "lev", "tile", None), P(None, "tile"))
    return jax.shard_map(body, mesh=mesh, in_specs=in_specs, out_specs=out_specs, check_vma=False)
```

profile of v0, /device:TPU:1, one launch (start us, length us, event | category | flops | bytes accessed | tf_op | source)
XLA Modules:
  0.0 413.5 jit_solution(3378710399320378499)
XLA Ops:
  0.6 0.9 slice.83
  1.6 3.3 collective-permute-start
  4.9 0.9 copy.56
  5.8 0.7 fusion.26
  6.6 4.3 %collective-permute-start.1 = (f32[2,18,1,512]{3,2,0,1:T(1,128)S(1)}, f32[2,18,1,512]{3,2,0,1:T(1,128)S(1)}, u32[]{:S(2)}, u32[]{:S(2)}) collective-permute-start(f32[2,18,1,512]{3,2,0,1:T(1,128)S(1)} %get-tuple-element.35), channel_id=1, source_target_pairs={{4,0},{8,4},{12,8},{16,12},{20,16},{24,20},{28,24},{32,28},{36,32}... | collective-permute-start | bytes 221192 | tf_op jit(solution)/shard_map/ppermute | solution.py:23
  11.6 0.8 fusion.4
  12.5 18.4 %reduce-window.6 = s32[64,32,128]{2,1,0:T(8,128)S(1)} reduce-window(s32[64,32,128]{2,1,0:T(8,128)S(1)} %fusion.4, s32[]{:T(128)} %constant.102.clone.1), window={size=1x1x128 pad=0_0x0_0x127_0}, to_apply=%region_0.0 | reduce-window | flops 33292288 | bytes 2097156 | tf_op jit(solution)/shard_map/reduce-window
  30.9 0.3 slice.116
  31.3 0.4 copy.72
  31.7 0.2 reduce-window.9
  31.9 0.3 broadcast_add_fusion
  32.3 0.8 fusion.3
  33.2 15.5 %scatter_custom_fusion = s32[12288]{0:T(1024)S(1)} fusion(s32[4096]{0:T(1024)S(1)} %get-tuple-element.39, s32[4096]{0:T(1024)S(1)} %iota.31, s32[]{:T(128)} %constant.110.clone.1), kind=kCustom, calls=%fused_computation.58 | custom fusion | bytes 49156 | tf_op jit(solution)/shard_map/scatter | solution.py:82
  48.8 68.0 %gather_fusion = s32[12288]{0:T(1024)S(1)} fusion(s32[4096]{0:T(1024)S(1)} %copy-done.1, s32[12288]{0:T(1024)S(1)} %fusion.20), kind=kCustom, calls=%fused_computation | custom fusion | bytes 147456 | tf_op jit(solution)/shard_map/jit(_take)/gather | solution.py:88
  116.9 0.8 all_to_all.24
  117.6 8.5 %all-to-all-start = ((f32[64,192,1]{1,2,0:T(1,128)}), f32[64,192,1]{1,2,0:T(1,128)S(1)}, u32[]{:S(2)}, u32[]{:S(2)}) async-start(f32[64,192,1]{1,2,0:T(1,128)} %all_to_all.24), calls=%async_computation | async-start | bytes 131072 | tf_op jit(solution)/shard_map/all_to_all | solution.py:92
  126.4 2.0 copy.64
  128.4 2.5 fusion
  130.9 41.3 %gather_fusion.2 = f32[12288,18]{1,0:T(8,128)} fusion(f32[4096,18]{1,0:T(8,128)S(1)} %get-tuple-element.32, s32[12288]{0:T(1024)S(1)} %fusion.20), kind=kCustom, calls=%fused_computation.2 | custom fusion | bytes 1818624 | tf_op jit(solution)/shard_map/jit(_take)/gather | solution.py:86
  172.2 5.1 %copy.65 = f32[64,192,18]{1,2,0:T(8,128)S(1)} copy(f32[64,192,18]{2,1,0:T(8,128)} %bitcast.52) | data formatting | bytes 1769472 | tf_op jit(solution)/shard_map/jit(_take)/gather | solution.py:86
  177.3 1.5 select_select_fusion
  178.8 0.2 select_multiply_fusion.1
  179.1 0.2 slice.111
  179.5 0.5 fusion.17
  180.0 0.2 select_multiply_fusion
  180.4 0.2 slice.115
  180.6 0.5 collective-permute-start.3
  181.1 1.4 collective-permute-start.4
  182.6 12.4 %all-to-all-start.1 = ((f32[64,192,18]{1,2,0:T(8,128)}), f32[64,192,18]{1,2,0:T(8,128)}, u32[]{:S(2)}, u32[]{:S(2)}) async-start(f32[64,192,18]{1,2,0:T(8,128)} %select_select_fusion), calls=%async_computation.1 | async-start | bytes 3145728 | tf_op jit(solution)/shard_map/all_to_all | solution.py:91
  195.5 0.5 fusion.10
  196.0 32.4 %all_gather.3 = f32[2,72,2,512]{3,2,0,1:T(2,128)S(1)} all-gather(f32[2,18,2,512]{3,2,0,1:T(2,128)S(1)} %fusion.10), channel_id=1, replica_groups=mesh['tile'=64,'lev'=4] {'lev'}, dimensions={1}, use_global_device_ids=true | all-gather | bytes 737280 | tf_op jit(solution)/shard_map/all_gather | solution.py:64
  228.4 0.6 convolution_bitcast_fusion
  229.3 0.2 copy.62
  229.5 41.3 %gather_fusion.1 = f32[12288,36]{1,0:T(8,128)} fusion(f32[1024,36]{1,0:T(8,128)S(1)} %bitcast.50, s32[12288]{0:T(1024)S(1)} %broadcast_clamp_fusion), kind=kCustom, calls=%fused_computation.1 | custom fusion | bytes 3588096 | tf_op jit(solution)/shard_map/jit(_take)/gather | solution.py:96
  270.8 5.8 %copy.63 = f32[12288,36]{0,1:T(8,128)} copy(f32[12288,36]{1,0:T(8,128)} %gather_fusion.1) | data formatting | bytes 3538944 | tf_op jit(solution)/shard_map/jit(_take)/gather | solution.py:96
  276.5 1.7 gather.22
  278.3 2.8 copy.66
  281.1 2.8 mul.86
  283.9 1.9 multiply_reduce_fusion
  286.0 0.8 copy.67
  286.7 10.1 %all-to-all-start.2 = ((f32[64,192,2]{1,2,0:T(2,128)}), f32[64,192,2]{1,2,0:T(2,128)S(1)}, u32[]{:S(2)}, u32[]{:S(2)}) async-start(f32[64,192,2]{1,2,0:T(2,128)} %copy.67), calls=%async_computation.2 | async-start | bytes 262144 | tf_op jit(solution)/shard_map/all_to_all | solution.py:98
  296.9 8.5 %all-to-all-done.2 = f32[64,192,2]{1,2,0:T(2,128)S(1)} async-done(((f32[64,192,2]{1,2,0:T(2,128)}), f32[64,192,2]{1,2,0:T(2,128)S(1)}, u32[]{:S(2)}, u32[]{:S(2)}) %all-to-all-start.2) | async-done | bytes 98336 | tf_op jit(solution)/shard_map/all_to_all | solution.py:98
  305.4 4.1 copy.68
  309.5 17.0 %gather_fusion.3 = f32[4096,2]{1,0:T(8,128)} fusion(f32[12288,2]{1,0:T(8,128)} %bitcast.51, s32[4096]{0:T(1024)S(1)} %get-tuple-element.38), kind=kCustom, calls=%fused_computation.3 | custom fusion | bytes 81920 | tf_op jit(solution)/shard_map/jit(_take)/gather | solution.py:99
  326.5 3.6 select_bitcast_fusion
  330.1 79.0 %all-reduce.4 = (f32[2,4096]{0,1:T(8,128)}, f32[4096]{0:T(1024)S(1)}) all-reduce(f32[2,4096]{0,1:T(8,128)S(1)} %select_bitcast_fusion, f32[4096]{0:T(1024)S(1)} %get-tuple-element.31), channel_id=1, replica_groups=mesh['tile'=64,'lev'=4] {'lev'}, use_global_device_ids=true, to_apply=%region_5.6 | all-reduce | flops 12288 | bytes 98304 | tf_op jit(solution)/shard_map/psum | solution.py:100
  409.1 3.2 divide_select_fusion
  412.3 1.2 copy.70
  (49 shorter events, 1.6 us)
Async XLA Ops:
  0.6 227.8 %copy-start = (f32[72,72]{1,0:T(8,128)S(1)}, f32[72,72]{1,0:T(8,128)}, u32[]{:S(2)}) copy-start(f32[72,72]{1,0:T(8,128)} %param.16) | copy-start | bytes 62212
  1.6 177.7 %collective-permute-start = (f32[18,1,512]{2,1,0:T(1,128)S(1)}, f32[18,1,512]{2,1,0:T(1,128)S(1)}, u32[]{:S(2)}, u32[]{:S(2)}) collective-permute-start(f32[18,1,512]{2,1,0:T(1,128)S(1)} %slice.83), channel_id=1, source_target_pairs={{4,0},{8,4},{12,8},{16,12},{20,16},{24,20},{28,24},{32,28},{36,32}... | collective-permute-start | bytes 110600 | tf_op jit(solution)/shard_map/ppermute | solution.py:12
  6.6 172.8 %collective-permute-start.1 = (f32[2,18,1,512]{3,2,0,1:T(1,128)S(1)}, f32[2,18,1,512]{3,2,0,1:T(1,128)S(1)}, u32[]{:S(2)}, u32[]{:S(2)}) collective-permute-start(f32[2,18,1,512]{3,2,0,1:T(1,128)S(1)} %get-tuple-element.35), channel_id=1, source_target_pairs={{4,0},{8,4},{12,8},{16,12},{20,16},{24,20},{28,24},{32,28},{36,32}... | collective-permute-start | bytes 221192 | tf_op jit(solution)/shard_map/ppermute | solution.py:23
  11.0 168.5 %collective-permute-start.2 = (f32[2,18,1,512]{3,2,0,1:T(1,128)S(1)}, f32[2,18,1,512]{3,2,0,1:T(1,128)S(1)}, u32[]{:S(2)}, u32[]{:S(2)}) collective-permute-start(f32[2,18,1,512]{3,2,0,1:T(1,128)S(1)} %get-tuple-element.36), channel_id=1, source_target_pairs={{0,4},{4,8},{8,12},{12,16},{16,20},{20,24},{24,28},{28,32},{32,36}... | collective-permute-start | bytes 221192 | tf_op jit(solution)/shard_map/ppermute | solution.py:22
  31.3 1.0 copy-start.6
  31.3 17.5 %copy-start.1 = (s32[4096]{0:T(1024)S(1)}, s32[4096]{0:T(1024)}, u32[]{:S(2)}) copy-start(s32[4096]{0:T(1024)} %param.18) | copy-start | bytes 49156
  48.7 77.4 %copy-start.5 = (f32[18,2,512]{2,1,0:T(2,128)S(1)}, f32[18,2,512]{2,1,0:T(2,128)}, u32[]{:S(2)}) copy-start(f32[18,2,512]{2,1,0:T(2,128)} %param.14) | copy-start | bytes 221188
  48.8 77.7 %copy-start.4 = (f32[18,4096]{1,0:T(8,128)S(1)}, f32[18,4096]{1,0:T(8,128)}, u32[]{:S(2)}) copy-start(f32[18,4096]{1,0:T(8,128)} %param.17) | copy-start | bytes 884740
  116.8 11.6 %copy-start.7 = (s32[4096]{0:T(1024)S(1)}, s32[4096]{0:T(1024)}, u32[]{:S(2)}) copy-start(s32[4096]{0:T(1024)} %param.20) | copy-start | bytes 49156
  117.6 65.0 %all-to-all-start = ((f32[64,192,1]{1,2,0:T(1,128)}), f32[64,192,1]{1,2,0:T(1,128)S(1)}, u32[]{:S(2)}, u32[]{:S(2)}) async-start(f32[64,192,1]{1,2,0:T(1,128)} %all_to_all.24), calls=%async_computation | async-start | bytes 131072 | tf_op jit(solution)/shard_map/all_to_all | solution.py:92
  177.3 2.0 copy-start.2
  180.6 14.9 %collective-permute-start.3 = (f32[2,18,1,512]{3,2,0,1:T(1,128)S(1)}, f32[2,18,1,512]{3,2,0,1:T(1,128)S(1)}, u32[]{:S(2)}, u32[]{:S(2)}) collective-permute-start(f32[2,18,1,512]{3,2,0,1:T(1,128)S(1)} %get-tuple-element.33), channel_id=1, source_target_pairs={{4,0},{8,4},{12,8},{16,12},{20,16},{24,20},{28,24},{32,28},{36,32}... | collective-permute-start | bytes 221192 | tf_op jit(solution)/shard_map/ppermute | solution.py:23
  181.1 14.3 %collective-permute-start.4 = (f32[2,18,1,512]{3,2,0,1:T(1,128)S(1)}, f32[2,18,1,512]{3,2,0,1:T(1,128)S(1)}, u32[]{:S(2)}, u32[]{:S(2)}) collective-permute-start(f32[2,18,1,512]{3,2,0,1:T(1,128)S(1)} %get-tuple-element.34), channel_id=1, source_target_pairs={{0,4},{4,8},{8,12},{12,16},{16,20},{20,24},{24,28},{28,32},{32,36}... | collective-permute-start | bytes 221192 | tf_op jit(solution)/shard_map/ppermute | solution.py:22
  182.6 95.7 %all-to-all-start.1 = ((f32[64,192,18]{1,2,0:T(8,128)}), f32[64,192,18]{1,2,0:T(8,128)}, u32[]{:S(2)}, u32[]{:S(2)}) async-start(f32[64,192,18]{1,2,0:T(8,128)} %select_select_fusion), calls=%async_computation.1 | async-start | bytes 3145728 | tf_op jit(solution)/shard_map/all_to_all | solution.py:91
  229.2 41.6 %copy-start.3 = (f32[2,18,2,512]{3,2,1,0:T(2,128)}, f32[2,18,2,512]{3,2,1,0:T(2,128)S(1)}, u32[]{:S(2)}) copy-start(f32[2,18,2,512]{3,2,1,0:T(2,128)S(1)} %copy.69) | copy-start | bytes 442372
  286.7 18.7 %all-to-all-start.2 = ((f32[64,192,2]{1,2,0:T(2,128)}), f32[64,192,2]{1,2,0:T(2,128)S(1)}, u32[]{:S(2)}, u32[]{:S(2)}) async-start(f32[64,192,2]{1,2,0:T(2,128)} %copy.67), calls=%async_computation.2 | async-start | bytes 262144 | tf_op jit(solution)/shard_map/all_to_all | solution.py:98
where the time goes:
time: 414 us
  local copies, waits for them, and re-layouts  214 us (52%)
  blocking collectives  111 us (27%)
  starting transfers between devices  40.6 us (10%)
  other arithmetic  36.1 us (9%)
  waiting for transfers between devices  8.52 us (2%)
    psum x1, blocking collectives, body(): numerator, total_weight = lax.psum((own_sums, denominator), 'lev')  79 us
    gather x1, local copies, waits for them, and re-layouts, body(): column_rows = jnp.take(column, safe_ids, axis=0).astype(jnp.float32)  68 us
    gather x3, local copies, waits for them, and re-layouts, body(): jnp.take(field_rows, column_ids, axis=0)  48.8 us
    gather x2, local copies, waits for them, and re-layouts, body(): weight_rows = jnp.take(weighted.T, safe_ids, axis=0)  46.4 us
    all_gather x1, blocking collectives, body(): lax.all_gather(advected, 'lev', axis=1, tiled=True)  32.4 us
    another operation x3, other arithmetic  19 us
    gather x1, local copies, waits for them, and re-layouts, body(): jnp.take(returned_sums, jnp.minimum(slot_ids, buffer_len - 1), axis=0)  17 us
    scatter x1, local copies, waits for them, and re-layouts, body(): jnp.full((buffer_len,), snd_here, jnp.int32).at[slot_ids]  15.5 us
  transfers between devices with their start and end apart: 8, of which 1 were waited for; matrix products, arithmetic and copies ran while one was open for 51% of the time, Pallas kernels for 0%

commit v1 on v0

v1 whole, which is shorter than its diff:
```python
import jax
import jax.numpy as jnp
from jax import lax
from jax.experimental import pallas as pl
from jax.experimental.pallas import tpu as pltpu
from jax.sharding import PartitionSpec as P

LANES = 128
SUBS = 8
HERE = 18
ROWS = 24
TILES = 64
CAP = 192
SND = 4096
F32 = jnp.float32
BF16 = jnp.bfloat16
VMEM = pltpu.MemorySpace.VMEM
SMEM = pltpu.MemorySpace.SMEM


def params(mib):
    return pltpu.CompilerParams(vmem_limit_bytes=mib * 2**20)


def spec(space=VMEM):
    return pl.BlockSpec(memory_space=space)


def iota(shape, dim):
    return lax.broadcasted_iota(jnp.int32, shape, dim)


def split(x):
    high = x.astype(BF16)
    low = (x - high.astype(F32)).astype(BF16)
    return high, low


def roll(x, shift, axis):
    return pltpu.roll(x, shift % x.shape[axis], axis)


def swap(x, first):
    return jnp.where(first, roll(x, -1, 0), roll(x, 1, 0))


def inner(c, u, v, first):
    sub, lane = iota(c.shape, 0), iota(c.shape, 1)
    shifted = roll(c, 1, 1)
    south = jnp.where(lane == 0, roll(shifted, 2, 0), shifted)
    wall = (sub < 2) & (lane == 0)
    flux_south = jnp.where(wall, 0.0, v * jnp.where(v > 0, south, c))
    back = roll(flux_south, -1, 1)
    flux_north = jnp.where(lane == LANES - 1, roll(back, -2, 0), back)
    middle = u * jnp.where(u > 0, roll(c, 1, 0), c)
    return c - (flux_north - flux_south) + jnp.where(first, -roll(middle, -1, 0), middle)


def surfaced(c_ref, f_ref, s, level):
    c = c_ref[s * HERE + level]
    ground = (lax.axis_index("lev") == 0) & (level == 0)
    return c + jnp.where(ground, f_ref[s], 0.0)


def halo_kernel(c_ref, u_ref, v_ref, f_ref, east_ref, west_ref, part_ref):
    first = iota((SUBS, LANES), 0) % 2 == 0

    for level in range(HERE):
        u, v = u_ref[level], v_ref[level]
        for s in range(2):
            row = s * HERE + level
            c = c_ref[row]
            if level == 0:
                c = surfaced(c_ref, f_ref, s, level)
            y = inner(c, u, v, first)
            part_ref[row] = y
            east_ref[row] = jnp.where(first, roll(c, -1, 0), y)
            west_ref[row] = jnp.where(first, y, roll(c, 1, 0))
    for level in range(HERE // 2):
        west_ref[2 * HERE + level] = jnp.where(first, u_ref[level], roll(u_ref[level + HERE // 2], 1, 0))


def advect_kernel(c_ref, u_ref, v_ref, f_ref, part_ref, a_ref, b_ref, out_ref):
    first = iota((SUBS, LANES), 0) % 2 == 0
    for level in range(HERE):
        u, v = u_ref[level], v_ref[level]
        packed = b_ref[2 * HERE + level % (HERE // 2)]
        beyond = roll(packed, 1, 0) if level < HERE // 2 else packed
        outer = jnp.where(first, u, beyond)
        forward = outer > 0
        for s in range(2):
            row = s * HERE + level
            c = c_ref[row]
            if level == 0:
                c = surfaced(c_ref, f_ref, s, level)
            a, b = a_ref[row], b_ref[row]
            flux = outer * jnp.where(forward, jnp.where(first, a, c), jnp.where(first, c, b))
            own = part_ref[row] + jnp.where(first, flux, -flux)
            near = swap(jnp.where(first, b + roll(flux, -1, 0), a - roll(flux, 1, 0)), first)
            flux = outer * jnp.where(forward, jnp.where(first, near, own), jnp.where(first, own, near))
            out_ref[row] = inner(own, u, v, first) + jnp.where(first, flux, -flux)


def mix_kernel(mix_ref, x0_ref, x1_ref, x2_ref, x3_ref, out_ref, field_ref):
    z = lax.axis_index("lev")
    refs = (x0_ref, x1_ref, x2_ref, x3_ref)
    cols = [lax.rem(z + d, 4) * HERE for d in range(4)]

    def step(l, acc):
        acc = list(acc)
        for d in range(4):
            xs = [refs[d][s * HERE + l] for s in range(2)]
            for k in range(HERE):
                m = mix_ref[z * HERE + k, cols[d] + l]
                for s in range(2):
                    acc[s * HERE + k] = acc[s * HERE + k] + m * xs[s]
        return tuple(acc)

    zero = jnp.zeros((SUBS, LANES), F32)
    acc = lax.fori_loop(0, HERE, step, (zero,) * (2 * HERE))
    for row in range(2 * HERE):
        out_ref[row] = acc[row]
    for sub in range(SUBS):
        for s in range(2):
            field_ref[sub, s, 0:HERE, :] = out_ref[s * HERE : (s + 1) * HERE, sub, :]
            field_ref[sub, s, HERE:ROWS, :] = jnp.zeros((ROWS - HERE, LANES), F32)


def send_kernel(kern_ref, col_ref, own_ref, off_ref, send_ref, rank_ref, den_ref, w_ref, own8_ref, hot_ref):
    z = lax.axis_index("lev")
    levels = z * HERE + iota((HERE, SND), 0)
    weighted = jnp.where(levels >= off_ref[...], kern_ref[...], 0.0)
    den_ref[...] = jnp.sum(weighted, axis=0, keepdims=True)
    col = col_ref[...].astype(F32)
    w_ref[0:HERE, :] = weighted
    w_ref[HERE : HERE + 1, :] = col
    w_ref[HERE + 1 : HERE + 3, :] = weighted[HERE - 2 : HERE]
    w_ref[HERE + 3 : HERE + 4, :] = col
    w_ref[HERE + 4 : ROWS, :] = jnp.zeros((2, SND), F32)
    own8_ref[...] = jnp.broadcast_to(own_ref[...], (SUBS, SND))

    wide = 256
    before = (iota((wide, wide), 0) < iota((wide, wide), 1)).astype(BF16)
    slot = iota((wide, 1), 0)
    slot = jnp.where(slot < CAP, slot, slot - 64)
    carry = jnp.zeros((TILES, 1), F32)
    for b in range(SND // wide):
        at = pl.ds(b * wide, wide)
        onehot = (iota((TILES, wide), 0) == own_ref[:, at]).astype(F32)
        prefix = jnp.dot(onehot.astype(BF16), before, preferred_element_type=F32)
        rank = jnp.sum(onehot * (prefix + carry), axis=0, keepdims=True).astype(jnp.int32)
        carry = carry + jnp.sum(onehot, axis=1, keepdims=True)
        rank_ref[:, at] = rank
        hot_ref[:, at] = (slot == rank).astype(F32).astype(BF16)

    group, chunk = 8, 1024
    lane = iota((SUBS, LANES), 1)
    sub = iota((SUBS, LANES), 0)

    def some(g, _):
        acc = jnp.zeros((group * ROWS, wide), F32)
        for b in range(SND // chunk):
            at = pl.ds(b * chunk, chunk)
            w = w_ref[:, at]
            high = w.astype(BF16).astype(F32)
            low = w - high
            own = own8_ref[:, at]
            own = jnp.concatenate([own] * 3, axis=0)
            masks = [own == g * group + j for j in range(group)]
            for part in (high, low):
                lhs = jnp.concatenate([jnp.where(m, part, 0.0) for m in masks], axis=0).astype(BF16)
                acc = acc + lax.dot_general(
                    lhs, hot_ref[:, at], (((1,), (1,)), ((), ())), preferred_element_type=F32
                )
        for j in range(group):
            top = acc[j * ROWS : (j + 1) * ROWS, 0:LANES]
            rest = acc[j * ROWS : (j + 1) * ROWS, LANES:]
            t = g * group + j
            send_ref[t, 0:16, :] = top[0:16]
            send_ref[t, 16:24, :] = jnp.where(sub < 3, top[16:24], rest[16:24])
            send_ref[t, 24:32, :] = jnp.where(lane < 64, rest[0:8], rest[8:16])
        return 0

    lax.fori_loop(0, TILES // group, some, 0)


def sample_kernel(got_ref, field_ref, out_ref):
    lane = iota((SUBS, LANES), 1)
    sub = iota((SUBS, LANES), 0)
    left = lane < 64

    def sums(w, colf):
        col = colf.astype(jnp.int32)
        at_lane = jnp.broadcast_to(col & (LANES - 1), (SUBS, LANES))
        at_sub = jnp.broadcast_to(((col >> 7) & 3) * 2 + (col >> 9), (SUBS, LANES))
        totals = []
        hits = [at_sub == k for k in range(SUBS)]
        for s in range(2):
            total = jnp.zeros((SUBS, LANES), F32)
            for g in range(3):
                value = jnp.zeros((SUBS, LANES), F32)
                for k in range(SUBS):
                    rows = field_ref[k, s, 8 * g : 8 * g + 8, :]
                    value = jnp.where(hits[k], jnp.take_along_axis(rows, at_lane, axis=1), value)
                total = total + value * w[g]
            totals.append(jnp.sum(total, axis=0, keepdims=True))
        return totals

    def pair(p, _):
        xs = [[got_ref[2 * p + i, 8 * g : 8 * g + 8, :] for g in range(4)] for i in range(2)]
        full = []
        for x in xs:
            full.append(sums((x[0], x[1], jnp.where(sub < 2, x[2], 0.0)), x[2][2:3]))
        x, y = xs
        last = roll(jnp.where(left, x[2], y[2]), -3, 0)
        rest = sums(
            (
                jnp.where(left, x[3], roll(y[3], 64, 1)),
                jnp.where(left, roll(x[3], 64, 1), y[3]),
                jnp.where(sub < 2, last, 0.0),
            ),
            last[2:3],
        )
        half = lane[0:1] < 64
        tails = (
            jnp.where(half, rest[0], roll(rest[1], 64, 1)),
            jnp.where(half, roll(rest[0], 64, 1), rest[1]),
        )
        for i in range(2):
            out_ref[2 * p + i, 0:1, :] = full[i][0]
            out_ref[2 * p + i, 1:2, :] = full[i][1]
            out_ref[2 * p + i, 2:3, :] = tails[i]
            out_ref[2 * p + i, 3:8, :] = jnp.zeros((5, LANES), F32)
        return 0

    lax.fori_loop(0, TILES // 2, pair, 0)


def home_kernel(back_ref, own_ref, rank_ref, out_ref):
    tail = back_ref[:, 2, :]
    first = jnp.concatenate([back_ref[:, 0, :], tail], axis=1)
    second = jnp.concatenate([back_ref[:, 1, :], roll(tail, 64, 1)], axis=1)
    high, low = split(jnp.concatenate([first, second], axis=0))
    wide = 256
    slot = iota((wide, 1), 0)
    for b in range(SND // wide):
        at = pl.ds(b * wide, wide)
        hot = (slot == rank_ref[:, at]).astype(F32).astype(BF16)
        values = jnp.dot(high, hot, preferred_element_type=F32) + jnp.dot(low, hot, preferred_element_type=F32)
        mine = iota((TILES, wide), 0) == own_ref[:, at]
        for s in range(2):
            picked = jnp.where(mine, values[s * TILES : (s + 1) * TILES], 0.0)
            out_ref[s : s + 1, at] = jnp.sum(picked, axis=0, keepdims=True)


def last_kernel(count_ref, a_ref, b_ref, c_ref, d_ref, da_ref, db_ref, dc_ref, dd_ref, out_ref):
    num = (a_ref[...] + c_ref[...]) + (b_ref[...] + d_ref[...])
    den = (da_ref[...] + dc_ref[...]) + (db_ref[...] + dd_ref[...])
    used = iota((2, SND), 1) < count_ref[0]
    out_ref[...] = jnp.where(used, num / den, 0.0)


def call(kernel, outs, in_specs, scratch=(), mib=12, flops=10**6, name=None):
    single = not isinstance(outs, (list, tuple))
    shapes = [outs] if single else outs
    return pl.pallas_call(
        kernel,
        out_shape=outs if single else list(outs),
        in_specs=in_specs,
        out_specs=spec() if single else [spec() for _ in shapes],
        scratch_shapes=list(scratch),
        compiler_params=params(mib),
        name=name,
        cost_estimate=pl.CostEstimate(flops=flops, bytes_accessed=10**5, transcendentals=0),
    )


def arr(shape, dtype=F32):
    return jax.ShapeDtypeStruct(shape, dtype)


def registers(x):
    rows = x.size // (SUBS * LANES)
    return x.reshape(rows, 2, 4, LANES).transpose(0, 2, 1, 3).reshape(rows, SUBS, LANES)


def shift(x, axis, distance):
    size = lax.axis_size(axis)
    return lax.ppermute(x, axis, [(i, (i + distance) % size) for i in range(size)])


def body(tracer, u_courant, v_courant, surface_flux, mixing, kernel, column, owner_tile, offset, counts):
    c, u, v, f = (registers(x) for x in (tracer, u_courant, v_courant, surface_flux))
    col, own, off = (x.reshape(1, SND) for x in (column, owner_tile, offset))
    east, west, part = call(
        halo_kernel, [arr((36, SUBS, LANES)), arr((45, SUBS, LANES)), arr((36, SUBS, LANES))], [spec()] * 4, name="halo"
    )(c, u, v, f)
    from_west = shift(east, "tile", 1)
    from_east = shift(west, "tile", -1)
    send, rank, den = call(
        send_kernel,
        [arr((TILES, 32, LANES)), arr((1, SND), jnp.int32), arr((1, SND))],
        [spec()] * 4,
        [pltpu.VMEM((ROWS, SND), F32), pltpu.VMEM((SUBS, SND), jnp.int32), pltpu.VMEM((256, SND), BF16)],
        mib=24,
        flops=10**9,
        name="send",
    )(kernel, col, own, off)
    got = lax.all_to_all(send, "tile", 0, 0, tiled=True)
    adv = call(advect_kernel, arr((36, SUBS, LANES)), [spec()] * 7, name="advect")(c, u, v, f, part, from_west, from_east)
    others = [shift(adv, "lev", -d) for d in (1, 2, 3)]
    dens = [shift(den, "lev", -d) for d in (1, 2, 3)]
    transported, field = call(
        mix_kernel,
        [arr((36, SUBS, LANES)), arr((SUBS, 2, ROWS, LANES))],
        [spec(SMEM)] + [spec()] * 4,
        name="mix",
    )(mixing, adv, *others)
    sums = call(sample_kernel, arr((TILES, SUBS, LANES)), [spec()] * 2, name="sample")(got, field)
    back = lax.all_to_all(sums, "tile", 0, 0, tiled=True)
    mine = call(home_kernel, arr((2, SND)), [spec()] * 3, name="home")(back, own, rank)
    nums = [shift(mine, "lev", -d) for d in (1, 2, 3)]
    evolved = call(last_kernel, arr((2, SND)), [spec(SMEM)] + [spec()] * 8, name="last")(
        counts, mine, *nums, den, *dens
    )
    out = transported.reshape(36, 4, 2, LANES).transpose(0, 2, 1, 3).reshape(tracer.shape)
    return out, evolved


def solution(mesh):
    in_specs = (
        P(None, "lev", "tile", None),
        P("lev", "tile", None),
        P("lev", "tile", None),
        P(None, "tile", None),
        P(),
        P("lev", "tile"),
        P("tile"),
        P("tile"),
        P("tile"),
        P("tile"),
    )
    out_specs = (P(None, "lev", "tile", None), P(None, "tile"))
    return jax.shard_map(body, mesh=mesh, in_specs=in_specs, out_specs=out_specs, check_vma=False)
```

time: 414 us -> 119 us (0.29)
  local copies, waits for them, and re-layouts: 214 us -> 3.16 us
  blocking collectives: 111 us -> 0 us
  other arithmetic: 36.1 us -> 0 us
  Pallas kernels: 0 us -> 32.1 us
  waiting for transfers between devices: 8.52 us -> 34.6 us
  starting transfers between devices: 40.6 us -> 46.7 us
    gather x7 -> x0, local copies, waits for them, and re-layouts: 180 us -> none  [the longest x1 68 us: body(): column_rows = jnp.take(column, safe_ids, axis=0).astype(jnp.float32)]
    psum x1 -> x0, blocking collectives: 79 us -> none  [body(): numerator, total_weight = lax.psum((own_sums, denominator), 'lev')]
    all_gather x1 -> x0, blocking collectives: 32.4 us -> none  [body(): lax.all_gather(advected, 'lev', axis=1, tiled=True)]
    pallas_call x0 -> x7, Pallas kernels: none -> 32.1 us  [the longest x1 14.6 us: body(): call(send_kernel, [arr((TILES, 32, LANES)), arr((1, SND), jnp.int32), arr...]
    ppermute x5 -> x11, waiting for transfers between devices: 0.01 us -> 26.9 us  [shift(): lax.ppermute(x, axis, [(i, (i + distance) % size) for i in range(size)])]
    another operation x3 -> x0, other arithmetic: 19 us -> none
    ppermute x5 -> x11, starting transfers between devices: 9.64 us -> 25.5 us  [shift(): lax.ppermute(x, axis, [(i, (i + distance) % size) for i in range(size)])]
    scatter x1 -> x0, local copies, waits for them, and re-layouts: 15.5 us -> none  [body(): jnp.full((buffer_len,), snd_here, jnp.int32).at[slot_ids]]
  transfers between devices with their start and end apart: 8 -> 13, of which waited for: 1 -> 7; matrix products, arithmetic and copies ran while one was open for 51% -> 0% of each run, Pallas kernels for 0% -> 5%
where the time goes in v1:
time: 119 us; the launch traced here: 118 us
  starting transfers between devices  46.7 us (39%)
  waiting for transfers between devices  34.6 us (29%)
  Pallas kernels  32.1 us (27%)
  local copies, waits for them, and re-layouts  3.16 us (3%)
  between operations  1.39 us (1%)
    ppermute x11, waiting for transfers between devices, shift(): lax.ppermute(x, axis, [(i, (i + distance) % size) for i in range(size)])  26.9 us
    ppermute x11, starting transfers between devices, shift(): lax.ppermute(x, axis, [(i, (i + distance) % size) for i in range(size)])  25.5 us
    pallas_call x1, Pallas kernels, body(): call(send_kernel, [arr((TILES, 32, LANES)), arr((1, SND), jnp.int32), arr...  14.6 us
    all_to_all x1, starting transfers between devices, body(): back = lax.all_to_all(sums, 'tile', 0, 0, tiled=True)  10.7 us
    pallas_call x1, Pallas kernels, body(): call(sample_kernel, arr((TILES, SUBS, LANES)), [spec()] * 2, name='sample')  10.7 us
    all_to_all x1, starting transfers between devices, body(): got = lax.all_to_all(send, 'tile', 0, 0, tiled=True)  10.5 us
    all_to_all x1, waiting for transfers between devices, body(): back = lax.all_to_all(sums, 'tile', 0, 0, tiled=True)  7.72 us
    pallas_call x1, Pallas kernels, body(): call(mix_kernel, [arr((36, SUBS, LANES)), arr((SUBS, 2, ROWS, LANES))], [...  4.32 us
  transfers between devices with their start and end apart: 13, of which 7 were waited for; matrix products, arithmetic and copies ran while one was open for 0% of the time, Pallas kernels for 5%

profile of v1, /device:TPU:1, one launch (start us, length us, event | category | flops | bytes accessed | tf_op | source)
XLA Modules:
  0.0 118.0 jit_solution(16689588463412968467)
XLA Ops:
  0.6 0.0 copy-start.5
  0.6 0.7 copy-done.5
  1.4 0.0 copy-start.7
  1.4 1.0 copy-done.7
  2.3 0.0 copy-start.8
  2.3 0.7 copy-done.8
  3.1 0.0 copy-start.9
  3.1 0.7 copy-done.9
  3.8 14.6 %send.1 = (f32[64,32,128]{2,1,0:T(8,128)}, s32[1,4096]{1,0:T(1,128)S(1)}, f32[1,4096]{1,0:T(1,128)S(1)}) custom-call(f32[18,4096]{1,0:T(8,128)S(1)} %copy-done.7, s32[1,4096]{1,0:T(1,128)S(1)} %bitcast.38, s32[1,4096]{1,0:T(1,128)S(1)} %bitcast.36, s32[1,4096]{1,0:T(1,128)S(1)} %bitcast.39), custom_call_target="tpu_custom_call" | custom-call | flops 1000000000 | bytes 100000 | tf_op jit(solution)/shard_map/send/pallas_call | solution.py:300
  18.4 0.0 copy-start
  18.4 10.5 %all-to-all-start = ((f32[64,32,128]{2,1,0:T(8,128)}), f32[64,32,128]{2,1,0:T(8,128)S(1)}, u32[]{:S(2)}, u32[]{:S(2)}) async-start(f32[64,32,128]{2,1,0:T(8,128)} %get-tuple-element.14), calls=%async_computation | async-start | bytes 2097152 | tf_op jit(solution)/shard_map/all_to_all | solution.py:309
  28.9 0.0 copy-done
  28.9 0.0 copy-done.1
  28.9 0.0 copy-done.2
  29.0 0.0 copy-done.4
  29.0 0.2 halo.1
  29.2 0.5 collective-permute-start.1
  29.7 1.3 %collective-permute-start = (f32[36,8,128]{2,1,0:T(8,128)S(1)}, f32[36,8,128]{2,1,0:T(8,128)S(1)}, u32[]{:S(2)}, u32[]{:S(2)}) collective-permute-start(f32[36,8,128]{2,1,0:T(8,128)S(1)} %get-tuple-element.11), channel_id=1, source_target_pairs={{0,4},{4,8},{8,12},{12,16},{16,20},{20,24},{24,28},{28,32},{32,36}... | collective-permute-start | bytes 442376 | tf_op jit(solution)/shard_map/ppermute | solution.py:289
  31.0 12.2 %collective-permute-done.a_ref = f32[36,8,128]{2,1,0:T(8,128)S(1)} collective-permute-done((f32[36,8,128]{2,1,0:T(8,128)S(1)}, f32[36,8,128]{2,1,0:T(8,128)S(1)}, u32[]{:S(2)}, u32[]{:S(2)}) %collective-permute-start) | collective-permute-done | bytes 147488 | tf_op jit(solution)/shard_map/ppermute | solution.py:289
  43.2 3.0 %collective-permute-done.1.b_ref = f32[45,8,128]{2,1,0:T(8,128)S(1)} collective-permute-done((f32[45,8,128]{2,1,0:T(8,128)S(1)}, f32[45,8,128]{2,1,0:T(8,128)S(1)}, u32[]{:S(2)}, u32[]{:S(2)}) %collective-permute-start.1) | collective-permute-done | bytes 184352 | tf_op jit(solution)/shard_map/ppermute | solution.py:289
  46.2 0.2 advect.1.x0_ref
  46.4 5.2 %collective-permute-start.2 = (f32[36,8,128]{2,1,0:T(8,128)S(1)}, f32[36,8,128]{2,1,0:T(8,128)S(1)}, u32[]{:S(2)}, u32[]{:S(2)}) collective-permute-start(f32[36,8,128]{2,1,0:T(8,128)S(1)} %advect.1.x0_ref), channel_id=1, source_target_pairs={{0,3},{1,0},{2,1},{3,2},{4,7},{5,4},{6,5},{7,6},{8,11},{9,8},{10,9... | collective-permute-start | bytes 442376 | tf_op jit(solution)/shard_map/ppermute | solution.py:289
  51.6 1.2 collective-permute-start.3
  52.8 2.1 %collective-permute-start.4 = (f32[36,8,128]{2,1,0:T(8,128)S(1)}, f32[36,8,128]{2,1,0:T(8,128)S(1)}, u32[]{:S(2)}, u32[]{:S(2)}) collective-permute-start(f32[36,8,128]{2,1,0:T(8,128)S(1)} %advect.1.x0_ref), channel_id=1, source_target_pairs={{0,1},{1,2},{2,3},{3,0},{4,5},{5,6},{6,7},{7,4},{8,9},{9,10},{10,1... | collective-permute-start | bytes 442376 | tf_op jit(solution)/shard_map/ppermute | solution.py:289
  54.9 0.2 collective-permute-done.2.x1_ref
  55.1 6.1 %collective-permute-done.3.x2_ref = f32[36,8,128]{2,1,0:T(8,128)S(1)} collective-permute-done((f32[36,8,128]{2,1,0:T(8,128)S(1)}, f32[36,8,128]{2,1,0:T(8,128)S(1)}, u32[]{:S(2)}, u32[]{:S(2)}) %collective-permute-start.3) | collective-permute-done | bytes 147488 | tf_op jit(solution)/shard_map/ppermute | solution.py:289
  61.2 3.4 %collective-permute-done.4.x3_ref = f32[36,8,128]{2,1,0:T(8,128)S(1)} collective-permute-done((f32[36,8,128]{2,1,0:T(8,128)S(1)}, f32[36,8,128]{2,1,0:T(8,128)S(1)}, u32[]{:S(2)}, u32[]{:S(2)}) %collective-permute-start.4) | collective-permute-done | bytes 147488 | tf_op jit(solution)/shard_map/ppermute | solution.py:289
  64.6 0.0 copy-done.3
  64.6 4.3 %mix.1 = (f32[36,8,128]{2,1,0:T(8,128)}, f32[8,2,24,128]{3,2,1,0:T(8,128)S(1)}) custom-call(f32[72,72]{1,0:T(8,128)S(1)} %copy-done.3, f32[36,8,128]{2,1,0:T(8,128)S(1)} %advect.1.x0_ref, f32[36,8,128]{2,1,0:T(8,128)S(1)} %collective-permute-done.2.x1_ref, f32[36,8,128]{2,1,0:T(8,128)S(1)} %collective-permute-done.3.x2_ref, ...), custom_call_target="tpu_custom_call" | custom-call | flops 1000000 | bytes 100000 | tf_op jit(solution)/shard_map/mix/pallas_call | solution.py:313
  68.9 0.0 all-to-all-done.got_ref
  68.9 10.7 %sample.1 = f32[64,8,128]{2,1,0:T(8,128)} custom-call(f32[64,32,128]{2,1,0:T(8,128)S(1)} %all-to-all-done.got_ref, f32[8,2,24,128]{3,2,1,0:T(8,128)S(1)} %get-tuple-element.15.field_ref), custom_call_target="tpu_custom_call" | custom-call | flops 1000000 | bytes 100000 | tf_op jit(solution)/shard_map/sample/pallas_call | solution.py:319
  79.6 10.7 %all-to-all-start.1 = ((f32[64,8,128]{2,1,0:T(8,128)}), f32[64,8,128]{2,1,0:T(8,128)S(1)}, u32[]{:S(2)}, u32[]{:S(2)}) async-start(f32[64,8,128]{2,1,0:T(8,128)} %sample.1), calls=%async_computation.1 | async-start | bytes 524288 | tf_op jit(solution)/shard_map/all_to_all | solution.py:320
  90.3 2.3 %collective-permute-start.10 = (f32[1,4096]{1,0:T(1,128)S(1)}, f32[1,4096]{1,0:T(1,128)S(1)}, u32[]{:S(2)}, u32[]{:S(2)}) collective-permute-start(f32[1,4096]{1,0:T(1,128)S(1)} %get-tuple-element.17.da_ref), channel_id=1, source_target_pairs={{0,1},{1,2},{2,3},{3,0},{4,5},{5,6},{6,7},{7,4},{8,9},{9,10},{10,1... | collective-permute-start | bytes 49160 | tf_op jit(solution)/shard_map/ppermute | solution.py:289
  92.6 7.7 %all-to-all-done.1.back_ref = f32[64,8,128]{2,1,0:T(8,128)S(1)} async-done(((f32[64,8,128]{2,1,0:T(8,128)}), f32[64,8,128]{2,1,0:T(8,128)S(1)}, u32[]{:S(2)}, u32[]{:S(2)}) %all-to-all-start.1) | async-done | bytes 262176 | tf_op jit(solution)/shard_map/all_to_all | solution.py:320
  100.3 0.0 copy-done.6
  100.3 1.3 %home.1.a_ref = f32[2,4096]{1,0:T(2,128)S(1)} custom-call(f32[64,8,128]{2,1,0:T(8,128)S(1)} %all-to-all-done.1.back_ref, s32[1,4096]{1,0:T(1,128)S(1)} %bitcast.37, s32[1,4096]{1,0:T(1,128)S(1)} %get-tuple-element.16.rank_ref), custom_call_target="tpu_custom_call" | custom-call | flops 1000000 | bytes 100000 | tf_op jit(solution)/shard_map/home/pallas_call | solution.py:321
  101.7 4.0 %collective-permute-start.5 = (f32[2,4096]{1,0:T(2,128)S(1)}, f32[2,4096]{1,0:T(2,128)S(1)}, u32[]{:S(2)}, u32[]{:S(2)}) collective-permute-start(f32[2,4096]{1,0:T(2,128)S(1)} %home.1.a_ref), channel_id=1, source_target_pairs={{0,3},{1,0},{2,1},{3,2},{4,7},{5,4},{6,5},{7,6},{8,11},{9,8},{10,9... | collective-permute-start | bytes 98312 | tf_op jit(solution)/shard_map/ppermute | solution.py:289
  105.7 1.5 %collective-permute-start.6 = (f32[2,4096]{1,0:T(2,128)S(1)}, f32[2,4096]{1,0:T(2,128)S(1)}, u32[]{:S(2)}, u32[]{:S(2)}) collective-permute-start(f32[2,4096]{1,0:T(2,128)S(1)} %home.1.a_ref), channel_id=1, source_target_pairs={{0,2},{1,3},{2,0},{3,1},{4,6},{5,7},{6,4},{7,5},{8,10},{9,11},{10,... | collective-permute-start | bytes 98312 | tf_op jit(solution)/shard_map/ppermute | solution.py:289
  107.2 2.1 %collective-permute-start.7 = (f32[2,4096]{1,0:T(2,128)S(1)}, f32[2,4096]{1,0:T(2,128)S(1)}, u32[]{:S(2)}, u32[]{:S(2)}) collective-permute-start(f32[2,4096]{1,0:T(2,128)S(1)} %home.1.a_ref), channel_id=1, source_target_pairs={{0,1},{1,2},{2,3},{3,0},{4,5},{5,6},{6,7},{7,4},{8,9},{9,10},{10,1... | collective-permute-start | bytes 98312 | tf_op jit(solution)/shard_map/ppermute | solution.py:289
  109.3 1.5 %collective-permute-start.8 = (f32[1,4096]{1,0:T(1,128)S(1)}, f32[1,4096]{1,0:T(1,128)S(1)}, u32[]{:S(2)}, u32[]{:S(2)}) collective-permute-start(f32[1,4096]{1,0:T(1,128)S(1)} %get-tuple-element.17.da_ref), channel_id=1, source_target_pairs={{0,3},{1,0},{2,1},{3,2},{4,7},{5,4},{6,5},{7,6},{8,11},{9,8},{10,9... | collective-permute-start | bytes 49160 | tf_op jit(solution)/shard_map/ppermute | solution.py:289
  110.8 0.0 collective-permute-done.10.dd_ref
  110.8 3.9 %collective-permute-start.9 = (f32[1,4096]{1,0:T(1,128)S(1)}, f32[1,4096]{1,0:T(1,128)S(1)}, u32[]{:S(2)}, u32[]{:S(2)}) collective-permute-start(f32[1,4096]{1,0:T(1,128)S(1)} %get-tuple-element.17.da_ref), channel_id=1, source_target_pairs={{0,2},{1,3},{2,0},{3,1},{4,6},{5,7},{6,4},{7,5},{8,10},{9,11},{10,... | collective-permute-start | bytes 49160 | tf_op jit(solution)/shard_map/ppermute | solution.py:289
  115.3 0.0 collective-permute-done.8.db_ref
  115.3 2.0 %collective-permute-done.9.dc_ref = f32[1,4096]{1,0:T(1,128)S(1)} collective-permute-done((f32[1,4096]{1,0:T(1,128)S(1)}, f32[1,4096]{1,0:T(1,128)S(1)}, u32[]{:S(2)}, u32[]{:S(2)}) %collective-permute-start.9) | collective-permute-done | bytes 16416 | tf_op jit(solution)/shard_map/ppermute | solution.py:289
  117.3 0.0 collective-permute-done.5.b_ref
  117.3 0.0 collective-permute-done.6.c_ref
  117.3 0.0 collective-permute-done.7.d_ref
  117.3 0.7 last.1
  (5 shorter events, 0.0 us)
Async XLA Ops:
  0.6 0.7 copy-start.5
  1.4 1.0 copy-start.7
  2.3 0.7 copy-start.8
  3.1 0.7 copy-start.9
  18.4 10.5 %copy-start = (f32[2,18,2,512]{3,2,1,0:T(2,128)S(1)}, f32[2,18,2,512]{3,2,1,0:T(2,128)}, u32[]{:S(2)}) copy-start(f32[2,18,2,512]{3,2,1,0:T(2,128)} %param.10) | copy-start | bytes 442372
  18.4 10.5 %copy-start.1 = (f32[18,2,512]{2,1,0:T(2,128)S(1)}, f32[18,2,512]{2,1,0:T(2,128)}, u32[]{:S(2)}) copy-start(f32[18,2,512]{2,1,0:T(2,128)} %param.11) | copy-start | bytes 221188
  18.4 10.5 %copy-start.2 = (f32[18,2,512]{2,1,0:T(2,128)S(1)}, f32[18,2,512]{2,1,0:T(2,128)}, u32[]{:S(2)}) copy-start(f32[18,2,512]{2,1,0:T(2,128)} %param.12) | copy-start | bytes 221188
  18.4 10.5 %copy-start.4 = (f32[2,2,512]{2,1,0:T(2,128)S(1)}, f32[2,2,512]{2,1,0:T(2,128)}, u32[]{:S(2)}) copy-start(f32[2,2,512]{2,1,0:T(2,128)} %param.13) | copy-start | bytes 24580
  18.4 50.5 %all-to-all-start = ((f32[64,32,128]{2,1,0:T(8,128)}), f32[64,32,128]{2,1,0:T(8,128)S(1)}, u32[]{:S(2)}, u32[]{:S(2)}) async-start(f32[64,32,128]{2,1,0:T(8,128)} %get-tuple-element.14), calls=%async_computation | async-start | bytes 2097152 | tf_op jit(solution)/shard_map/all_to_all | solution.py:309
  29.2 17.0 %collective-permute-start.1 = (f32[45,8,128]{2,1,0:T(8,128)S(1)}, f32[45,8,128]{2,1,0:T(8,128)S(1)}, u32[]{:S(2)}, u32[]{:S(2)}) collective-permute-start(f32[45,8,128]{2,1,0:T(8,128)S(1)} %get-tuple-element.12), channel_id=1, source_target_pairs={{0,252},{4,0},{8,4},{12,8},{16,12},{20,16},{24,20},{28,24},{32,28}... | collective-permute-start | bytes 552968 | tf_op jit(solution)/shard_map/ppermute | solution.py:289
  29.7 13.5 %collective-permute-start = (f32[36,8,128]{2,1,0:T(8,128)S(1)}, f32[36,8,128]{2,1,0:T(8,128)S(1)}, u32[]{:S(2)}, u32[]{:S(2)}) collective-permute-start(f32[36,8,128]{2,1,0:T(8,128)S(1)} %get-tuple-element.11), channel_id=1, source_target_pairs={{0,4},{4,8},{8,12},{12,16},{16,20},{20,24},{24,28},{28,32},{32,36}... | collective-permute-start | bytes 442376 | tf_op jit(solution)/shard_map/ppermute | solution.py:289
  46.2 18.4 %copy-start.3 = (f32[72,72]{1,0:T(8,128)S(1)}, f32[72,72]{1,0:T(8,128)}, u32[]{:S(2)}) copy-start(f32[72,72]{1,0:T(8,128)} %mix_ref.1) | copy-start | bytes 62212
  46.4 8.7 %collective-permute-start.2 = (f32[36,8,128]{2,1,0:T(8,128)S(1)}, f32[36,8,128]{2,1,0:T(8,128)S(1)}, u32[]{:S(2)}, u32[]{:S(2)}) collective-permute-start(f32[36,8,128]{2,1,0:T(8,128)S(1)} %advect.1.x0_ref), channel_id=1, source_target_pairs={{0,3},{1,0},{2,1},{3,2},{4,7},{5,4},{6,5},{7,6},{8,11},{9,8},{10,9... | collective-permute-start | bytes 442376 | tf_op jit(solution)/shard_map/ppermute | solution.py:289
  51.6 9.6 %collective-permute-start.3 = (f32[36,8,128]{2,1,0:T(8,128)S(1)}, f32[36,8,128]{2,1,0:T(8,128)S(1)}, u32[]{:S(2)}, u32[]{:S(2)}) collective-permute-start(f32[36,8,128]{2,1,0:T(8,128)S(1)} %advect.1.x0_ref), channel_id=1, source_target_pairs={{0,2},{1,3},{2,0},{3,1},{4,6},{5,7},{6,4},{7,5},{8,10},{9,11},{10,... | collective-permute-start | bytes 442376 | tf_op jit(solution)/shard_map/ppermute | solution.py:289
  52.8 11.8 %collective-permute-start.4 = (f32[36,8,128]{2,1,0:T(8,128)S(1)}, f32[36,8,128]{2,1,0:T(8,128)S(1)}, u32[]{:S(2)}, u32[]{:S(2)}) collective-permute-start(f32[36,8,128]{2,1,0:T(8,128)S(1)} %advect.1.x0_ref), channel_id=1, source_target_pairs={{0,1},{1,2},{2,3},{3,0},{4,5},{5,6},{6,7},{7,4},{8,9},{9,10},{10,1... | collective-permute-start | bytes 442376 | tf_op jit(solution)/shard_map/ppermute | solution.py:289
  79.6 20.7 %copy-start.6 = (s32[4096]{0:T(1024)S(1)}, s32[4096]{0:T(1024)}, u32[]{:S(2)}) copy-start(s32[4096]{0:T(1024)} %param.17) | copy-start | bytes 49156
  79.6 20.7 %all-to-all-start.1 = ((f32[64,8,128]{2,1,0:T(8,128)}), f32[64,8,128]{2,1,0:T(8,128)S(1)}, u32[]{:S(2)}, u32[]{:S(2)}) async-start(f32[64,8,128]{2,1,0:T(8,128)} %sample.1), calls=%async_computation.1 | async-start | bytes 524288 | tf_op jit(solution)/shard_map/all_to_all | solution.py:320
  90.3 20.4 %collective-permute-start.10 = (f32[1,4096]{1,0:T(1,128)S(1)}, f32[1,4096]{1,0:T(1,128)S(1)}, u32[]{:S(2)}, u32[]{:S(2)}) collective-permute-start(f32[1,4096]{1,0:T(1,128)S(1)} %get-tuple-element.17.da_ref), channel_id=1, source_target_pairs={{0,1},{1,2},{2,3},{3,0},{4,5},{5,6},{6,7},{7,4},{8,9},{9,10},{10,1... | collective-permute-start | bytes 49160 | tf_op jit(solution)/shard_map/ppermute | solution.py:289
  101.7 15.6 %collective-permute-start.5 = (f32[2,4096]{1,0:T(2,128)S(1)}, f32[2,4096]{1,0:T(2,128)S(1)}, u32[]{:S(2)}, u32[]{:S(2)}) collective-permute-start(f32[2,4096]{1,0:T(2,128)S(1)} %home.1.a_ref), channel_id=1, source_target_pairs={{0,3},{1,0},{2,1},{3,2},{4,7},{5,4},{6,5},{7,6},{8,11},{9,8},{10,9... | collective-permute-start | bytes 98312 | tf_op jit(solution)/shard_map/ppermute | solution.py:289
  105.7 11.6 %collective-permute-start.6 = (f32[2,4096]{1,0:T(2,128)S(1)}, f32[2,4096]{1,0:T(2,128)S(1)}, u32[]{:S(2)}, u32[]{:S(2)}) collective-permute-start(f32[2,4096]{1,0:T(2,128)S(1)} %home.1.a_ref), channel_id=1, source_target_pairs={{0,2},{1,3},{2,0},{3,1},{4,6},{5,7},{6,4},{7,5},{8,10},{9,11},{10,... | collective-permute-start | bytes 98312 | tf_op jit(solution)/shard_map/ppermute | solution.py:289
  107.2 10.1 %collective-permute-start.7 = (f32[2,4096]{1,0:T(2,128)S(1)}, f32[2,4096]{1,0:T(2,128)S(1)}, u32[]{:S(2)}, u32[]{:S(2)}) collective-permute-start(f32[2,4096]{1,0:T(2,128)S(1)} %home.1.a_ref), channel_id=1, source_target_pairs={{0,1},{1,2},{2,3},{3,0},{4,5},{5,6},{6,7},{7,4},{8,9},{9,10},{10,1... | collective-permute-start | bytes 98312 | tf_op jit(solution)/shard_map/ppermute | solution.py:289
  109.3 6.0 %collective-permute-start.8 = (f32[1,4096]{1,0:T(1,128)S(1)}, f32[1,4096]{1,0:T(1,128)S(1)}, u32[]{:S(2)}, u32[]{:S(2)}) collective-permute-start(f32[1,4096]{1,0:T(1,128)S(1)} %get-tuple-element.17.da_ref), channel_id=1, source_target_pairs={{0,3},{1,0},{2,1},{3,2},{4,7},{5,4},{6,5},{7,6},{8,11},{9,8},{10,9... | collective-permute-start | bytes 49160 | tf_op jit(solution)/shard_map/ppermute | solution.py:289
  110.8 6.5 %collective-permute-start.9 = (f32[1,4096]{1,0:T(1,128)S(1)}, f32[1,4096]{1,0:T(1,128)S(1)}, u32[]{:S(2)}, u32[]{:S(2)}) collective-permute-start(f32[1,4096]{1,0:T(1,128)S(1)} %get-tuple-element.17.da_ref), channel_id=1, source_target_pairs={{0,2},{1,3},{2,0},{3,1},{4,6},{5,7},{6,4},{7,5},{8,10},{9,11},{10,... | collective-permute-start | bytes 49160 | tf_op jit(solution)/shard_map/ppermute | solution.py:289

commit v2 on v1

v2 whole, which is shorter than its diff:
```python
import jax
import jax.numpy as jnp
from jax import lax
from jax.experimental import pallas as pl
from jax.experimental.pallas import tpu as pltpu
from jax.sharding import PartitionSpec as P

LANES = 128
SUBS = 8
HERE = 18
ROWS = 24
TILES = 64
WIDE = 256
QUADS = 4
SND = 4096
F32 = jnp.float32
BF16 = jnp.bfloat16
VMEM = pltpu.MemorySpace.VMEM
SMEM = pltpu.MemorySpace.SMEM
HBM = pltpu.MemorySpace.HBM


def params(mib):
    return pltpu.CompilerParams(vmem_limit_bytes=mib * 2**20)


def spec(space=VMEM):
    return pl.BlockSpec(memory_space=space)


def iota(shape, dim):
    return lax.broadcasted_iota(jnp.int32, shape, dim)


def split(x):
    high = x.astype(BF16)
    low = (x - high.astype(F32)).astype(BF16)
    return high, low


def roll(x, shift, axis):
    return pltpu.roll(x, shift % x.shape[axis], axis)


def swap(x, first):
    return jnp.where(first, roll(x, -1, 0), roll(x, 1, 0))


def inner(c, u, v, first):
    sub, lane = iota(c.shape, 0), iota(c.shape, 1)
    shifted = roll(c, 1, 1)
    south = jnp.where(lane == 0, roll(shifted, 2, 0), shifted)
    wall = (sub < 2) & (lane == 0)
    flux_south = jnp.where(wall, 0.0, v * jnp.where(v > 0, south, c))
    back = roll(flux_south, -1, 1)
    flux_north = jnp.where(lane == LANES - 1, roll(back, -2, 0), back)
    middle = u * jnp.where(u > 0, roll(c, 1, 0), c)
    return c - (flux_north - flux_south) + jnp.where(first, -roll(middle, -1, 0), middle)


def surfaced(c_ref, f_ref, s, level):
    c = c_ref[s * HERE + level]
    if level > 0:
        return c
    return c + jnp.where(lax.axis_index("lev") == 0, f_ref[s], 0.0)


def halo_kernel(c_in, u_in, v_in, f_in, east_ref, west_ref, part_ref, c_ref, u_ref, v_ref, f_ref, sem):
    fetch(((c_in, c_ref), (u_in, u_ref), (v_in, v_ref), (f_in, f_ref)), sem)
    first = iota((SUBS, LANES), 0) % 2 == 0
    for level in range(HERE):
        u, v = u_ref[level], v_ref[level]
        for s in range(2):
            row = s * HERE + level
            c = surfaced(c_ref, f_ref, s, level)
            y = inner(c, u, v, first)
            part_ref[row] = y
            east_ref[row] = jnp.where(first, roll(c, -1, 0), y)
            west_ref[row] = jnp.where(first, y, roll(c, 1, 0))
    for level in range(HERE // 2):
        west_ref[2 * HERE + level] = jnp.where(first, u_ref[level], roll(u_ref[level + HERE // 2], 1, 0))


def advect_kernel(c_ref, u_ref, v_ref, f_ref, part_ref, a_ref, b_ref, den_ref, out_ref):
    first = iota((SUBS, LANES), 0) % 2 == 0
    for level in range(HERE):
        u, v = u_ref[level], v_ref[level]
        packed = b_ref[2 * HERE + level % (HERE // 2)]
        beyond = roll(packed, 1, 0) if level < HERE // 2 else packed
        outer = jnp.where(first, u, beyond)
        forward = outer > 0
        for s in range(2):
            row = s * HERE + level
            c = surfaced(c_ref, f_ref, s, level)
            a, b = a_ref[row], b_ref[row]
            flux = outer * jnp.where(forward, jnp.where(first, a, c), jnp.where(first, c, b))
            own = part_ref[row] + jnp.where(first, flux, -flux)
            near = swap(jnp.where(first, b + roll(flux, -1, 0), a - roll(flux, 1, 0)), first)
            flux = outer * jnp.where(forward, jnp.where(first, near, own), jnp.where(first, own, near))
            out_ref[row] = inner(own, u, v, first) + jnp.where(first, flux, -flux)
    for row in range(4):
        out_ref[2 * HERE + row] = den_ref[row]


def mix_kernel(mix_ref, x0_ref, x1_ref, x2_ref, x3_ref, out_ref, field_ref, den_ref):
    refs = (x0_ref, x1_ref, x2_ref, x3_ref)
    high, low = split(mix_ref[...])
    both = jnp.concatenate([high.astype(F32), low.astype(F32)], axis=0).astype(BF16)
    pad = jnp.zeros((ROWS - HERE, 2 * LANES), F32)
    for s in range(2):
        rows = slice(s * HERE, (s + 1) * HERE)
        for sub in range(0, SUBS, 2):
            parts = []
            for ref in refs:
                parts += [jnp.concatenate([ref[rows, sub, :], ref[rows, sub + 1, :]], axis=1), pad]
            x_high, x_low = split(jnp.concatenate(parts, axis=0))
            r = jnp.dot(both, x_high, preferred_element_type=F32)
            mixed = r[0:ROWS] + r[ROWS:] + jnp.dot(high, x_low, preferred_element_type=F32)
            for i in range(2):
                half = mixed[:, i * LANES : (i + 1) * LANES]
                field_ref[sub + i, s] = half
                out_ref[rows, sub + i, :] = half[0:HERE]
    for row in range(4):
        a, b, c, d = (ref[2 * HERE + row] for ref in refs)
        den_ref[row] = (a + c) + (b + d)


def place(own, rank):
    full = rank < LANES
    group = (own >> 2) * 3 + jnp.where(full, (own & 3) >> 1, 2)
    lane = jnp.where(full, (own & 1) * LANES + rank, (own & 3) * 64 + rank - LANES)
    return group, lane


def fetch(pairs, sem):
    copies = [pltpu.make_async_copy(a, b, sem.at[i]) for i, (a, b) in enumerate(pairs)]
    for copy in copies:
        copy.start()
    for copy in copies:
        copy.wait()


def send_kernel(
    kern_in, col_in, own_in, off_in, part_ref, send_ref, rank_ref, den_ref,
    kern_ref, col_ref, own_ref, off_ref, w_ref, grp_ref, hot_ref, sem,
):
    fetch(((kern_in, kern_ref), (col_in, col_ref), (own_in, own_ref), (off_in, off_ref)), sem)
    z = lax.axis_index("lev")
    levels = z * HERE + iota((HERE, SND), 0)
    weighted = jnp.where(levels >= off_ref[...], kern_ref[...], 0.0)
    den = jnp.sum(weighted, axis=0, keepdims=True)
    for j in range(SND // LANES):
        den_ref[j // SUBS, j % SUBS : j % SUBS + 1, :] = den[:, j * LANES : (j + 1) * LANES]
    col = col_ref[...].astype(F32)
    w_ref[0:HERE, :] = weighted
    w_ref[HERE : HERE + 1, :] = col
    w_ref[HERE + 1 : HERE + 3, :] = weighted[HERE - 2 : HERE]
    w_ref[HERE + 3 : HERE + 4, :] = col
    w_ref[HERE + 4 : ROWS, :] = jnp.zeros((2, SND), F32)

    before = (iota((WIDE, WIDE), 0) < iota((WIDE, WIDE), 1)).astype(BF16)
    slot = iota((WIDE, 1), 0)
    carry = jnp.zeros((TILES, 1), F32)
    for b in range(SND // WIDE):
        at = pl.ds(b * WIDE, WIDE)
        own = own_ref[:, at]
        onehot = (iota((TILES, WIDE), 0) == own).astype(F32)
        prefix = jnp.dot(onehot.astype(BF16), before, preferred_element_type=F32)
        rank = jnp.sum(onehot * (prefix + carry), axis=0, keepdims=True).astype(jnp.int32)
        carry = carry + jnp.sum(onehot, axis=1, keepdims=True)
        rank_ref[:, at] = rank
        group, lane = place(own, rank)
        grp_ref[:, at] = jnp.broadcast_to(group, (SUBS, WIDE))
        hot_ref[at, :] = (slot == lane).astype(F32).T.astype(BF16)

    quads, chunk = 8, 1024
    sub, left = iota((SUBS, LANES), 0), iota((SUBS, LANES), 1) < 64

    def some(i, _):
        acc = jnp.zeros((quads * 3 * 2 * ROWS, WIDE), F32)
        for b in range(SND // chunk):
            at = pl.ds(b * chunk, chunk)
            w = w_ref[:, at]
            high = w.astype(BF16).astype(F32)
            low = w - high
            group = jnp.concatenate([grp_ref[:, at]] * 3, axis=0)
            rows = []
            for j in range(quads * 3):
                here = group == i * quads * 3 + j
                rows += [jnp.where(here, high, 0.0), jnp.where(here, low, 0.0)]
            lhs = jnp.concatenate(rows, axis=0).astype(BF16)
            acc = acc + jnp.dot(lhs, hot_ref[at, :], preferred_element_type=F32)
        for q in range(quads):
            sums = []
            for j in range(3):
                base = (q * 3 + j) * 2 * ROWS
                sums.append(acc[base : base + ROWS] + acc[base + ROWS : base + 2 * ROWS])
            for k in range(4):
                t = (i * quads + q) * 4 + k
                top = sums[k // 2][:, (k % 2) * LANES : (k % 2 + 1) * LANES]
                rest = sums[2][:, (k // 2) * LANES : (k // 2 + 1) * LANES]
                middle = rest[16:24]
                if k % 2 == 0:
                    bottom = jnp.where(left, rest[0:8], roll(rest[8:16], 64, 1))
                else:
                    bottom = jnp.where(left, roll(rest[0:8], 64, 1), rest[8:16])
                    middle = roll(middle, 64, 1)
                send_ref[t, 0:16, :] = top[0:16]
                send_ref[t, 16:24, :] = jnp.where(sub < 3, top[16:24], middle)
                send_ref[t, 24:32, :] = bottom
        return 0

    lax.fori_loop(0, TILES // (4 * quads), some, 0)


FIELD = 40


def sample_kernel(got_ref, field_ref, out_ref, f_ref):
    sub, lane = iota((SUBS, LANES), 0), iota((SUBS, LANES), 1)
    left = lane < 64
    for h in range(4):
        blocks = []
        for lon in range(2):
            x, y = field_ref[2 * h + lon, 0], field_ref[2 * h + lon, 1]
            third = jnp.where(sub < 2, x[16:24], roll(y[16:24], 3, 0))
            blocks.append(jnp.concatenate([x[0:16], y[0:16], third], axis=0))
        high, low = split(jnp.concatenate(blocks, axis=1))
        f_ref[h * FIELD : (h + 1) * FIELD, :] = high
        f_ref[(4 + h) * FIELD : (5 + h) * FIELD, :] = low
    spot = iota((WIDE, 1), 0)
    row = iota((SUBS, WIDE), 0)

    def sums(w, col):
        col = col.astype(jnp.int32)
        hot = (spot == (col & 127) + ((col >> 9) << 7)).astype(F32).astype(BF16)
        block = jnp.broadcast_to((col >> 7) & 3, (SUBS, WIDE))
        hits = [block == h for h in range(4)]
        both = jnp.dot(f_ref[...], hot, preferred_element_type=F32)
        values = both[0 : 4 * FIELD] + both[4 * FIELD :]

        def pick(base):
            out = values[base : base + 8]
            for h in range(1, 4):
                out = jnp.where(hits[h], values[h * FIELD + base : h * FIELD + base + 8], out)
            return out

        last = jnp.where(row < 2, w[2], 0.0)
        last = pick(32) * (last + roll(last, 3, 0))
        totals = []
        for s in range(2):
            total = pick(16 * s) * w[0] + pick(16 * s + 8) * w[1] + jnp.where((row < 3) == (s == 0), last, 0.0)
            totals.append(jnp.sum(total, axis=0, keepdims=True))
        return totals

    def wide(a, b):
        return jnp.concatenate([a, b], axis=1)

    quads = QUADS
    half = lane[0:1] < 64

    def some(i, _):
        rows = ([], [], [])
        for q in range(quads):
            t = (i * quads + q) * 4
            xs = [[got_ref[t + k, 8 * g : 8 * g + 8, :] for g in range(4)] for k in range(4)]
            results, rest = [], []
            for x, y in (xs[0:2], xs[2:4]):
                w = [wide(x[g], y[g]) for g in range(3)]
                results.append(sums(w, w[2][2:3]))
                rest.append(
                    (
                        jnp.where(left, x[3], roll(y[3], 64, 1)),
                        jnp.where(left, roll(x[3], 64, 1), y[3]),
                        roll(jnp.where(left, x[2], roll(y[2], 64, 1)), -3, 0),
                    )
                )
            w = [wide(rest[0][g], rest[1][g]) for g in range(3)]
            tails = sums(w, w[2][2:3])
            for k in range(4):
                mine = slice((k % 2) * LANES, (k % 2 + 1) * LANES)
                pair = slice((k // 2) * LANES, (k // 2 + 1) * LANES)
                a, b = tails[0][:, pair], tails[1][:, pair]
                tail = jnp.where(half, a, roll(b, 64, 1)) if k % 2 == 0 else jnp.where(half, roll(a, 64, 1), b)
                for j, x in enumerate((results[k // 2][0][:, mine], results[k // 2][1][:, mine], tail)):
                    rows[j].append(x)
        at = pl.ds(pl.multiple_of(i * 4 * quads, 4 * quads), 4 * quads)
        for j in range(3):
            out_ref[at, j * LANES : (j + 1) * LANES] = jnp.concatenate(rows[j], axis=0)
        return 0

    lax.fori_loop(0, TILES // (4 * quads), some, 0)


def home_kernel(back_ref, own_ref, rank_ref, out_ref):
    tail = back_ref[:, 2 * LANES : 3 * LANES]
    first = jnp.concatenate([back_ref[:, 0:LANES], tail], axis=1)
    second = jnp.concatenate([back_ref[:, LANES : 2 * LANES], roll(tail, 64, 1)], axis=1)
    high, low = split(jnp.concatenate([first, second], axis=0))
    slot = iota((WIDE, 1), 0)
    for b in range(SND // WIDE):
        at = pl.ds(b * WIDE, WIDE)
        hot = (slot == rank_ref[:, at]).astype(F32).astype(BF16)
        values = jnp.dot(high, hot, preferred_element_type=F32) + jnp.dot(low, hot, preferred_element_type=F32)
        mine = iota((TILES, WIDE), 0) == own_ref[:, at]
        for s in range(2):
            picked = jnp.where(mine, values[s * TILES : (s + 1) * TILES], 0.0)
            total = jnp.sum(picked, axis=0, keepdims=True)
            for i in range(2):
                j = s * 32 + 2 * b + i
                out_ref[j // SUBS, j % SUBS : j % SUBS + 1, :] = total[:, i * LANES : (i + 1) * LANES]


def last_kernel(count_ref, a_ref, b_ref, c_ref, d_ref, den_ref, out_ref):
    count = count_ref[0]
    for row in range(4):
        number = (row * SUBS + iota((SUBS, LANES), 0)) * LANES + iota((SUBS, LANES), 1)
        den = den_ref[row]
        for s in range(2):
            k = s * 4 + row
            num = (a_ref[k] + c_ref[k]) + (b_ref[k] + d_ref[k])
            value = jnp.where(number < count, num / den, 0.0)
            for j in range(SUBS):
                at = (row * SUBS + j) * LANES
                out_ref[s : s + 1, at : at + LANES] = value[j : j + 1]


def call(kernel, outs, in_specs, scratch=(), mib=12, flops=10**6, name=None):
    single = not isinstance(outs, (list, tuple))
    shapes = [outs] if single else outs
    return pl.pallas_call(
        kernel,
        out_shape=outs if single else list(outs),
        in_specs=in_specs,
        out_specs=spec() if single else [spec() for _ in shapes],
        scratch_shapes=list(scratch),
        compiler_params=params(mib),
        name=name,
        cost_estimate=pl.CostEstimate(flops=flops, bytes_accessed=10**5, transcendentals=0),
    )


def arr(shape, dtype=F32):
    return jax.ShapeDtypeStruct(shape, dtype)


def registers(x):
    rows = x.size // (SUBS * LANES)
    return x.reshape(rows, 2, 4, LANES).transpose(0, 2, 1, 3).reshape(rows, SUBS, LANES)


def far(x):
    return pltpu.with_memory_space_constraint(x, HBM)


def shift(x, axis, distance):
    size = lax.axis_size(axis)
    return lax.ppermute(x, axis, [(i, (i + distance) % size) for i in range(size)])


def body(tracer, u_courant, v_courant, surface_flux, mixing, kernel, column, owner_tile, offset, counts):
    c, u, v, f = (registers(x) for x in (tracer, u_courant, v_courant, surface_flux))
    col, own, off = (x.reshape(1, SND) for x in (column, owner_tile, offset))
    block = arr((2 * HERE, SUBS, LANES))
    east, west, part = call(
        halo_kernel,
        [block, arr((45, SUBS, LANES)), block],
        [spec(HBM)] * 4,
        [
            pltpu.VMEM((2 * HERE, SUBS, LANES), F32),
            pltpu.VMEM((HERE, SUBS, LANES), F32),
            pltpu.VMEM((HERE, SUBS, LANES), F32),
            pltpu.VMEM((2, SUBS, LANES), F32),
            pltpu.SemaphoreType.DMA((4,)),
        ],
        name="halo",
    )(*(far(x) for x in (c, u, v, f)))
    from_west = shift(east, "tile", 1)
    from_east = shift(west, "tile", -1)
    send, rank, den = call(
        send_kernel,
        [arr((TILES, 32, LANES)), arr((1, SND), jnp.int32), arr((4, SUBS, LANES))],
        [spec(HBM)] * 4 + [spec()],
        [pltpu.VMEM((HERE, SND), F32)]
        + [pltpu.VMEM((1, SND), jnp.int32)] * 3
        + [pltpu.VMEM((ROWS, SND), F32), pltpu.VMEM((SUBS, SND), jnp.int32), pltpu.VMEM((SND, WIDE), BF16), pltpu.SemaphoreType.DMA((4,))],
        mib=28,
        flops=9 * 10**9,
        name="send",
    )(*(far(x) for x in (kernel, col, own, off)), part)
    send, from_west, from_east = lax.optimization_barrier((send, from_west, from_east))
    got = lax.all_to_all(send, "tile", 0, 0, tiled=True)
    adv = call(advect_kernel, arr((40, SUBS, LANES)), [spec()] * 8, name="advect")(
        c, u, v, f, part, from_west, from_east, den
    )
    others = [shift(adv, "lev", -d) for d in (1, 2, 3)]
    first = lax.axis_index("lev") * HERE
    twice = jnp.concatenate([mixing, mixing], axis=1)
    rows = lax.dynamic_slice(twice, (first, first), (HERE, 4 * HERE)).reshape(HERE, 4, HERE)
    rows = jnp.pad(rows, ((0, ROWS - HERE), (0, 0), (0, ROWS - HERE))).reshape(ROWS, 4 * ROWS)
    transported, field, weight = call(
        mix_kernel,
        [block, arr((SUBS, 2, ROWS, LANES)), arr((4, SUBS, LANES))],
        [spec()] * 5,
        name="mix",
    )(rows, adv, *others)
    sums = call(
        sample_kernel,
        arr((TILES, 3 * LANES)),
        [spec()] * 2,
        [pltpu.VMEM((8 * FIELD, WIDE), BF16)],
        mib=24,
        name="sample",
    )(got, field)
    back = lax.all_to_all(sums, "tile", 0, 0, tiled=True)
    mine = call(home_kernel, arr((8, SUBS, LANES)), [spec()] * 3, name="home")(back, own, rank)
    nums = [shift(mine, "lev", -d) for d in (1, 2, 3)]
    evolved = call(last_kernel, arr((2, SND)), [spec(SMEM)] + [spec()] * 5, name="last")(counts, mine, *nums, weight)
    out = transported.reshape(2 * HERE, 4, 2, LANES).transpose(0, 2, 1, 3).reshape(tracer.shape)
    return out, evolved


def solution(mesh):
    in_specs = (
        P(None, "lev", "tile", None),
        P("lev", "tile", None),
        P("lev", "tile", None),
        P(None, "tile", None),
        P(),
        P("lev", "tile"),
        P("tile"),
        P("tile"),
        P("tile"),
        P("tile"),
    )
    out_specs = (P(None, "lev", "tile", None), P(None, "tile"))
    return jax.shard_map(body, mesh=mesh, in_specs=in_specs, out_specs=out_specs, check_vma=False)
```

time: 119 us -> 89.2 us (0.75)
  blocking collectives: 0 us -> 19.6 us
  starting transfers between devices: 46.7 us -> 28.2 us
  Pallas kernels: 32.1 us -> 17 us
  waiting for transfers between devices: 34.6 us -> 21.5 us
  local copies, waits for them, and re-layouts: 3.16 us -> 1.04 us
    all_to_all x0 -> x1, blocking collectives: none -> 19.6 us  [body(): back = lax.all_to_all(sums, 'tile', 0, 0, tiled=True)]
    all_to_all x1 -> x0, starting transfers between devices: 10.7 us -> none  [body(): back = lax.all_to_all(sums, 'tile', 0, 0, tiled=True)]
    pallas_call x6, Pallas kernels: 17.4 us -> 8.24 us  [the longest x1 3.67 us: body(): call(sample_kernel, arr((TILES, 3 * LANES)), [spec()] * 2, [pltpu.VMEM((8...]
    all_to_all x1 -> x0, waiting for transfers between devices: 7.72 us -> none  [body(): back = lax.all_to_all(sums, 'tile', 0, 0, tiled=True)]
    ppermute x11 -> x8, starting transfers between devices: 25.5 us -> 18.1 us  [shift(): lax.ppermute(x, axis, [(i, (i + distance) % size) for i in range(size)])]
    pallas_call x1, Pallas kernels: 14.6 us -> 8.78 us  [body(): call(send_kernel, [arr((TILES, 32, LANES)), arr((1, SND), jnp.int32), arr...]
    ppermute x11 -> x8, waiting for transfers between devices: 26.9 us -> 21.5 us  [shift(): lax.ppermute(x, axis, [(i, (i + distance) % size) for i in range(size)])]
    unnamed x20 -> x13, local copies, waits for them, and re-layouts: 3.16 us -> 0.75 us
  transfers between devices with their start and end apart: 13 -> 9, of which waited for: 7 -> 4; matrix products, arithmetic and copies ran while one was open for 0% -> 0% of each run, Pallas kernels for 5% -> 2%
where the time goes in v2:
time: 89.2 us; the launch traced here: 88.8 us
  starting transfers between devices  28.2 us (32%)
  waiting for transfers between devices  21.5 us (24%)
  blocking collectives  19.6 us (22%)
  Pallas kernels  17 us (19%)
  between operations  1.45 us (2%)
  local copies, waits for them, and re-layouts  1.04 us (1%)
    ppermute x8, waiting for transfers between devices, shift(): lax.ppermute(x, axis, [(i, (i + distance) % size) for i in range(size)])  21.5 us
    all_to_all x1, blocking collectives, body(): back = lax.all_to_all(sums, 'tile', 0, 0, tiled=True)  19.6 us
    ppermute x8, starting transfers between devices, shift(): lax.ppermute(x, axis, [(i, (i + distance) % size) for i in range(size)])  18.1 us
    all_to_all x1, starting transfers between devices, body(): got = lax.all_to_all(send, 'tile', 0, 0, tiled=True)  10.1 us
    pallas_call x1, Pallas kernels, body(): call(send_kernel, [arr((TILES, 32, LANES)), arr((1, SND), jnp.int32), arr...  8.78 us
    pallas_call x1, Pallas kernels, body(): call(sample_kernel, arr((TILES, 3 * LANES)), [spec()] * 2, [pltpu.VMEM((8...  3.67 us
  transfers between devices with their start and end apart: 9, of which 4 were waited for; matrix products, arithmetic and copies ran while one was open for 0% of the time, Pallas kernels for 2%

profile of v2, /device:TPU:1, one launch (start us, length us, event | category | flops | bytes accessed | tf_op | source)
XLA Modules:
  0.0 88.8 jit_solution(4382197292067023722)
XLA Ops:
  0.6 1.2 %halo.1 = (f32[36,8,128]{2,1,0:T(8,128)S(1)}, f32[45,8,128]{2,1,0:T(8,128)S(1)}, f32[36,8,128]{2,1,0:T(8,128)S(1)}) custom-call(f32[36,8,128]{2,1,0:T(8,128)} %bitcast.32, f32[18,8,128]{2,1,0:T(8,128)} %bitcast.36, f32[18,8,128]{2,1,0:T(8,128)} %bitcast.38, f32[2,8,128]{2,1,0:T(8,128)} %bitcast.40), custom_call_target="tpu_custom_call" | custom-call | flops 1000000 | bytes 100000 | tf_op jit(solution)/shard_map/halo/pallas_call | solution.py:365
  1.9 3.1 %collective-permute-start = (f32[36,8,128]{2,1,0:T(8,128)S(1)}, f32[36,8,128]{2,1,0:T(8,128)S(1)}, u32[]{:S(2)}, u32[]{:S(2)}) collective-permute-start(f32[36,8,128]{2,1,0:T(8,128)S(1)} %get-tuple-element.16), channel_id=1, source_target_pairs={{0,4},{4,8},{8,12},{12,16},{16,20},{20,24},{24,28},{28,32},{32,36}... | collective-permute-start | bytes 442376 | tf_op jit(solution)/shard_map/ppermute | solution.py:358
  5.0 0.3 collective-permute-start.1
  5.3 8.8 %send.1 = (f32[64,32,128]{2,1,0:T(8,128)}, s32[1,4096]{1,0:T(1,128)S(1)}, f32[4,8,128]{2,1,0:T(8,128)S(1)}) custom-call(f32[18,4096]{1,0:T(8,128)} %kern_in.1, s32[1,4096]{1,0:T(1,128)} %bitcast.45, s32[1,4096]{1,0:T(1,128)} %bitcast.42, s32[1,4096]{1,0:T(1,128)} %bitcast.46, f32[36,8,128]{2,1,0:T(8,128)S(1)} %get-tuple-element.14.part_ref), custom_call_target="tpu_custom_call" | custom-call | flops 8999999488 | bytes 100000 | tf_op jit(solution)/shard_map/send/pallas_call | solution.py:380
  14.1 0.0 collective-permute-done.a_ref
  14.1 0.0 collective-permute-done.1.b_ref
  14.1 0.0 copy-start
  14.1 0.0 copy-start.1
  14.1 0.0 copy-start.2
  14.1 0.0 copy-start.3
  14.1 10.1 %all-to-all-start = ((f32[64,32,128]{2,1,0:T(8,128)}), f32[64,32,128]{2,1,0:T(8,128)S(1)}, u32[]{:S(2)}, u32[]{:S(2)}) async-start(f32[64,32,128]{2,1,0:T(8,128)} %get-tuple-element.22), calls=%async_computation | async-start | bytes 2097152 | tf_op jit(solution)/shard_map/all_to_all | solution.py:392
  24.2 0.0 copy-done
  24.2 0.0 copy-done.1
  24.3 0.0 copy-done.2
  24.3 0.0 copy-done.3
  24.3 0.0 copy-start.5
  24.3 0.2 advect.1.x0_ref
  24.5 1.9 %collective-permute-start.4 = (f32[40,8,128]{2,1,0:T(8,128)S(1)}, f32[40,8,128]{2,1,0:T(8,128)S(1)}, u32[]{:S(2)}, u32[]{:S(2)}) collective-permute-start(f32[40,8,128]{2,1,0:T(8,128)S(1)} %advect.1.x0_ref), channel_id=1, source_target_pairs={{0,1},{1,2},{2,3},{3,0},{4,5},{5,6},{6,7},{7,4},{8,9},{9,10},{10,1... | collective-permute-start | bytes 491528 | tf_op jit(solution)/shard_map/ppermute | solution.py:358
  26.4 4.7 %collective-permute-start.3 = (f32[40,8,128]{2,1,0:T(8,128)S(1)}, f32[40,8,128]{2,1,0:T(8,128)S(1)}, u32[]{:S(2)}, u32[]{:S(2)}) collective-permute-start(f32[40,8,128]{2,1,0:T(8,128)S(1)} %advect.1.x0_ref), channel_id=1, source_target_pairs={{0,2},{1,3},{2,0},{3,1},{4,6},{5,7},{6,4},{7,5},{8,10},{9,11},{10,... | collective-permute-start | bytes 491528 | tf_op jit(solution)/shard_map/ppermute | solution.py:358
  31.1 2.4 %collective-permute-start.2 = (f32[40,8,128]{2,1,0:T(8,128)S(1)}, f32[40,8,128]{2,1,0:T(8,128)S(1)}, u32[]{:S(2)}, u32[]{:S(2)}) collective-permute-start(f32[40,8,128]{2,1,0:T(8,128)S(1)} %advect.1.x0_ref), channel_id=1, source_target_pairs={{0,3},{1,0},{2,1},{3,2},{4,7},{5,4},{6,5},{7,6},{8,11},{9,8},{10,9... | collective-permute-start | bytes 491528 | tf_op jit(solution)/shard_map/ppermute | solution.py:358
  33.4 0.0 copy-done.5
  33.4 0.1 fusion
  33.5 0.1 reshape.51
  33.6 0.1 reshape.52.mix_ref
  33.7 13.7 %collective-permute-done.4.x3_ref = f32[40,8,128]{2,1,0:T(8,128)S(1)} collective-permute-done((f32[40,8,128]{2,1,0:T(8,128)S(1)}, f32[40,8,128]{2,1,0:T(8,128)S(1)}, u32[]{:S(2)}, u32[]{:S(2)}) %collective-permute-start.4) | collective-permute-done | bytes 163872 | tf_op jit(solution)/shard_map/ppermute | solution.py:358
  47.5 4.8 %collective-permute-done.3.x2_ref = f32[40,8,128]{2,1,0:T(8,128)S(1)} collective-permute-done((f32[40,8,128]{2,1,0:T(8,128)S(1)}, f32[40,8,128]{2,1,0:T(8,128)S(1)}, u32[]{:S(2)}, u32[]{:S(2)}) %collective-permute-start.3) | collective-permute-done | bytes 163872 | tf_op jit(solution)/shard_map/ppermute | solution.py:358
  52.3 0.0 collective-permute-done.2.x1_ref
  52.3 1.2 %mix.1 = (f32[36,8,128]{2,1,0:T(8,128)}, f32[8,2,24,128]{3,2,1,0:T(8,128)S(1)}, f32[4,8,128]{2,1,0:T(8,128)S(1)}) custom-call(f32[24,96]{1,0:T(8,128)S(1)} %reshape.52.mix_ref, f32[40,8,128]{2,1,0:T(8,128)S(1)} %advect.1.x0_ref, f32[40,8,128]{2,1,0:T(8,128)S(1)} %collective-permute-done.2.x1_ref, f32[40,8,128]{2,1,0:T(8,128)S(1)} %collective-permute-done.3.x2_ref, ...), custom_call_target="tpu_custom_call" | custom-call | flops 1000000 | bytes 100000 | tf_op jit(solution)/shard_map/mix/pallas_call | solution.py:401
  53.4 0.0 all-to-all-done.got_ref
  53.4 3.7 %sample.1 = f32[64,384]{1,0:T(8,128)S(1)} custom-call(f32[64,32,128]{2,1,0:T(8,128)S(1)} %all-to-all-done.got_ref, f32[8,2,24,128]{3,2,1,0:T(8,128)S(1)} %get-tuple-element.23.field_ref), custom_call_target="tpu_custom_call" | custom-call | flops 1000000 | bytes 100000 | tf_op jit(solution)/shard_map/sample/pallas_call | solution.py:407
  57.1 0.1 copy.22
  57.2 19.6 %all_to_all.16 = f32[64,1,384]{2,1,0:T(1,128)S(1)} all-to-all(f32[64,1,384]{2,1,0:T(1,128)S(1)} %copy.22), channel_id=1, replica_groups=mesh['tile'=64,'lev'=4] {'tile'}, dimensions={0} | all-to-all | bytes 196608 | tf_op jit(solution)/shard_map/all_to_all | solution.py:415
  76.8 0.0 copy-start.4
  76.8 0.7 copy-done.4
  77.5 1.3 %home.1.a_ref = f32[8,8,128]{2,1,0:T(8,128)S(1)} custom-call(f32[64,384]{1,0:T(8,128)S(1)} %bitcast.34, s32[1,4096]{1,0:T(1,128)S(1)} %bitcast.43, s32[1,4096]{1,0:T(1,128)S(1)} %get-tuple-element.24.rank_ref), custom_call_target="tpu_custom_call" | custom-call | flops 1000000 | bytes 100000 | tf_op jit(solution)/shard_map/home/pallas_call | solution.py:416
  78.9 1.2 %collective-permute-start.7 = (f32[8,8,128]{2,1,0:T(8,128)S(1)}, f32[8,8,128]{2,1,0:T(8,128)S(1)}, u32[]{:S(2)}, u32[]{:S(2)}) collective-permute-start(f32[8,8,128]{2,1,0:T(8,128)S(1)} %home.1.a_ref), channel_id=1, source_target_pairs={{0,1},{1,2},{2,3},{3,0},{4,5},{5,6},{6,7},{7,4},{8,9},{9,10},{10,1... | collective-permute-start | bytes 98312 | tf_op jit(solution)/shard_map/ppermute | solution.py:358
  80.1 1.1 %collective-permute-start.6 = (f32[8,8,128]{2,1,0:T(8,128)S(1)}, f32[8,8,128]{2,1,0:T(8,128)S(1)}, u32[]{:S(2)}, u32[]{:S(2)}) collective-permute-start(f32[8,8,128]{2,1,0:T(8,128)S(1)} %home.1.a_ref), channel_id=1, source_target_pairs={{0,2},{1,3},{2,0},{3,1},{4,6},{5,7},{6,4},{7,5},{8,10},{9,11},{10,... | collective-permute-start | bytes 98312 | tf_op jit(solution)/shard_map/ppermute | solution.py:358
  81.1 3.5 %collective-permute-start.5 = (f32[8,8,128]{2,1,0:T(8,128)S(1)}, f32[8,8,128]{2,1,0:T(8,128)S(1)}, u32[]{:S(2)}, u32[]{:S(2)}) collective-permute-start(f32[8,8,128]{2,1,0:T(8,128)S(1)} %home.1.a_ref), channel_id=1, source_target_pairs={{0,3},{1,0},{2,1},{3,2},{4,7},{5,4},{6,5},{7,6},{8,11},{9,8},{10,9... | collective-permute-start | bytes 98312 | tf_op jit(solution)/shard_map/ppermute | solution.py:358
  85.3 0.0 collective-permute-done.7.d_ref
  85.3 1.5 %collective-permute-done.6.c_ref = f32[8,8,128]{2,1,0:T(8,128)S(1)} collective-permute-done((f32[8,8,128]{2,1,0:T(8,128)S(1)}, f32[8,8,128]{2,1,0:T(8,128)S(1)}, u32[]{:S(2)}, u32[]{:S(2)}) %collective-permute-start.6) | collective-permute-done | bytes 32800 | tf_op jit(solution)/shard_map/ppermute | solution.py:358
  86.8 1.4 %collective-permute-done.5.b_ref = f32[8,8,128]{2,1,0:T(8,128)S(1)} collective-permute-done((f32[8,8,128]{2,1,0:T(8,128)S(1)}, f32[8,8,128]{2,1,0:T(8,128)S(1)}, u32[]{:S(2)}, u32[]{:S(2)}) %collective-permute-start.5) | collective-permute-done | bytes 32800 | tf_op jit(solution)/shard_map/ppermute | solution.py:358
  88.2 0.6 last.1
  (2 shorter events, 0.0 us)
Async XLA Ops:
  1.9 12.2 %collective-permute-start = (f32[36,8,128]{2,1,0:T(8,128)S(1)}, f32[36,8,128]{2,1,0:T(8,128)S(1)}, u32[]{:S(2)}, u32[]{:S(2)}) collective-permute-start(f32[36,8,128]{2,1,0:T(8,128)S(1)} %get-tuple-element.16), channel_id=1, source_target_pairs={{0,4},{4,8},{8,12},{12,16},{16,20},{20,24},{24,28},{28,32},{32,36}... | collective-permute-start | bytes 442376 | tf_op jit(solution)/shard_map/ppermute | solution.py:358
  5.0 9.1 %collective-permute-start.1 = (f32[45,8,128]{2,1,0:T(8,128)S(1)}, f32[45,8,128]{2,1,0:T(8,128)S(1)}, u32[]{:S(2)}, u32[]{:S(2)}) collective-permute-start(f32[45,8,128]{2,1,0:T(8,128)S(1)} %get-tuple-element.17), channel_id=1, source_target_pairs={{0,252},{4,0},{8,4},{12,8},{16,12},{20,16},{24,20},{28,24},{32,28}... | collective-permute-start | bytes 552968 | tf_op jit(solution)/shard_map/ppermute | solution.py:358
  14.1 10.2 %copy-start = (f32[2,18,2,512]{3,2,1,0:T(2,128)S(1)}, f32[2,18,2,512]{3,2,1,0:T(2,128)}, u32[]{:S(2)}) copy-start(f32[2,18,2,512]{3,2,1,0:T(2,128)} %param.10) | copy-start | bytes 442372
  14.1 10.2 %copy-start.1 = (f32[18,2,512]{2,1,0:T(2,128)S(1)}, f32[18,2,512]{2,1,0:T(2,128)}, u32[]{:S(2)}) copy-start(f32[18,2,512]{2,1,0:T(2,128)} %param.11) | copy-start | bytes 221188
  14.1 10.2 %copy-start.2 = (f32[18,2,512]{2,1,0:T(2,128)S(1)}, f32[18,2,512]{2,1,0:T(2,128)}, u32[]{:S(2)}) copy-start(f32[18,2,512]{2,1,0:T(2,128)} %param.12) | copy-start | bytes 221188
  14.1 10.2 %copy-start.3 = (f32[2,2,512]{2,1,0:T(2,128)S(1)}, f32[2,2,512]{2,1,0:T(2,128)}, u32[]{:S(2)}) copy-start(f32[2,2,512]{2,1,0:T(2,128)} %param.13) | copy-start | bytes 24580
  14.1 39.3 %all-to-all-start = ((f32[64,32,128]{2,1,0:T(8,128)}), f32[64,32,128]{2,1,0:T(8,128)S(1)}, u32[]{:S(2)}, u32[]{:S(2)}) async-start(f32[64,32,128]{2,1,0:T(8,128)} %get-tuple-element.22), calls=%async_computation | async-start | bytes 2097152 | tf_op jit(solution)/shard_map/all_to_all | solution.py:392
  24.3 9.2 %copy-start.5 = (f32[72,72]{1,0:T(8,128)S(1)}, f32[72,72]{1,0:T(8,128)}, u32[]{:S(2)}) copy-start(f32[72,72]{1,0:T(8,128)} %param.14) | copy-start | bytes 62212
  24.5 22.9 %collective-permute-start.4 = (f32[40,8,128]{2,1,0:T(8,128)S(1)}, f32[40,8,128]{2,1,0:T(8,128)S(1)}, u32[]{:S(2)}, u32[]{:S(2)}) collective-permute-start(f32[40,8,128]{2,1,0:T(8,128)S(1)} %advect.1.x0_ref), channel_id=1, source_target_pairs={{0,1},{1,2},{2,3},{3,0},{4,5},{5,6},{6,7},{7,4},{8,9},{9,10},{10,1... | collective-permute-start | bytes 491528 | tf_op jit(solution)/shard_map/ppermute | solution.py:358
  26.4 25.9 %collective-permute-start.3 = (f32[40,8,128]{2,1,0:T(8,128)S(1)}, f32[40,8,128]{2,1,0:T(8,128)S(1)}, u32[]{:S(2)}, u32[]{:S(2)}) collective-permute-start(f32[40,8,128]{2,1,0:T(8,128)S(1)} %advect.1.x0_ref), channel_id=1, source_target_pairs={{0,2},{1,3},{2,0},{3,1},{4,6},{5,7},{6,4},{7,5},{8,10},{9,11},{10,... | collective-permute-start | bytes 491528 | tf_op jit(solution)/shard_map/ppermute | solution.py:358
  31.1 21.2 %collective-permute-start.2 = (f32[40,8,128]{2,1,0:T(8,128)S(1)}, f32[40,8,128]{2,1,0:T(8,128)S(1)}, u32[]{:S(2)}, u32[]{:S(2)}) collective-permute-start(f32[40,8,128]{2,1,0:T(8,128)S(1)} %advect.1.x0_ref), channel_id=1, source_target_pairs={{0,3},{1,0},{2,1},{3,2},{4,7},{5,4},{6,5},{7,6},{8,11},{9,8},{10,9... | collective-permute-start | bytes 491528 | tf_op jit(solution)/shard_map/ppermute | solution.py:358
  76.8 0.7 copy-start.4
  78.9 6.4 %collective-permute-start.7 = (f32[8,8,128]{2,1,0:T(8,128)S(1)}, f32[8,8,128]{2,1,0:T(8,128)S(1)}, u32[]{:S(2)}, u32[]{:S(2)}) collective-permute-start(f32[8,8,128]{2,1,0:T(8,128)S(1)} %home.1.a_ref), channel_id=1, source_target_pairs={{0,1},{1,2},{2,3},{3,0},{4,5},{5,6},{6,7},{7,4},{8,9},{9,10},{10,1... | collective-permute-start | bytes 98312 | tf_op jit(solution)/shard_map/ppermute | solution.py:358
  80.1 6.7 %collective-permute-start.6 = (f32[8,8,128]{2,1,0:T(8,128)S(1)}, f32[8,8,128]{2,1,0:T(8,128)S(1)}, u32[]{:S(2)}, u32[]{:S(2)}) collective-permute-start(f32[8,8,128]{2,1,0:T(8,128)S(1)} %home.1.a_ref), channel_id=1, source_target_pairs={{0,2},{1,3},{2,0},{3,1},{4,6},{5,7},{6,4},{7,5},{8,10},{9,11},{10,... | collective-permute-start | bytes 98312 | tf_op jit(solution)/shard_map/ppermute | solution.py:358
  81.1 7.0 %collective-permute-start.5 = (f32[8,8,128]{2,1,0:T(8,128)S(1)}, f32[8,8,128]{2,1,0:T(8,128)S(1)}, u32[]{:S(2)}, u32[]{:S(2)}) collective-permute-start(f32[8,8,128]{2,1,0:T(8,128)S(1)} %home.1.a_ref), channel_id=1, source_target_pairs={{0,3},{1,0},{2,1},{3,2},{4,7},{5,4},{6,5},{7,6},{8,11},{9,8},{10,9... | collective-permute-start | bytes 98312 | tf_op jit(solution)/shard_map/ppermute | solution.py:358

commit v3 on v2

--- a/solution.py
+++ b/solution.py
@@ -11,7 +11,11 @@
 ROWS = 24
 TILES = 64
 WIDE = 256
-QUADS = 4
+QUADS = 8
+ORDER = "H"
+MARK = 1000000
+MIX = 100000000000
+RELAY = False
 SND = 4096
 F32 = jnp.float32
 BF16 = jnp.bfloat16
@@ -65,9 +69,10 @@
     return c + jnp.where(lax.axis_index("lev") == 0, f_ref[s], 0.0)
 
 
-def halo_kernel(c_in, u_in, v_in, f_in, east_ref, west_ref, part_ref, c_ref, u_ref, v_ref, f_ref, sem):
+def halo_kernel(c_in, u_in, v_in, f_in, near_ref, far_ref, part_ref, c_ref, u_ref, v_ref, f_ref, sem):
     fetch(((c_in, c_ref), (u_in, u_ref), (v_in, v_ref), (f_in, f_ref)), sem)
     first = iota((SUBS, LANES), 0) % 2 == 0
+    even = lax.axis_index("tile") % 2 == 0
     for level in range(HERE):
         u, v = u_ref[level], v_ref[level]
         for s in range(2):
@@ -75,24 +80,31 @@
             c = surfaced(c_ref, f_ref, s, level)
             y = inner(c, u, v, first)
             part_ref[row] = y
-            east_ref[row] = jnp.where(first, roll(c, -1, 0), y)
-            west_ref[row] = jnp.where(first, y, roll(c, 1, 0))
+            east = jnp.where(first, roll(c, -1, 0), y)
+            west = jnp.where(first, y, roll(c, 1, 0))
+            near_ref[row] = jnp.where(even, east, west)
+            far_ref[row] = jnp.where(even, west, east)
     for level in range(HERE // 2):
-        west_ref[2 * HERE + level] = jnp.where(first, u_ref[level], roll(u_ref[level + HERE // 2], 1, 0))
-
-
-def advect_kernel(c_ref, u_ref, v_ref, f_ref, part_ref, a_ref, b_ref, den_ref, out_ref):
+        u = jnp.where(first, u_ref[level], roll(u_ref[level + HERE // 2], 1, 0))
+        near_ref[2 * HERE + level] = u
+        far_ref[2 * HERE + level] = u
+
+
+def advect_kernel(c_ref, u_ref, v_ref, f_ref, part_ref, near_ref, far_ref, den_ref, out_ref):
+    even = lax.axis_index("tile") % 2 == 0
     first = iota((SUBS, LANES), 0) % 2 == 0
     for level in range(HERE):
         u, v = u_ref[level], v_ref[level]
-        packed = b_ref[2 * HERE + level % (HERE // 2)]
+        row = 2 * HERE + level % (HERE // 2)
+        packed = jnp.where(even, near_ref[row], far_ref[row])
         beyond = roll(packed, 1, 0) if level < HERE // 2 else packed
         outer = jnp.where(first, u, beyond)
         forward = outer > 0
         for s in range(2):
             row = s * HERE + level
             c = surfaced(c_ref, f_ref, s, level)
-            a, b = a_ref[row], b_ref[row]
+            a = jnp.where(even, far_ref[row], near_ref[row])
+            b = jnp.where(even, near_ref[row], far_ref[row])
             flux = outer * jnp.where(forward, jnp.where(first, a, c), jnp.where(first, c, b))
             own = part_ref[row] + jnp.where(first, flux, -flux)
             near = swap(jnp.where(first, b + roll(flux, -1, 0), a - roll(flux, 1, 0)), first)
@@ -102,8 +114,31 @@
         out_ref[2 * HERE + row] = den_ref[row]
 
 
-def mix_kernel(mix_ref, x0_ref, x1_ref, x2_ref, x3_ref, out_ref, field_ref, den_ref):
-    refs = (x0_ref, x1_ref, x2_ref, x3_ref)
+def mark_kernel(x_ref, out_ref):
+    out_ref[...] = x_ref[0]
+
+
+def mix_kernel(mix_ref, mark_ref, *refs):
+    *refs, out_ref, field_ref, den_ref = refs
+    size = 2 * HERE + 4
+
+    def block(d, row, count, sub):
+        if d == 2 and len(refs) == 5:
+            lower, upper = refs[2:4]
+            cut = size // 2
+            parts = []
+            if row < cut:
+                parts.append(lower[row : min(row + count, cut), sub, :])
+            if row + count > cut:
+                parts.append(upper[max(row - cut, 0) : row + count - cut, sub, :])
+            return parts[0] if len(parts) == 1 else jnp.concatenate(parts, axis=0)
+        return refs[d if d < 3 else -1][row : row + count, sub, :]
+
+    def weights(d, row):
+        if d == 2 and len(refs) == 5:
+            return refs[3][row - size // 2]
+        return refs[d if d < 3 else -1][row]
+
     high, low = split(mix_ref[...])
     both = jnp.concatenate([high.astype(F32), low.astype(F32)], axis=0).astype(BF16)
     pad = jnp.zeros((ROWS - HERE, 2 * LANES), F32)
@@ -111,8 +146,8 @@
         rows = slice(s * HERE, (s + 1) * HERE)
         for sub in range(0, SUBS, 2):
             parts = []
-            for ref in refs:
-                parts += [jnp.concatenate([ref[rows, sub, :], ref[rows, sub + 1, :]], axis=1), pad]
+            for d in range(4):
+                parts += [jnp.concatenate([block(d, s * HERE, HERE, sub + i) for i in range(2)], axis=1), pad]
             x_high, x_low = split(jnp.concatenate(parts, axis=0))
             r = jnp.dot(both, x_high, preferred_element_type=F32)
             mixed = r[0:ROWS] + r[ROWS:] + jnp.dot(high, x_low, preferred_element_type=F32)
@@ -121,7 +156,7 @@
                 field_ref[sub + i, s] = half
                 out_ref[rows, sub + i, :] = half[0:HERE]
     for row in range(4):
-        a, b, c, d = (ref[2 * HERE + row] for ref in refs)
+        a, b, c, d = (weights(i, 2 * HERE + row) for i in range(4))
         den_ref[row] = (a + c) + (b + d)
 
 
@@ -132,32 +167,23 @@
     return group, lane
 
 
-def fetch(pairs, sem):
+def fetch(pairs, sem, needed=None):
     copies = [pltpu.make_async_copy(a, b, sem.at[i]) for i, (a, b) in enumerate(pairs)]
     for copy in copies:
         copy.start()
-    for copy in copies:
+    for copy in copies[:needed]:
         copy.wait()
+    return copies[needed:] if needed else []
+
+
+BOTH = 40
 
 
 def send_kernel(
-    kern_in, col_in, own_in, off_in, part_ref, send_ref, rank_ref, den_ref,
+    kern_in, col_in, own_in, off_in, part_ref, send_ref, place_ref, den_ref,
     kern_ref, col_ref, own_ref, off_ref, w_ref, grp_ref, hot_ref, sem,
 ):
-    fetch(((kern_in, kern_ref), (col_in, col_ref), (own_in, own_ref), (off_in, off_ref)), sem)
-    z = lax.axis_index("lev")
-    levels = z * HERE + iota((HERE, SND), 0)
-    weighted = jnp.where(levels >= off_ref[...], kern_ref[...], 0.0)
-    den = jnp.sum(weighted, axis=0, keepdims=True)
-    for j in range(SND // LANES):
-        den_ref[j // SUBS, j % SUBS : j % SUBS + 1, :] = den[:, j * LANES : (j + 1) * LANES]
-    col = col_ref[...].astype(F32)
-    w_ref[0:HERE, :] = weighted
-    w_ref[HERE : HERE + 1, :] = col
-    w_ref[HERE + 1 : HERE + 3, :] = weighted[HERE - 2 : HERE]
-    w_ref[HERE + 3 : HERE + 4, :] = col
-    w_ref[HERE + 4 : ROWS, :] = jnp.zeros((2, SND), F32)
-
+    rest = fetch(((own_in, own_ref), (off_in, off_ref), (col_in, col_ref), (kern_in, kern_ref)), sem, 1)
     before = (iota((WIDE, WIDE), 0) < iota((WIDE, WIDE), 1)).astype(BF16)
     slot = iota((WIDE, 1), 0)
     carry = jnp.zeros((TILES, 1), F32)
@@ -168,45 +194,66 @@
         prefix = jnp.dot(onehot.astype(BF16), before, preferred_element_type=F32)
         rank = jnp.sum(onehot * (prefix + carry), axis=0, keepdims=True).astype(jnp.int32)
         carry = carry + jnp.sum(onehot, axis=1, keepdims=True)
-        rank_ref[:, at] = rank
+        place_ref[:, at] = own * WIDE + rank
         group, lane = place(own, rank)
         grp_ref[:, at] = jnp.broadcast_to(group, (SUBS, WIDE))
         hot_ref[at, :] = (slot == lane).astype(F32).T.astype(BF16)
 
-    quads, chunk = 8, 1024
+    for copy in rest:
+        copy.wait()
+    z = lax.axis_index("lev")
+    levels = z * HERE + iota((HERE, SND), 0)
+    weighted = jnp.where(levels >= off_ref[...], kern_ref[...], 0.0)
+    den = jnp.sum(weighted, axis=0, keepdims=True)
+    for j in range(SND // LANES):
+        den_ref[j // SUBS, j % SUBS : j % SUBS + 1, :] = den[:, j * LANES : (j + 1) * LANES]
+    col = col_ref[...]
+    high = weighted.astype(BF16).astype(F32)
+    col_high = (col & ~3).astype(F32)
+    last = slice(HERE - 2, HERE)
+    w_ref[0:16, :] = high[0:16]
+    w_ref[16:32, :] = (weighted - high)[0:16]
+    w_ref[32:34, :] = high[last]
+    w_ref[34:35, :] = col_high
+    w_ref[35:37, :] = (weighted - high)[last]
+    w_ref[37:38, :] = (col & 3).astype(F32)
+    w_ref[38:40, :] = jnp.zeros((2, SND), F32)
+
+    quads, chunk = 16, 512
     sub, left = iota((SUBS, LANES), 0), iota((SUBS, LANES), 1) < 64
 
     def some(i, _):
-        acc = jnp.zeros((quads * 3 * 2 * ROWS, WIDE), F32)
+        acc = jnp.zeros((quads * 3 * BOTH, WIDE), F32)
         for b in range(SND // chunk):
             at = pl.ds(b * chunk, chunk)
             w = w_ref[:, at]
-            high = w.astype(BF16).astype(F32)
-            low = w - high
-            group = jnp.concatenate([grp_ref[:, at]] * 3, axis=0)
+            group = grp_ref[:, at]
             rows = []
             for j in range(quads * 3):
                 here = group == i * quads * 3 + j
-                rows += [jnp.where(here, high, 0.0), jnp.where(here, low, 0.0)]
+                rows += [jnp.where(here, w[k : k + SUBS], 0.0) for k in range(0, BOTH, SUBS)]
             lhs = jnp.concatenate(rows, axis=0).astype(BF16)
             acc = acc + jnp.dot(lhs, hot_ref[at, :], preferred_element_type=F32)
         for q in range(quads):
             sums = []
             for j in range(3):
-                base = (q * 3 + j) * 2 * ROWS
-                sums.append(acc[base : base + ROWS] + acc[base + ROWS : base + 2 * ROWS])
+                base = (q * 3 + j) * BOTH
+                third = acc[base + 32 : base + 40]
+                third = third + roll(third, 3 if j == 2 else -3, 0)
+                sums.append((acc[base : base + 16] + acc[base + 16 : base + 32], third))
             for k in range(4):
                 t = (i * quads + q) * 4 + k
-                top = sums[k // 2][:, (k % 2) * LANES : (k % 2 + 1) * LANES]
-                rest = sums[2][:, (k // 2) * LANES : (k // 2 + 1) * LANES]
-                middle = rest[16:24]
+                mine = slice((k % 2) * LANES, (k % 2 + 1) * LANES)
+                pair = slice((k // 2) * LANES, (k // 2 + 1) * LANES)
+                top, third = (x[:, mine] for x in sums[k // 2])
+                rest, middle = (x[:, pair] for x in sums[2])
                 if k % 2 == 0:
                     bottom = jnp.where(left, rest[0:8], roll(rest[8:16], 64, 1))
                 else:
                     bottom = jnp.where(left, roll(rest[0:8], 64, 1), rest[8:16])
                     middle = roll(middle, 64, 1)
-                send_ref[t, 0:16, :] = top[0:16]
-                send_ref[t, 16:24, :] = jnp.where(sub < 3, top[16:24], middle)
+                send_ref[t, 0:16, :] = top
+                send_ref[t, 16:24, :] = jnp.where(sub < 3, third, jnp.where(sub < 6, middle, 0.0))
                 send_ref[t, 24:32, :] = bottom
         return 0
 
@@ -292,7 +339,7 @@
     lax.fori_loop(0, TILES // (4 * quads), some, 0)
 
 
-def home_kernel(back_ref, own_ref, rank_ref, out_ref):
+def home_kernel(back_ref, place_ref, out_ref):
     tail = back_ref[:, 2 * LANES : 3 * LANES]
     first = jnp.concatenate([back_ref[:, 0:LANES], tail], axis=1)
     second = jnp.concatenate([back_ref[:, LANES : 2 * LANES], roll(tail, 64, 1)], axis=1)
@@ -300,9 +347,9 @@
     slot = iota((WIDE, 1), 0)
     for b in range(SND // WIDE):
         at = pl.ds(b * WIDE, WIDE)
-        hot = (slot == rank_ref[:, at]).astype(F32).astype(BF16)
+        hot = (slot == (place_ref[:, at] & (WIDE - 1))).astype(F32).astype(BF16)
         values = jnp.dot(high, hot, preferred_element_type=F32) + jnp.dot(low, hot, preferred_element_type=F32)
-        mine = iota((TILES, WIDE), 0) == own_ref[:, at]
+        mine = iota((TILES, WIDE), 0) == (place_ref[:, at] >> 8)
         for s in range(2):
             picked = jnp.where(mine, values[s * TILES : (s + 1) * TILES], 0.0)
             total = jnp.sum(picked, axis=0, keepdims=True)
@@ -349,6 +396,12 @@
     return x.reshape(rows, 2, 4, LANES).transpose(0, 2, 1, 3).reshape(rows, SUBS, LANES)
 
 
+def swapped(x, start):
+    size = lax.axis_size("tile")
+    pairs = [((i + start) % size, (i + start + 1) % size) for i in range(0, size, 2)]
+    return lax.ppermute(x, "tile", pairs + [(b, a) for a, b in pairs])
+
+
 def far(x):
     return pltpu.with_memory_space_constraint(x, HBM)
 
@@ -362,9 +415,9 @@
     c, u, v, f = (registers(x) for x in (tracer, u_courant, v_courant, surface_flux))
     col, own, off = (x.reshape(1, SND) for x in (column, owner_tile, offset))
     block = arr((2 * HERE, SUBS, LANES))
-    east, west, part = call(
+    near_half, far_half, part = call(
         halo_kernel,
-        [block, arr((45, SUBS, LANES)), block],
+        [arr((45, SUBS, LANES)), arr((45, SUBS, LANES)), block],
         [spec(HBM)] * 4,
         [
             pltpu.VMEM((2 * HERE, SUBS, LANES), F32),
@@ -375,25 +428,42 @@
         ],
         name="halo",
     )(*(far(x) for x in (c, u, v, f)))
-    from_west = shift(east, "tile", 1)
-    from_east = shift(west, "tile", -1)
-    send, rank, den = call(
+    from_near, from_far = swapped(near_half, 0), swapped(far_half, 1)
+    send, place_of, den = call(
         send_kernel,
         [arr((TILES, 32, LANES)), arr((1, SND), jnp.int32), arr((4, SUBS, LANES))],
         [spec(HBM)] * 4 + [spec()],
         [pltpu.VMEM((HERE, SND), F32)]
         + [pltpu.VMEM((1, SND), jnp.int32)] * 3
-        + [pltpu.VMEM((ROWS, SND), F32), pltpu.VMEM((SUBS, SND), jnp.int32), pltpu.VMEM((SND, WIDE), BF16), pltpu.SemaphoreType.DMA((4,))],
+        + [pltpu.VMEM((BOTH, SND), F32), pltpu.VMEM((SUBS, SND), jnp.int32), pltpu.VMEM((SND, WIDE), BF16), pltpu.SemaphoreType.DMA((4,))],
         mib=28,
         flops=9 * 10**9,
         name="send",
     )(*(far(x) for x in (kernel, col, own, off)), part)
-    send, from_west, from_east = lax.optimization_barrier((send, from_west, from_east))
-    got = lax.all_to_all(send, "tile", 0, 0, tiled=True)
+    if ORDER == "A":
+        send, from_west, from_east = lax.optimization_barrier((send, from_west, from_east))
+        got = lax.all_to_all(send, "tile", 0, 0, tiled=True)
     adv = call(advect_kernel, arr((40, SUBS, LANES)), [spec()] * 8, name="advect")(
-        c, u, v, f, part, from_west, from_east, den
+        c, u, v, f, part, from_near, from_far, den
     )
-    others = [shift(adv, "lev", -d) for d in (1, 2, 3)]
+    up, down = shift(adv, "lev", -1), shift(adv, "lev", 1)
+    if ORDER == "B":
+        send, adv = lax.optimization_barrier((send, adv))
+        got = lax.all_to_all(send, "tile", 0, 0, tiled=True)
+    if ORDER == "C":
+        send, up = lax.optimization_barrier((send, up))
+        got = lax.all_to_all(send, "tile", 0, 0, tiled=True)
+    if ORDER == "H":
+        mark = call(mark_kernel, arr((SUBS, LANES)), [spec()], flops=MARK, name="mark")(adv)
+        send, mark = lax.optimization_barrier((send, mark))
+        got = lax.all_to_all(send, "tile", 0, 0, tiled=True)
+    if RELAY:
+        across = [shift(up[:20], "lev", -1), shift(down[20:], "lev", 1)]
+    else:
+        across = [shift(adv, "lev", 2)]
+    if ORDER == "D":
+        send, *across = lax.optimization_barrier((send, *across))
+        got = lax.all_to_all(send, "tile", 0, 0, tiled=True)
     first = lax.axis_index("lev") * HERE
     twice = jnp.concatenate([mixing, mixing], axis=1)
     rows = lax.dynamic_slice(twice, (first, first), (HERE, 4 * HERE)).reshape(HERE, 4, HERE)
@@ -401,9 +471,10 @@
     transported, field, weight = call(
         mix_kernel,
         [block, arr((SUBS, 2, ROWS, LANES)), arr((4, SUBS, LANES))],
-        [spec()] * 5,
+        [spec()] * (5 + len(across)),
+        flops=MIX,
         name="mix",
-    )(rows, adv, *others)
+    )(rows, mark, adv, up, *across, down)
     sums = call(
         sample_kernel,
         arr((TILES, 3 * LANES)),
@@ -413,7 +484,7 @@
         name="sample",
     )(got, field)
     back = lax.all_to_all(sums, "tile", 0, 0, tiled=True)
-    mine = call(home_kernel, arr((8, SUBS, LANES)), [spec()] * 3, name="home")(back, own, rank)
+    mine = call(home_kernel, arr((8, SUBS, LANES)), [spec()] * 2, name="home")(back, place_of)
     nums = [shift(mine, "lev", -d) for d in (1, 2, 3)]
     evolved = call(last_kernel, arr((2, SND)), [spec(SMEM)] + [spec()] * 5, name="last")(counts, mine, *nums, weight)
     out = transported.reshape(2 * HERE, 4, 2, LANES).transpose(0, 2, 1, 3).reshape(tracer.shape)

time: 89.2 us -> 80.2 us (0.90)
  blocking collectives: 19.6 us -> 12.3 us
  Pallas kernels: 17 us -> 15.9 us
    ppermute x8 -> x6, waiting for transfers between devices: 21.5 us -> 2.73 us  [shift(): lax.ppermute(x, axis, [(i, (i + distance) % size) for i in range(size)])]
    all_to_all x1, waiting for transfers between devices: 0.01 us -> 18.4 us  [body(): got = lax.all_to_all(send, 'tile', 0, 0, tiled=True)]
    all_to_all x1, blocking collectives: 19.6 us -> 12.3 us  [body(): back = lax.all_to_all(sums, 'tile', 0, 0, tiled=True)]
    ppermute x0 -> x2, starting transfers between devices: none -> 3.33 us  [swapped(): return lax.ppermute(x, 'tile', pairs + [(b, a) for a, b in pairs])]
    ppermute x8 -> x6, starting transfers between devices: 18.1 us -> 15.4 us  [shift(): lax.ppermute(x, axis, [(i, (i + distance) % size) for i in range(size)])]
    pallas_call x2 -> x3, Pallas kernels: 2.53 us -> 2.56 us  [the longest x1 1.32 us: body(): call(home_kernel, arr((8, SUBS, LANES)), [spec()] * 2, name='home')]
  transfers between devices with their start and end apart: 9 -> 9, of which waited for: 4 -> 3; matrix products, arithmetic and copies ran while one was open for 0% -> 0% of each run, Pallas kernels for 2% -> 1%
where the time goes in v3:
time: 80.2 us; the launch traced here: 79.9 us
  starting transfers between devices  28.7 us (36%)
  waiting for transfers between devices  21.2 us (26%)
  Pallas kernels  15.9 us (20%)
  blocking collectives  12.3 us (15%)
  between operations  1.46 us (2%)
    all_to_all x1, waiting for transfers between devices, body(): got = lax.all_to_all(send, 'tile', 0, 0, tiled=True)  18.4 us
    ppermute x6, starting transfers between devices, shift(): lax.ppermute(x, axis, [(i, (i + distance) % size) for i in range(size)])  15.4 us
    all_to_all x1, blocking collectives, body(): back = lax.all_to_all(sums, 'tile', 0, 0, tiled=True)  12.3 us
    all_to_all x1, starting transfers between devices, body(): got = lax.all_to_all(send, 'tile', 0, 0, tiled=True)  9.99 us
    pallas_call x1, Pallas kernels, body(): call(send_kernel, [arr((TILES, 32, LANES)), arr((1, SND), jnp.int32), arr...  7.9 us
    pallas_call x1, Pallas kernels, body(): call(sample_kernel, arr((TILES, 3 * LANES)), [spec()] * 2, [pltpu.VMEM((8...  3.39 us
    ppermute x2, starting transfers between devices, swapped(): return lax.ppermute(x, 'tile', pairs + [(b, a) for a, b in pairs])  3.33 us
    ppermute x6, waiting for transfers between devices, shift(): lax.ppermute(x, axis, [(i, (i + distance) % size) for i in range(size)])  2.73 us
  transfers between devices with their start and end apart: 9, of which 3 were waited for; matrix products, arithmetic and copies ran while one was open for 0% of the time, Pallas kernels for 1%

profile of v3, /device:TPU:1, one launch (start us, length us, event | category | flops | bytes accessed | tf_op | source)
XLA Modules:
  0.0 79.9 jit_solution(17147246017848238686)
XLA Ops:
  0.6 1.2 %halo.1 = (f32[45,8,128]{2,1,0:T(8,128)S(1)}, f32[45,8,128]{2,1,0:T(8,128)S(1)}, f32[36,8,128]{2,1,0:T(8,128)S(1)}) custom-call(f32[36,8,128]{2,1,0:T(8,128)} %bitcast.32, f32[18,8,128]{2,1,0:T(8,128)} %bitcast.36, f32[18,8,128]{2,1,0:T(8,128)} %bitcast.38, f32[2,8,128]{2,1,0:T(8,128)} %bitcast.40), custom_call_target="tpu_custom_call" | custom-call | flops 1000000 | bytes 100000 | tf_op jit(solution)/shard_map/halo/pallas_call | solution.py:418
  1.9 3.3 %collective-permute-start = (f32[45,8,128]{2,1,0:T(8,128)S(1)}, f32[45,8,128]{2,1,0:T(8,128)S(1)}, u32[]{:S(2)}, u32[]{:S(2)}) collective-permute-start(f32[45,8,128]{2,1,0:T(8,128)S(1)} %get-tuple-element.15), channel_id=1, source_target_pairs={{0,4},{8,12},{16,20},{24,28},{32,36},{40,44},{48,52},{56,60},{64,6... | collective-permute-start | bytes 552968 | tf_op jit(solution)/shard_map/ppermute | solution.py:402
  5.2 0.0 collective-permute-start.1
  5.2 0.0 copy-start
  5.2 0.0 copy-start.1
  5.2 0.0 copy-start.2
  5.2 0.0 copy-start.3
  5.2 7.9 %send.1 = (f32[64,32,128]{2,1,0:T(8,128)}, s32[1,4096]{1,0:T(1,128)S(1)}, f32[4,8,128]{2,1,0:T(8,128)S(1)}) custom-call(f32[18,4096]{1,0:T(8,128)} %kern_in.1, s32[1,4096]{1,0:T(1,128)} %bitcast.42, s32[1,4096]{1,0:T(1,128)} %bitcast.43, s32[1,4096]{1,0:T(1,128)} %bitcast.44, f32[36,8,128]{2,1,0:T(8,128)S(1)} %get-tuple-element.13.part_ref), custom_call_target="tpu_custom_call" | custom-call | flops 8999999488 | bytes 100000 | tf_op jit(solution)/shard_map/send/pallas_call | solution.py:432
  13.1 0.0 collective-permute-done.near_ref
  13.1 0.0 collective-permute-done.1.far_ref
  13.2 0.0 copy-done
  13.2 0.0 copy-done.1
  13.2 0.0 copy-done.2
  13.2 0.0 copy-done.3
  13.2 0.0 copy-start.4
  13.2 0.3 advect.1.x_ref.refs_0_
  13.5 2.9 %collective-permute-start.4 = (f32[40,8,128]{2,1,0:T(8,128)S(1)}, f32[40,8,128]{2,1,0:T(8,128)S(1)}, u32[]{:S(2)}, u32[]{:S(2)}) collective-permute-start(f32[40,8,128]{2,1,0:T(8,128)S(1)} %advect.1.x_ref.refs_0_), channel_id=1, source_target_pairs={{0,1},{1,2},{2,3},{3,0},{4,5},{5,6},{6,7},{7,4},{8,9},{9,10},{10,1... | collective-permute-start | bytes 491528 | tf_op jit(solution)/shard_map/ppermute | solution.py:411
  16.4 4.2 %collective-permute-start.3 = (f32[40,8,128]{2,1,0:T(8,128)S(1)}, f32[40,8,128]{2,1,0:T(8,128)S(1)}, u32[]{:S(2)}, u32[]{:S(2)}) collective-permute-start(f32[40,8,128]{2,1,0:T(8,128)S(1)} %advect.1.x_ref.refs_0_), channel_id=1, source_target_pairs={{0,2},{1,3},{2,0},{3,1},{4,6},{5,7},{6,4},{7,5},{8,10},{9,11},{10,... | collective-permute-start | bytes 491528 | tf_op jit(solution)/shard_map/ppermute | solution.py:411
  20.6 2.4 %collective-permute-start.2 = (f32[40,8,128]{2,1,0:T(8,128)S(1)}, f32[40,8,128]{2,1,0:T(8,128)S(1)}, u32[]{:S(2)}, u32[]{:S(2)}) collective-permute-start(f32[40,8,128]{2,1,0:T(8,128)S(1)} %advect.1.x_ref.refs_0_), channel_id=1, source_target_pairs={{0,3},{1,0},{2,1},{3,2},{4,7},{5,4},{6,5},{7,6},{8,11},{9,8},{10,9... | collective-permute-start | bytes 491528 | tf_op jit(solution)/shard_map/ppermute | solution.py:411
  23.0 0.0 copy-done.4
  23.0 0.1 fusion
  23.1 0.1 reshape.51
  23.2 0.1 reshape.52.mix_ref
  23.3 10.0 %all-to-all-start = ((f32[64,32,128]{2,1,0:T(8,128)}), f32[64,32,128]{2,1,0:T(8,128)S(1)}, u32[]{:S(2)}, u32[]{:S(2)}) async-start(f32[64,32,128]{2,1,0:T(8,128)} %get-tuple-element.20), calls=%async_computation | async-start | bytes 2097152 | tf_op jit(solution)/shard_map/all_to_all | solution.py:459
  33.3 0.0 collective-permute-done.4.refs_3_
  33.3 0.0 collective-permute-done.3.refs_2_
  33.3 0.0 collective-permute-done.2.refs_1_
  33.3 1.2 %mix.1 = (f32[36,8,128]{2,1,0:T(8,128)}, f32[8,2,24,128]{3,2,1,0:T(8,128)S(1)}, f32[4,8,128]{2,1,0:T(8,128)S(1)}) custom-call(f32[24,96]{1,0:T(8,128)S(1)} %reshape.52.mix_ref, f32[8,128]{1,0:T(8,128)S(1)} %mark.1.mark_ref, f32[40,8,128]{2,1,0:T(8,128)S(1)} %advect.1.x_ref.refs_0_, f32[40,8,128]{2,1,0:T(8,128)S(1)} %collective-permute-done.2.refs_1_, ...), custom_call_target="tpu_custom_call" | custom-call | flops 99999997952 | bytes 100000 | tf_op jit(solution)/shard_map/mix/pallas_call | solution.py:471
  34.5 18.4 %all-to-all-done.got_ref = f32[64,32,128]{2,1,0:T(8,128)S(1)} async-done(((f32[64,32,128]{2,1,0:T(8,128)}), f32[64,32,128]{2,1,0:T(8,128)S(1)}, u32[]{:S(2)}, u32[]{:S(2)}) %all-to-all-start) | async-done | bytes 1048608 | tf_op jit(solution)/shard_map/all_to_all | solution.py:459
  52.9 3.4 %sample.1 = f32[64,384]{1,0:T(8,128)S(1)} custom-call(f32[64,32,128]{2,1,0:T(8,128)S(1)} %all-to-all-done.got_ref, f32[8,2,24,128]{3,2,1,0:T(8,128)S(1)} %get-tuple-element.21.field_ref), custom_call_target="tpu_custom_call" | custom-call | flops 1000000 | bytes 100000 | tf_op jit(solution)/shard_map/sample/pallas_call | solution.py:478
  56.3 0.1 copy.22
  56.4 12.3 %all_to_all.16 = f32[64,1,384]{2,1,0:T(1,128)S(1)} all-to-all(f32[64,1,384]{2,1,0:T(1,128)S(1)} %copy.22), channel_id=1, replica_groups=mesh['tile'=64,'lev'=4] {'tile'}, dimensions={0} | all-to-all | bytes 196608 | tf_op jit(solution)/shard_map/all_to_all | solution.py:486
  68.7 1.3 %home.1.a_ref = f32[8,8,128]{2,1,0:T(8,128)S(1)} custom-call(f32[64,384]{1,0:T(8,128)S(1)} %bitcast.34, s32[1,4096]{1,0:T(1,128)S(1)} %get-tuple-element.22.place_ref), custom_call_target="tpu_custom_call" | custom-call | flops 1000000 | bytes 100000 | tf_op jit(solution)/shard_map/home/pallas_call | solution.py:487
  70.0 0.3 collective-permute-start.7
  70.4 4.5 %collective-permute-start.6 = (f32[8,8,128]{2,1,0:T(8,128)S(1)}, f32[8,8,128]{2,1,0:T(8,128)S(1)}, u32[]{:S(2)}, u32[]{:S(2)}) collective-permute-start(f32[8,8,128]{2,1,0:T(8,128)S(1)} %home.1.a_ref), channel_id=1, source_target_pairs={{0,2},{1,3},{2,0},{3,1},{4,6},{5,7},{6,4},{7,5},{8,10},{9,11},{10,... | collective-permute-start | bytes 98312 | tf_op jit(solution)/shard_map/ppermute | solution.py:411
  74.9 1.0 %collective-permute-start.5 = (f32[8,8,128]{2,1,0:T(8,128)S(1)}, f32[8,8,128]{2,1,0:T(8,128)S(1)}, u32[]{:S(2)}, u32[]{:S(2)}) collective-permute-start(f32[8,8,128]{2,1,0:T(8,128)S(1)} %home.1.a_ref), channel_id=1, source_target_pairs={{0,3},{1,0},{2,1},{3,2},{4,7},{5,4},{6,5},{7,6},{8,11},{9,8},{10,9... | collective-permute-start | bytes 98312 | tf_op jit(solution)/shard_map/ppermute | solution.py:411
  76.6 0.0 collective-permute-done.7.d_ref
  76.6 0.9 %collective-permute-done.6.c_ref = f32[8,8,128]{2,1,0:T(8,128)S(1)} collective-permute-done((f32[8,8,128]{2,1,0:T(8,128)S(1)}, f32[8,8,128]{2,1,0:T(8,128)S(1)}, u32[]{:S(2)}, u32[]{:S(2)}) %collective-permute-start.6) | collective-permute-done | bytes 32800 | tf_op jit(solution)/shard_map/ppermute | solution.py:411
  77.5 1.8 %collective-permute-done.5.b_ref = f32[8,8,128]{2,1,0:T(8,128)S(1)} collective-permute-done((f32[8,8,128]{2,1,0:T(8,128)S(1)}, f32[8,8,128]{2,1,0:T(8,128)S(1)}, u32[]{:S(2)}, u32[]{:S(2)}) %collective-permute-start.5) | collective-permute-done | bytes 32800 | tf_op jit(solution)/shard_map/ppermute | solution.py:411
  79.3 0.6 last.1
  (3 shorter events, 0.0 us)
Async XLA Ops:
  1.9 11.3 %collective-permute-start = (f32[45,8,128]{2,1,0:T(8,128)S(1)}, f32[45,8,128]{2,1,0:T(8,128)S(1)}, u32[]{:S(2)}, u32[]{:S(2)}) collective-permute-start(f32[45,8,128]{2,1,0:T(8,128)S(1)} %get-tuple-element.15), channel_id=1, source_target_pairs={{0,4},{8,12},{16,20},{24,28},{32,36},{40,44},{48,52},{56,60},{64,6... | collective-permute-start | bytes 552968 | tf_op jit(solution)/shard_map/ppermute | solution.py:402
  5.2 7.9 %collective-permute-start.1 = (f32[45,8,128]{2,1,0:T(8,128)S(1)}, f32[45,8,128]{2,1,0:T(8,128)S(1)}, u32[]{:S(2)}, u32[]{:S(2)}) collective-permute-start(f32[45,8,128]{2,1,0:T(8,128)S(1)} %get-tuple-element.16), channel_id=1, source_target_pairs={{4,8},{12,16},{20,24},{28,32},{36,40},{44,48},{52,56},{60,64},{68,... | collective-permute-start | bytes 552968 | tf_op jit(solution)/shard_map/ppermute | solution.py:402
  5.2 8.0 %copy-start = (f32[2,18,2,512]{3,2,1,0:T(2,128)S(1)}, f32[2,18,2,512]{3,2,1,0:T(2,128)}, u32[]{:S(2)}) copy-start(f32[2,18,2,512]{3,2,1,0:T(2,128)} %param.10) | copy-start | bytes 442372
  5.2 8.0 %copy-start.1 = (f32[18,2,512]{2,1,0:T(2,128)S(1)}, f32[18,2,512]{2,1,0:T(2,128)}, u32[]{:S(2)}) copy-start(f32[18,2,512]{2,1,0:T(2,128)} %param.11) | copy-start | bytes 221188
  5.2 8.0 %copy-start.2 = (f32[18,2,512]{2,1,0:T(2,128)S(1)}, f32[18,2,512]{2,1,0:T(2,128)}, u32[]{:S(2)}) copy-start(f32[18,2,512]{2,1,0:T(2,128)} %param.12) | copy-start | bytes 221188
  5.2 8.0 %copy-start.3 = (f32[2,2,512]{2,1,0:T(2,128)S(1)}, f32[2,2,512]{2,1,0:T(2,128)}, u32[]{:S(2)}) copy-start(f32[2,2,512]{2,1,0:T(2,128)} %param.13) | copy-start | bytes 24580
  13.2 9.8 %copy-start.4 = (f32[72,72]{1,0:T(8,128)S(1)}, f32[72,72]{1,0:T(8,128)}, u32[]{:S(2)}) copy-start(f32[72,72]{1,0:T(8,128)} %param.14) | copy-start | bytes 62212
  13.5 19.8 %collective-permute-start.4 = (f32[40,8,128]{2,1,0:T(8,128)S(1)}, f32[40,8,128]{2,1,0:T(8,128)S(1)}, u32[]{:S(2)}, u32[]{:S(2)}) collective-permute-start(f32[40,8,128]{2,1,0:T(8,128)S(1)} %advect.1.x_ref.refs_0_), channel_id=1, source_target_pairs={{0,1},{1,2},{2,3},{3,0},{4,5},{5,6},{6,7},{7,4},{8,9},{9,10},{10,1... | collective-permute-start | bytes 491528 | tf_op jit(solution)/shard_map/ppermute | solution.py:411
  16.4 16.9 %collective-permute-start.3 = (f32[40,8,128]{2,1,0:T(8,128)S(1)}, f32[40,8,128]{2,1,0:T(8,128)S(1)}, u32[]{:S(2)}, u32[]{:S(2)}) collective-permute-start(f32[40,8,128]{2,1,0:T(8,128)S(1)} %advect.1.x_ref.refs_0_), channel_id=1, source_target_pairs={{0,2},{1,3},{2,0},{3,1},{4,6},{5,7},{6,4},{7,5},{8,10},{9,11},{10,... | collective-permute-start | bytes 491528 | tf_op jit(solution)/shard_map/ppermute | solution.py:411
  20.6 12.7 %collective-permute-start.2 = (f32[40,8,128]{2,1,0:T(8,128)S(1)}, f32[40,8,128]{2,1,0:T(8,128)S(1)}, u32[]{:S(2)}, u32[]{:S(2)}) collective-permute-start(f32[40,8,128]{2,1,0:T(8,128)S(1)} %advect.1.x_ref.refs_0_), channel_id=1, source_target_pairs={{0,3},{1,0},{2,1},{3,2},{4,7},{5,4},{6,5},{7,6},{8,11},{9,8},{10,9... | collective-permute-start | bytes 491528 | tf_op jit(solution)/shard_map/ppermute | solution.py:411
  23.3 29.6 %all-to-all-start = ((f32[64,32,128]{2,1,0:T(8,128)}), f32[64,32,128]{2,1,0:T(8,128)S(1)}, u32[]{:S(2)}, u32[]{:S(2)}) async-start(f32[64,32,128]{2,1,0:T(8,128)} %get-tuple-element.20), calls=%async_computation | async-start | bytes 2097152 | tf_op jit(solution)/shard_map/all_to_all | solution.py:459
  70.0 6.5 %collective-permute-start.7 = (f32[8,8,128]{2,1,0:T(8,128)S(1)}, f32[8,8,128]{2,1,0:T(8,128)S(1)}, u32[]{:S(2)}, u32[]{:S(2)}) collective-permute-start(f32[8,8,128]{2,1,0:T(8,128)S(1)} %home.1.a_ref), channel_id=1, source_target_pairs={{0,1},{1,2},{2,3},{3,0},{4,5},{5,6},{6,7},{7,4},{8,9},{9,10},{10,1... | collective-permute-start | bytes 98312 | tf_op jit(solution)/shard_map/ppermute | solution.py:411
  70.4 7.1 %collective-permute-start.6 = (f32[8,8,128]{2,1,0:T(8,128)S(1)}, f32[8,8,128]{2,1,0:T(8,128)S(1)}, u32[]{:S(2)}, u32[]{:S(2)}) collective-permute-start(f32[8,8,128]{2,1,0:T(8,128)S(1)} %home.1.a_ref), channel_id=1, source_target_pairs={{0,2},{1,3},{2,0},{3,1},{4,6},{5,7},{6,4},{7,5},{8,10},{9,11},{10,... | collective-permute-start | bytes 98312 | tf_op jit(solution)/shard_map/ppermute | solution.py:411
  74.9 4.4 %collective-permute-start.5 = (f32[8,8,128]{2,1,0:T(8,128)S(1)}, f32[8,8,128]{2,1,0:T(8,128)S(1)}, u32[]{:S(2)}, u32[]{:S(2)}) collective-permute-start(f32[8,8,128]{2,1,0:T(8,128)S(1)} %home.1.a_ref), channel_id=1, source_target_pairs={{0,3},{1,0},{2,1},{3,2},{4,7},{5,4},{6,5},{7,6},{8,11},{9,8},{10,9... | collective-permute-start | bytes 98312 | tf_op jit(solution)/shard_map/ppermute | solution.py:411

commit v4 on v3

--- a/solution.py
+++ b/solution.py
@@ -12,10 +12,6 @@
 TILES = 64
 WIDE = 256
 QUADS = 8
-ORDER = "H"
-MARK = 1000000
-MIX = 100000000000
-RELAY = False
 SND = 4096
 F32 = jnp.float32
 BF16 = jnp.bfloat16
@@ -139,7 +135,20 @@
             return refs[3][row - size // 2]
         return refs[d if d < 3 else -1][row]
 
-    high, low = split(mix_ref[...])
+    z = lax.axis_index("lev")
+    level = iota((ROWS, 4 * HERE), 0)
+    pick = ((iota((ROWS, 4 * HERE), 1) == z * HERE + level) & (level < HERE)).astype(F32).astype(BF16)
+    at = iota((4 * HERE, 4 * ROWS), 1)
+    turn = (at >= ROWS).astype(jnp.int32) + (at >= 2 * ROWS).astype(jnp.int32) + (at >= 3 * ROWS).astype(jnp.int32)
+    level = at - turn * ROWS
+    source = ((z + turn) & 3) * HERE + level
+    spread = ((iota((4 * HERE, 4 * ROWS), 0) == source) & (level < HERE)).astype(F32).astype(BF16)
+
+    def chosen(part):
+        rows = jnp.dot(pick, part, preferred_element_type=F32).astype(BF16)
+        return jnp.dot(rows, spread, preferred_element_type=F32).astype(BF16)
+
+    high, low = (chosen(part) for part in split(mix_ref[...]))
     both = jnp.concatenate([high.astype(F32), low.astype(F32)], axis=0).astype(BF16)
     pad = jnp.zeros((ROWS - HERE, 2 * LANES), F32)
     for s in range(2):
@@ -167,23 +176,24 @@
     return group, lane
 
 
-def fetch(pairs, sem, needed=None):
+def fetch(pairs, sem):
     copies = [pltpu.make_async_copy(a, b, sem.at[i]) for i, (a, b) in enumerate(pairs)]
     for copy in copies:
         copy.start()
-    for copy in copies[:needed]:
+    for copy in copies:
         copy.wait()
-    return copies[needed:] if needed else []
-
-
+
+
+MESSAGE = 29
 BOTH = 40
 
 
 def send_kernel(
-    kern_in, col_in, own_in, off_in, part_ref, send_ref, place_ref, den_ref,
-    kern_ref, col_ref, own_ref, off_ref, w_ref, grp_ref, hot_ref, sem,
+    kern_in, col_ref, own_ref, off_ref, part_ref, send_ref, place_ref, den_ref,
+    kern_ref, w_ref, grp_ref, hot_ref, sem,
 ):
-    rest = fetch(((own_in, own_ref), (off_in, off_ref), (col_in, col_ref), (kern_in, kern_ref)), sem, 1)
+    weights = pltpu.make_async_copy(kern_in, kern_ref, sem)
+    weights.start()
     before = (iota((WIDE, WIDE), 0) < iota((WIDE, WIDE), 1)).astype(BF16)
     slot = iota((WIDE, 1), 0)
     carry = jnp.zeros((TILES, 1), F32)
@@ -199,8 +209,7 @@
         grp_ref[:, at] = jnp.broadcast_to(group, (SUBS, WIDE))
         hot_ref[at, :] = (slot == lane).astype(F32).T.astype(BF16)
 
-    for copy in rest:
-        copy.wait()
+    weights.wait()
     z = lax.axis_index("lev")
     levels = z * HERE + iota((HERE, SND), 0)
     weighted = jnp.where(levels >= off_ref[...], kern_ref[...], 0.0)
@@ -222,7 +231,7 @@
     quads, chunk = 16, 512
     sub, left = iota((SUBS, LANES), 0), iota((SUBS, LANES), 1) < 64
 
-    def some(i, _):
+    def some(i):
         acc = jnp.zeros((quads * 3 * BOTH, WIDE), F32)
         for b in range(SND // chunk):
             at = pl.ds(b * chunk, chunk)
@@ -252,12 +261,15 @@
                 else:
                     bottom = jnp.where(left, roll(rest[0:8], 64, 1), rest[8:16])
                     middle = roll(middle, 64, 1)
-                send_ref[t, 0:16, :] = top
-                send_ref[t, 16:24, :] = jnp.where(sub < 3, third, jnp.where(sub < 6, middle, 0.0))
-                send_ref[t, 24:32, :] = bottom
-        return 0
-
-    lax.fori_loop(0, TILES // (4 * quads), some, 0)
+                send_ref[MESSAGE * t : MESSAGE * t + 16, :] = top
+                send_ref[MESSAGE * t + 16 : MESSAGE * t + 24, :] = bottom
+                after = roll(middle, -1, 0)
+                split_row = jnp.where(left, middle, roll(after, 64, 1))
+                tail = jnp.where(sub < 3, third, jnp.where(sub == 3, split_row, after))
+                send_ref[MESSAGE * t + 24 : MESSAGE * t + 29, :] = tail[0:5]
+
+    for i in range(TILES // (4 * quads)):
+        some(i)
 
 
 FIELD = 40
@@ -303,14 +315,24 @@
     def wide(a, b):
         return jnp.concatenate([a, b], axis=1)
 
+    def last_of(x, y):
+        a = jnp.where(left, x, roll(y, 64, 1))
+        b = jnp.where(left, roll(x, 64, 1), y)
+        return jnp.where(sub == 0, roll(a, -3, 0), jnp.where(sub == 1, roll(b, -2, 0), roll(a, -2, 0)))
+
     quads = QUADS
     half = lane[0:1] < 64
 
     def some(i, _):
-        rows = ([], [], [])
+        rows = []
+        step = 4 * quads * MESSAGE
+        got = got_ref.at[pl.ds(pl.multiple_of(i * step, SUBS), step)]
         for q in range(quads):
-            t = (i * quads + q) * 4
-            xs = [[got_ref[t + k, 8 * g : 8 * g + 8, :] for g in range(4)] for k in range(4)]
+            xs = []
+            for k in range(4):
+                base = (q * 4 + k) * MESSAGE
+                tail = jnp.concatenate([got[base + 24 : base + 29, :], jnp.zeros((3, LANES), F32)], axis=0)
+                xs.append([got[base : base + 8, :], got[base + 8 : base + 16, :], tail, got[base + 16 : base + 24, :]])
             results, rest = [], []
             for x, y in (xs[0:2], xs[2:4]):
                 w = [wide(x[g], y[g]) for g in range(3)]
@@ -319,7 +341,7 @@
                     (
                         jnp.where(left, x[3], roll(y[3], 64, 1)),
                         jnp.where(left, roll(x[3], 64, 1), y[3]),
-                        roll(jnp.where(left, x[2], roll(y[2], 64, 1)), -3, 0),
+                        last_of(x[2], y[2]),
                     )
                 )
             w = [wide(rest[0][g], rest[1][g]) for g in range(3)]
@@ -329,20 +351,18 @@
                 pair = slice((k // 2) * LANES, (k // 2 + 1) * LANES)
                 a, b = tails[0][:, pair], tails[1][:, pair]
                 tail = jnp.where(half, a, roll(b, 64, 1)) if k % 2 == 0 else jnp.where(half, roll(a, 64, 1), b)
-                for j, x in enumerate((results[k // 2][0][:, mine], results[k // 2][1][:, mine], tail)):
-                    rows[j].append(x)
-        at = pl.ds(pl.multiple_of(i * 4 * quads, 4 * quads), 4 * quads)
-        for j in range(3):
-            out_ref[at, j * LANES : (j + 1) * LANES] = jnp.concatenate(rows[j], axis=0)
+                rows += [results[k // 2][0][:, mine], results[k // 2][1][:, mine], tail]
+        size = 12 * quads
+        out_ref[pl.ds(pl.multiple_of(i * size, SUBS), size), :] = jnp.concatenate(rows, axis=0)
         return 0
 
     lax.fori_loop(0, TILES // (4 * quads), some, 0)
 
 
 def home_kernel(back_ref, place_ref, out_ref):
-    tail = back_ref[:, 2 * LANES : 3 * LANES]
-    first = jnp.concatenate([back_ref[:, 0:LANES], tail], axis=1)
-    second = jnp.concatenate([back_ref[:, LANES : 2 * LANES], roll(tail, 64, 1)], axis=1)
+    plain, other, tail = (back_ref[pl.ds(j, TILES, stride=3), :] for j in range(3))
+    first = jnp.concatenate([plain, tail], axis=1)
+    second = jnp.concatenate([other, roll(tail, 64, 1)], axis=1)
     high, low = split(jnp.concatenate([first, second], axis=0))
     slot = iota((WIDE, 1), 0)
     for b in range(SND // WIDE):
@@ -431,59 +451,39 @@
     from_near, from_far = swapped(near_half, 0), swapped(far_half, 1)
     send, place_of, den = call(
         send_kernel,
-        [arr((TILES, 32, LANES)), arr((1, SND), jnp.int32), arr((4, SUBS, LANES))],
-        [spec(HBM)] * 4 + [spec()],
-        [pltpu.VMEM((HERE, SND), F32)]
-        + [pltpu.VMEM((1, SND), jnp.int32)] * 3
-        + [pltpu.VMEM((BOTH, SND), F32), pltpu.VMEM((SUBS, SND), jnp.int32), pltpu.VMEM((SND, WIDE), BF16), pltpu.SemaphoreType.DMA((4,))],
+        [arr((TILES * MESSAGE, LANES)), arr((1, SND), jnp.int32), arr((4, SUBS, LANES))],
+        [spec(HBM)] + [spec()] * 4,
+        [pltpu.VMEM((HERE, SND), F32), pltpu.VMEM((BOTH, SND), F32), pltpu.VMEM((SUBS, SND), jnp.int32), pltpu.VMEM((SND, WIDE), BF16), pltpu.SemaphoreType.DMA],
         mib=28,
         flops=9 * 10**9,
         name="send",
-    )(*(far(x) for x in (kernel, col, own, off)), part)
-    if ORDER == "A":
-        send, from_west, from_east = lax.optimization_barrier((send, from_west, from_east))
-        got = lax.all_to_all(send, "tile", 0, 0, tiled=True)
+    )(far(kernel), col, own, off, part)
     adv = call(advect_kernel, arr((40, SUBS, LANES)), [spec()] * 8, name="advect")(
         c, u, v, f, part, from_near, from_far, den
     )
     up, down = shift(adv, "lev", -1), shift(adv, "lev", 1)
-    if ORDER == "B":
-        send, adv = lax.optimization_barrier((send, adv))
-        got = lax.all_to_all(send, "tile", 0, 0, tiled=True)
-    if ORDER == "C":
-        send, up = lax.optimization_barrier((send, up))
-        got = lax.all_to_all(send, "tile", 0, 0, tiled=True)
-    if ORDER == "H":
-        mark = call(mark_kernel, arr((SUBS, LANES)), [spec()], flops=MARK, name="mark")(adv)
-        send, mark = lax.optimization_barrier((send, mark))
-        got = lax.all_to_all(send, "tile", 0, 0, tiled=True)
-    if RELAY:
-        across = [shift(up[:20], "lev", -1), shift(down[20:], "lev", 1)]
-    else:
-        across = [shift(adv, "lev", 2)]
-    if ORDER == "D":
-        send, *across = lax.optimization_barrier((send, *across))
-        got = lax.all_to_all(send, "tile", 0, 0, tiled=True)
-    first = lax.axis_index("lev") * HERE
-    twice = jnp.concatenate([mixing, mixing], axis=1)
-    rows = lax.dynamic_slice(twice, (first, first), (HERE, 4 * HERE)).reshape(HERE, 4, HERE)
-    rows = jnp.pad(rows, ((0, ROWS - HERE), (0, 0), (0, ROWS - HERE))).reshape(ROWS, 4 * ROWS)
+    across = [shift(adv, "lev", 2)]
+    mark = call(mark_kernel, arr((SUBS, LANES)), [spec()], name="mark")(adv)
+    send, mark = lax.optimization_barrier((send, mark))
+    got = lax.all_to_all(send.reshape(TILES, 1, MESSAGE * LANES), "tile", 0, 0, tiled=True)
+    got = got.reshape(TILES * MESSAGE, LANES)
     transported, field, weight = call(
         mix_kernel,
         [block, arr((SUBS, 2, ROWS, LANES)), arr((4, SUBS, LANES))],
         [spec()] * (5 + len(across)),
-        flops=MIX,
+        flops=10**11,
         name="mix",
-    )(rows, mark, adv, up, *across, down)
+    )(mixing, mark, adv, up, *across, down)
     sums = call(
         sample_kernel,
-        arr((TILES, 3 * LANES)),
+        arr((3 * TILES, LANES)),
         [spec()] * 2,
         [pltpu.VMEM((8 * FIELD, WIDE), BF16)],
         mib=24,
         name="sample",
     )(got, field)
-    back = lax.all_to_all(sums, "tile", 0, 0, tiled=True)
+    back = lax.all_to_all(sums.reshape(TILES, 1, 3 * LANES), "tile", 0, 0, tiled=True)
+    back = back.reshape(3 * TILES, LANES)
     mine = call(home_kernel, arr((8, SUBS, LANES)), [spec()] * 2, name="home")(back, place_of)
     nums = [shift(mine, "lev", -d) for d in (1, 2, 3)]
     evolved = call(last_kernel, arr((2, SND)), [spec(SMEM)] + [spec()] * 5, name="last")(counts, mine, *nums, weight)

time: 80.2 us -> 79.1 us (0.986)
  waiting for transfers between devices: 21.2 us -> 20.3 us
    all_to_all x1, waiting for transfers between devices: 18.4 us -> 17.4 us  [body(): lax.all_to_all(send.reshape(TILES, 1, MESSAGE * LANES), 'tile', 0, 0, til...]
  transfers between devices with their start and end apart: 9 -> 9, of which waited for: 3 -> 3; matrix products, arithmetic and copies ran while one was open for 0% -> 0% of each run, Pallas kernels for 1% -> 2%
where the time goes in v4:
time: 79.1 us; the launch traced here: 78.8 us
  starting transfers between devices  28.7 us (36%)
  waiting for transfers between devices  20.3 us (26%)
  Pallas kernels  16 us (20%)
  blocking collectives  12.3 us (16%)
  between operations  1.48 us (2%)
    all_to_all x1, waiting for transfers between devices, body(): lax.all_to_all(send.reshape(TILES, 1, MESSAGE * LANES), 'tile', 0, 0, til...  17.4 us
    ppermute x6, starting transfers between devices, shift(): lax.ppermute(x, axis, [(i, (i + distance) % size) for i in range(size)])  15.3 us
    all_to_all x1, blocking collectives, body(): lax.all_to_all(sums.reshape(TILES, 1, 3 * LANES), 'tile', 0, 0, tiled=True)  12.3 us
    all_to_all x1, starting transfers between devices, body(): lax.all_to_all(send.reshape(TILES, 1, MESSAGE * LANES), 'tile', 0, 0, til...  10.1 us
    pallas_call x1, Pallas kernels, body(): call(send_kernel, [arr((TILES * MESSAGE, LANES)), arr((1, SND), jnp.int32...  7.76 us
    pallas_call x1, Pallas kernels, body(): call(sample_kernel, arr((3 * TILES, LANES)), [spec()] * 2, [pltpu.VMEM((8...  3.46 us
    ppermute x2, starting transfers between devices, swapped(): return lax.ppermute(x, 'tile', pairs + [(b, a) for a, b in pairs])  3.33 us
    ppermute x6, waiting for transfers between devices, shift(): lax.ppermute(x, axis, [(i, (i + distance) % size) for i in range(size)])  2.84 us
  transfers between devices with their start and end apart: 9, of which 3 were waited for; matrix products, arithmetic and copies ran while one was open for 0% of the time, Pallas kernels for 2%

profile of v4, /device:TPU:1, one launch (start us, length us, event | category | flops | bytes accessed | tf_op | source)
XLA Modules:
  0.0 78.8 jit_solution(7796252631286597611)
XLA Ops:
  0.6 0.0 copy-start.5
  0.6 0.0 copy-start.6
  0.7 0.0 copy-start.7
  0.7 1.2 %halo.1 = (f32[45,8,128]{2,1,0:T(8,128)S(1)}, f32[45,8,128]{2,1,0:T(8,128)S(1)}, f32[36,8,128]{2,1,0:T(8,128)S(1)}) custom-call(f32[36,8,128]{2,1,0:T(8,128)} %bitcast.33, f32[18,8,128]{2,1,0:T(8,128)} %bitcast.37, f32[18,8,128]{2,1,0:T(8,128)} %bitcast.39, f32[2,8,128]{2,1,0:T(8,128)} %bitcast.41), custom_call_target="tpu_custom_call" | custom-call | flops 1000000 | bytes 100000 | tf_op jit(solution)/shard_map/halo/pallas_call | solution.py:438
  1.9 3.3 %collective-permute-start = (f32[45,8,128]{2,1,0:T(8,128)S(1)}, f32[45,8,128]{2,1,0:T(8,128)S(1)}, u32[]{:S(2)}, u32[]{:S(2)}) collective-permute-start(f32[45,8,128]{2,1,0:T(8,128)S(1)} %get-tuple-element.15), channel_id=1, source_target_pairs={{0,4},{8,12},{16,20},{24,28},{32,36},{40,44},{48,52},{56,60},{64,6... | collective-permute-start | bytes 552968 | tf_op jit(solution)/shard_map/ppermute | solution.py:422
  5.2 0.0 collective-permute-start.1
  5.2 0.0 copy-done.5
  5.2 0.0 copy-done.6
  5.3 0.0 copy-done.7
  5.3 0.0 copy-start
  5.3 0.0 copy-start.1
  5.3 0.0 copy-start.2
  5.3 0.0 copy-start.3
  5.3 7.8 %send.1 = (f32[1856,128]{1,0:T(8,128)}, s32[1,4096]{1,0:T(1,128)S(1)}, f32[4,8,128]{2,1,0:T(8,128)S(1)}) custom-call(f32[18,4096]{1,0:T(8,128)} %kern_in.1, s32[1,4096]{1,0:T(1,128)S(1)} %bitcast.43, s32[1,4096]{1,0:T(1,128)S(1)} %bitcast.44, s32[1,4096]{1,0:T(1,128)S(1)} %bitcast.45, f32[36,8,128]{2,1,0:T(8,128)S(1)} %get-tuple-element.13.part_ref), custom_call_target="tpu_custom_call" | custom-call | flops 8999999488 | bytes 100000 | tf_op jit(solution)/shard_map/send/pallas_call | solution.py:452
  13.1 0.0 collective-permute-done.near_ref
  13.1 0.0 collective-permute-done.1.far_ref
  13.1 0.0 copy-done
  13.1 0.0 copy-done.1
  13.1 0.0 copy-done.2
  13.1 0.0 copy-done.3
  13.1 0.3 advect.1.x_ref.refs_0_
  13.4 3.0 %collective-permute-start.4 = (f32[40,8,128]{2,1,0:T(8,128)S(1)}, f32[40,8,128]{2,1,0:T(8,128)S(1)}, u32[]{:S(2)}, u32[]{:S(2)}) collective-permute-start(f32[40,8,128]{2,1,0:T(8,128)S(1)} %advect.1.x_ref.refs_0_), channel_id=1, source_target_pairs={{0,1},{1,2},{2,3},{3,0},{4,5},{5,6},{6,7},{7,4},{8,9},{9,10},{10,1... | collective-permute-start | bytes 491528 | tf_op jit(solution)/shard_map/ppermute | solution.py:431
  16.4 4.2 %collective-permute-start.3 = (f32[40,8,128]{2,1,0:T(8,128)S(1)}, f32[40,8,128]{2,1,0:T(8,128)S(1)}, u32[]{:S(2)}, u32[]{:S(2)}) collective-permute-start(f32[40,8,128]{2,1,0:T(8,128)S(1)} %advect.1.x_ref.refs_0_), channel_id=1, source_target_pairs={{0,2},{1,3},{2,0},{3,1},{4,6},{5,7},{6,4},{7,5},{8,10},{9,11},{10,... | collective-permute-start | bytes 491528 | tf_op jit(solution)/shard_map/ppermute | solution.py:431
  20.6 2.4 %collective-permute-start.2 = (f32[40,8,128]{2,1,0:T(8,128)S(1)}, f32[40,8,128]{2,1,0:T(8,128)S(1)}, u32[]{:S(2)}, u32[]{:S(2)}) collective-permute-start(f32[40,8,128]{2,1,0:T(8,128)S(1)} %advect.1.x_ref.refs_0_), channel_id=1, source_target_pairs={{0,3},{1,0},{2,1},{3,2},{4,7},{5,4},{6,5},{7,6},{8,11},{9,8},{10,9... | collective-permute-start | bytes 491528 | tf_op jit(solution)/shard_map/ppermute | solution.py:431
  23.0 0.0 copy-start.4
  23.0 10.1 %all-to-all-start = ((f32[64,1,3712]{2,1,0:T(1,128)}), f32[64,1,3712]{2,1,0:T(1,128)S(1)}, u32[]{:S(2)}, u32[]{:S(2)}) async-start(f32[64,1,3712]{2,1,0:T(1,128)} %bitcast.26), calls=%async_computation | async-start | bytes 1900544 | tf_op jit(solution)/shard_map/all_to_all | solution.py:468
  33.1 0.0 collective-permute-done.4.refs_3_
  33.1 0.0 collective-permute-done.3.refs_2_
  33.1 0.0 collective-permute-done.2.refs_1_
  33.1 0.0 copy-done.4
  33.1 1.3 %mix.1 = (f32[36,8,128]{2,1,0:T(8,128)}, f32[8,2,24,128]{3,2,1,0:T(8,128)S(1)}, f32[4,8,128]{2,1,0:T(8,128)S(1)}) custom-call(f32[72,72]{1,0:T(8,128)S(1)} %copy-done.4, f32[8,128]{1,0:T(8,128)S(1)} %mark.1.mark_ref, f32[40,8,128]{2,1,0:T(8,128)S(1)} %advect.1.x_ref.refs_0_, f32[40,8,128]{2,1,0:T(8,128)S(1)} %collective-permute-done.2.refs_1_, ...), custom_call_target="tpu_custom_call" | custom-call | flops 99999997952 | bytes 100000 | tf_op jit(solution)/shard_map/mix/pallas_call | solution.py:470
  34.4 17.4 %all-to-all-done = f32[64,1,3712]{2,1,0:T(1,128)S(1)} async-done(((f32[64,1,3712]{2,1,0:T(1,128)}), f32[64,1,3712]{2,1,0:T(1,128)S(1)}, u32[]{:S(2)}, u32[]{:S(2)}) %all-to-all-start) | async-done | bytes 950304 | tf_op jit(solution)/shard_map/all_to_all | solution.py:468
  51.8 3.5 %sample.1 = f32[192,128]{1,0:T(8,128)S(1)} custom-call(f32[1856,128]{1,0:T(8,128)S(1)} %bitcast.32, f32[8,2,24,128]{3,2,1,0:T(8,128)S(1)} %get-tuple-element.21.field_ref), custom_call_target="tpu_custom_call" | custom-call | flops 1000000 | bytes 100000 | tf_op jit(solution)/shard_map/sample/pallas_call | solution.py:477
  55.3 12.3 %all_to_all.10 = f32[64,1,384]{2,1,0:T(1,128)S(1)} all-to-all(f32[64,1,384]{2,1,0:T(1,128)S(1)} %bitcast.36), channel_id=1, replica_groups=mesh['tile'=64,'lev'=4] {'tile'}, dimensions={0} | all-to-all | bytes 196608 | tf_op jit(solution)/shard_map/all_to_all | solution.py:485
  67.6 1.3 %home.1.a_ref = f32[8,8,128]{2,1,0:T(8,128)S(1)} custom-call(f32[192,128]{1,0:T(8,128)S(1)} %bitcast.35, s32[1,4096]{1,0:T(1,128)S(1)} %get-tuple-element.22.place_ref), custom_call_target="tpu_custom_call" | custom-call | flops 1000000 | bytes 100000 | tf_op jit(solution)/shard_map/home/pallas_call | solution.py:487
  68.9 0.3 collective-permute-start.7
  69.3 4.5 %collective-permute-start.6 = (f32[8,8,128]{2,1,0:T(8,128)S(1)}, f32[8,8,128]{2,1,0:T(8,128)S(1)}, u32[]{:S(2)}, u32[]{:S(2)}) collective-permute-start(f32[8,8,128]{2,1,0:T(8,128)S(1)} %home.1.a_ref), channel_id=1, source_target_pairs={{0,2},{1,3},{2,0},{3,1},{4,6},{5,7},{6,4},{7,5},{8,10},{9,11},{10,... | collective-permute-start | bytes 98312 | tf_op jit(solution)/shard_map/ppermute | solution.py:431
  73.7 1.0 %collective-permute-start.5 = (f32[8,8,128]{2,1,0:T(8,128)S(1)}, f32[8,8,128]{2,1,0:T(8,128)S(1)}, u32[]{:S(2)}, u32[]{:S(2)}) collective-permute-start(f32[8,8,128]{2,1,0:T(8,128)S(1)} %home.1.a_ref), channel_id=1, source_target_pairs={{0,3},{1,0},{2,1},{3,2},{4,7},{5,4},{6,5},{7,6},{8,11},{9,8},{10,9... | collective-permute-start | bytes 98312 | tf_op jit(solution)/shard_map/ppermute | solution.py:431
  75.3 0.0 collective-permute-done.7.d_ref
  75.4 1.1 %collective-permute-done.6.c_ref = f32[8,8,128]{2,1,0:T(8,128)S(1)} collective-permute-done((f32[8,8,128]{2,1,0:T(8,128)S(1)}, f32[8,8,128]{2,1,0:T(8,128)S(1)}, u32[]{:S(2)}, u32[]{:S(2)}) %collective-permute-start.6) | collective-permute-done | bytes 32800 | tf_op jit(solution)/shard_map/ppermute | solution.py:431
  76.5 1.7 %collective-permute-done.5.b_ref = f32[8,8,128]{2,1,0:T(8,128)S(1)} collective-permute-done((f32[8,8,128]{2,1,0:T(8,128)S(1)}, f32[8,8,128]{2,1,0:T(8,128)S(1)}, u32[]{:S(2)}, u32[]{:S(2)}) %collective-permute-start.5) | collective-permute-done | bytes 32800 | tf_op jit(solution)/shard_map/ppermute | solution.py:431
  78.2 0.6 last.1
  (1 shorter events, 0.0 us)
Async XLA Ops:
  0.6 4.6 %copy-start.5 = (s32[4096]{0:T(1024)S(1)}, s32[4096]{0:T(1024)}, u32[]{:S(2)}) copy-start(s32[4096]{0:T(1024)} %param.16) | copy-start | bytes 49156
  0.6 4.6 %copy-start.6 = (s32[4096]{0:T(1024)S(1)}, s32[4096]{0:T(1024)}, u32[]{:S(2)}) copy-start(s32[4096]{0:T(1024)} %param.17) | copy-start | bytes 49156
  0.7 4.6 %copy-start.7 = (s32[4096]{0:T(1024)S(1)}, s32[4096]{0:T(1024)}, u32[]{:S(2)}) copy-start(s32[4096]{0:T(1024)} %param.18) | copy-start | bytes 49156
  1.9 11.2 %collective-permute-start = (f32[45,8,128]{2,1,0:T(8,128)S(1)}, f32[45,8,128]{2,1,0:T(8,128)S(1)}, u32[]{:S(2)}, u32[]{:S(2)}) collective-permute-start(f32[45,8,128]{2,1,0:T(8,128)S(1)} %get-tuple-element.15), channel_id=1, source_target_pairs={{0,4},{8,12},{16,20},{24,28},{32,36},{40,44},{48,52},{56,60},{64,6... | collective-permute-start | bytes 552968 | tf_op jit(solution)/shard_map/ppermute | solution.py:422
  5.2 7.8 %collective-permute-start.1 = (f32[45,8,128]{2,1,0:T(8,128)S(1)}, f32[45,8,128]{2,1,0:T(8,128)S(1)}, u32[]{:S(2)}, u32[]{:S(2)}) collective-permute-start(f32[45,8,128]{2,1,0:T(8,128)S(1)} %get-tuple-element.16), channel_id=1, source_target_pairs={{4,8},{12,16},{20,24},{28,32},{36,40},{44,48},{52,56},{60,64},{68,... | collective-permute-start | bytes 552968 | tf_op jit(solution)/shard_map/ppermute | solution.py:422
  5.3 7.8 %copy-start = (f32[2,18,2,512]{3,2,1,0:T(2,128)S(1)}, f32[2,18,2,512]{3,2,1,0:T(2,128)}, u32[]{:S(2)}) copy-start(f32[2,18,2,512]{3,2,1,0:T(2,128)} %param.10) | copy-start | bytes 442372
  5.3 7.8 %copy-start.1 = (f32[18,2,512]{2,1,0:T(2,128)S(1)}, f32[18,2,512]{2,1,0:T(2,128)}, u32[]{:S(2)}) copy-start(f32[18,2,512]{2,1,0:T(2,128)} %param.11) | copy-start | bytes 221188
  5.3 7.8 %copy-start.2 = (f32[18,2,512]{2,1,0:T(2,128)S(1)}, f32[18,2,512]{2,1,0:T(2,128)}, u32[]{:S(2)}) copy-start(f32[18,2,512]{2,1,0:T(2,128)} %param.12) | copy-start | bytes 221188
  5.3 7.8 %copy-start.3 = (f32[2,2,512]{2,1,0:T(2,128)S(1)}, f32[2,2,512]{2,1,0:T(2,128)}, u32[]{:S(2)}) copy-start(f32[2,2,512]{2,1,0:T(2,128)} %param.13) | copy-start | bytes 24580
  13.4 19.7 %collective-permute-start.4 = (f32[40,8,128]{2,1,0:T(8,128)S(1)}, f32[40,8,128]{2,1,0:T(8,128)S(1)}, u32[]{:S(2)}, u32[]{:S(2)}) collective-permute-start(f32[40,8,128]{2,1,0:T(8,128)S(1)} %advect.1.x_ref.refs_0_), channel_id=1, source_target_pairs={{0,1},{1,2},{2,3},{3,0},{4,5},{5,6},{6,7},{7,4},{8,9},{9,10},{10,1... | collective-permute-start | bytes 491528 | tf_op jit(solution)/shard_map/ppermute | solution.py:431
  16.4 16.7 %collective-permute-start.3 = (f32[40,8,128]{2,1,0:T(8,128)S(1)}, f32[40,8,128]{2,1,0:T(8,128)S(1)}, u32[]{:S(2)}, u32[]{:S(2)}) collective-permute-start(f32[40,8,128]{2,1,0:T(8,128)S(1)} %advect.1.x_ref.refs_0_), channel_id=1, source_target_pairs={{0,2},{1,3},{2,0},{3,1},{4,6},{5,7},{6,4},{7,5},{8,10},{9,11},{10,... | collective-permute-start | bytes 491528 | tf_op jit(solution)/shard_map/ppermute | solution.py:431
  20.6 12.5 %collective-permute-start.2 = (f32[40,8,128]{2,1,0:T(8,128)S(1)}, f32[40,8,128]{2,1,0:T(8,128)S(1)}, u32[]{:S(2)}, u32[]{:S(2)}) collective-permute-start(f32[40,8,128]{2,1,0:T(8,128)S(1)} %advect.1.x_ref.refs_0_), channel_id=1, source_target_pairs={{0,3},{1,0},{2,1},{3,2},{4,7},{5,4},{6,5},{7,6},{8,11},{9,8},{10,9... | collective-permute-start | bytes 491528 | tf_op jit(solution)/shard_map/ppermute | solution.py:431
  23.0 10.1 %copy-start.4 = (f32[72,72]{1,0:T(8,128)S(1)}, f32[72,72]{1,0:T(8,128)}, u32[]{:S(2)}) copy-start(f32[72,72]{1,0:T(8,128)} %mix_ref.1) | copy-start | bytes 62212
  23.0 28.9 %all-to-all-start = ((f32[64,1,3712]{2,1,0:T(1,128)}), f32[64,1,3712]{2,1,0:T(1,128)S(1)}, u32[]{:S(2)}, u32[]{:S(2)}) async-start(f32[64,1,3712]{2,1,0:T(1,128)} %bitcast.26), calls=%async_computation | async-start | bytes 1900544 | tf_op jit(solution)/shard_map/all_to_all | solution.py:468
  68.9 6.4 %collective-permute-start.7 = (f32[8,8,128]{2,1,0:T(8,128)S(1)}, f32[8,8,128]{2,1,0:T(8,128)S(1)}, u32[]{:S(2)}, u32[]{:S(2)}) collective-permute-start(f32[8,8,128]{2,1,0:T(8,128)S(1)} %home.1.a_ref), channel_id=1, source_target_pairs={{0,1},{1,2},{2,3},{3,0},{4,5},{5,6},{6,7},{7,4},{8,9},{9,10},{10,1... | collective-permute-start | bytes 98312 | tf_op jit(solution)/shard_map/ppermute | solution.py:431
  69.3 7.2 %collective-permute-start.6 = (f32[8,8,128]{2,1,0:T(8,128)S(1)}, f32[8,8,128]{2,1,0:T(8,128)S(1)}, u32[]{:S(2)}, u32[]{:S(2)}) collective-permute-start(f32[8,8,128]{2,1,0:T(8,128)S(1)} %home.1.a_ref), channel_id=1, source_target_pairs={{0,2},{1,3},{2,0},{3,1},{4,6},{5,7},{6,4},{7,5},{8,10},{9,11},{10,... | collective-permute-start | bytes 98312 | tf_op jit(solution)/shard_map/ppermute | solution.py:431
  73.7 4.5 %collective-permute-start.5 = (f32[8,8,128]{2,1,0:T(8,128)S(1)}, f32[8,8,128]{2,1,0:T(8,128)S(1)}, u32[]{:S(2)}, u32[]{:S(2)}) collective-permute-start(f32[8,8,128]{2,1,0:T(8,128)S(1)} %home.1.a_ref), channel_id=1, source_target_pairs={{0,3},{1,0},{2,1},{3,2},{4,7},{5,4},{6,5},{7,6},{8,11},{9,8},{10,9... | collective-permute-start | bytes 98312 | tf_op jit(solution)/shard_map/ppermute | solution.py:431

commit v5 on v4

--- a/solution.py
+++ b/solution.py
@@ -114,8 +114,8 @@
     out_ref[...] = x_ref[0]
 
 
-def mix_kernel(mix_ref, mark_ref, *refs):
-    *refs, out_ref, field_ref, den_ref = refs
+def mix_kernel(count_ref, mix_ref, mark_ref, *refs):
+    *refs, out_ref, field_ref, scale_ref = refs
     size = 2 * HERE + 4
 
     def block(d, row, count, sub):
@@ -166,7 +166,8 @@
                 out_ref[rows, sub + i, :] = half[0:HERE]
     for row in range(4):
         a, b, c, d = (weights(i, 2 * HERE + row) for i in range(4))
-        den_ref[row] = (a + c) + (b + d)
+        number = (row * SUBS + iota((SUBS, LANES), 0)) * LANES + iota((SUBS, LANES), 1)
+        scale_ref[row] = jnp.where(number < count_ref[0], 1.0 / ((a + c) + (b + d)), 0.0)
 
 
 def place(own, rank):
@@ -363,12 +364,13 @@
     plain, other, tail = (back_ref[pl.ds(j, TILES, stride=3), :] for j in range(3))
     first = jnp.concatenate([plain, tail], axis=1)
     second = jnp.concatenate([other, roll(tail, 64, 1)], axis=1)
-    high, low = split(jnp.concatenate([first, second], axis=0))
+    parts = jnp.concatenate(split(jnp.concatenate([first, second], axis=0)), axis=0)
     slot = iota((WIDE, 1), 0)
     for b in range(SND // WIDE):
         at = pl.ds(b * WIDE, WIDE)
         hot = (slot == (place_ref[:, at] & (WIDE - 1))).astype(F32).astype(BF16)
-        values = jnp.dot(high, hot, preferred_element_type=F32) + jnp.dot(low, hot, preferred_element_type=F32)
+        both = jnp.dot(parts, hot, preferred_element_type=F32)
+        values = both[0 : 2 * TILES] + both[2 * TILES :]
         mine = iota((TILES, WIDE), 0) == (place_ref[:, at] >> 8)
         for s in range(2):
             picked = jnp.where(mine, values[s * TILES : (s + 1) * TILES], 0.0)
@@ -378,15 +380,13 @@
                 out_ref[j // SUBS, j % SUBS : j % SUBS + 1, :] = total[:, i * LANES : (i + 1) * LANES]
 
 
-def last_kernel(count_ref, a_ref, b_ref, c_ref, d_ref, den_ref, out_ref):
-    count = count_ref[0]
+def last_kernel(a_ref, b_ref, d_ref, c_ref, scale_ref, out_ref):
     for row in range(4):
-        number = (row * SUBS + iota((SUBS, LANES), 0)) * LANES + iota((SUBS, LANES), 1)
-        den = den_ref[row]
+        scale = scale_ref[row]
         for s in range(2):
             k = s * 4 + row
             num = (a_ref[k] + c_ref[k]) + (b_ref[k] + d_ref[k])
-            value = jnp.where(number < count, num / den, 0.0)
+            value = jnp.where(scale > 0, num * scale, 0.0)
             for j in range(SUBS):
                 at = (row * SUBS + j) * LANES
                 out_ref[s : s + 1, at : at + LANES] = value[j : j + 1]
@@ -467,13 +467,13 @@
     send, mark = lax.optimization_barrier((send, mark))
     got = lax.all_to_all(send.reshape(TILES, 1, MESSAGE * LANES), "tile", 0, 0, tiled=True)
     got = got.reshape(TILES * MESSAGE, LANES)
-    transported, field, weight = call(
+    transported, field, scale = call(
         mix_kernel,
         [block, arr((SUBS, 2, ROWS, LANES)), arr((4, SUBS, LANES))],
-        [spec()] * (5 + len(across)),
+        [spec(SMEM)] + [spec()] * (5 + len(across)),
         flops=10**11,
         name="mix",
-    )(mixing, mark, adv, up, *across, down)
+    )(counts, mixing, mark, adv, up, *across, down)
     sums = call(
         sample_kernel,
         arr((3 * TILES, LANES)),
@@ -486,7 +486,7 @@
     back = back.reshape(3 * TILES, LANES)
     mine = call(home_kernel, arr((8, SUBS, LANES)), [spec()] * 2, name="home")(back, place_of)
     nums = [shift(mine, "lev", -d) for d in (1, 2, 3)]
-    evolved = call(last_kernel, arr((2, SND)), [spec(SMEM)] + [spec()] * 5, name="last")(counts, mine, *nums, weight)
+    evolved = call(last_kernel, arr((2, SND)), [spec()] * 5, name="last")(mine, nums[0], nums[2], nums[1], scale)
     out = transported.reshape(2 * HERE, 4, 2, LANES).transpose(0, 2, 1, 3).reshape(tracer.shape)
     return out, evolved
 

time: 79.1 us -> 78.6 us (level)
  transfers between devices with their start and end apart: 9 -> 9, of which waited for: 3 -> 4; matrix products, arithmetic and copies ran while one was open for 0% -> 0% of each run, Pallas kernels for 2% -> 2%
where the time goes in v5:
time: 78.6 us; the launch traced here: 78.3 us
  starting transfers between devices  28.7 us (37%)
  waiting for transfers between devices  20 us (25%)
  Pallas kernels  15.8 us (20%)
  blocking collectives  12.2 us (16%)
  between operations  1.49 us (2%)
    all_to_all x1, waiting for transfers between devices, body(): lax.all_to_all(send.reshape(TILES, 1, MESSAGE * LANES), 'tile', 0, 0, til...  16.9 us
    ppermute x6, starting transfers between devices, shift(): lax.ppermute(x, axis, [(i, (i + distance) % size) for i in range(size)])  15.4 us
    all_to_all x1, blocking collectives, body(): lax.all_to_all(sums.reshape(TILES, 1, 3 * LANES), 'tile', 0, 0, tiled=True)  12.2 us
    all_to_all x1, starting transfers between devices, body(): lax.all_to_all(send.reshape(TILES, 1, MESSAGE * LANES), 'tile', 0, 0, til...  9.97 us
    pallas_call x1, Pallas kernels, body(): call(send_kernel, [arr((TILES * MESSAGE, LANES)), arr((1, SND), jnp.int32...  7.76 us
    pallas_call x1, Pallas kernels, body(): call(sample_kernel, arr((3 * TILES, LANES)), [spec()] * 2, [pltpu.VMEM((8...  3.46 us
    ppermute x2, starting transfers between devices, swapped(): return lax.ppermute(x, 'tile', pairs + [(b, a) for a, b in pairs])  3.33 us
    ppermute x6, waiting for transfers between devices, shift(): lax.ppermute(x, axis, [(i, (i + distance) % size) for i in range(size)])  3.15 us
  transfers between devices with their start and end apart: 9, of which 4 were waited for; matrix products, arithmetic and copies ran while one was open for 0% of the time, Pallas kernels for 2%

profile of v5, /device:TPU:1, one launch (start us, length us, event | category | flops | bytes accessed | tf_op | source)
XLA Modules:
  0.0 78.3 jit_solution(10560229558494618629)
XLA Ops:
  0.6 0.0 copy-start.5
  0.6 0.0 copy-start.6
  0.7 0.0 copy-start.7
  0.7 1.2 %halo.1 = (f32[45,8,128]{2,1,0:T(8,128)S(1)}, f32[45,8,128]{2,1,0:T(8,128)S(1)}, f32[36,8,128]{2,1,0:T(8,128)S(1)}) custom-call(f32[36,8,128]{2,1,0:T(8,128)} %bitcast.33, f32[18,8,128]{2,1,0:T(8,128)} %bitcast.37, f32[18,8,128]{2,1,0:T(8,128)} %bitcast.39, f32[2,8,128]{2,1,0:T(8,128)} %bitcast.41), custom_call_target="tpu_custom_call" | custom-call | flops 1000000 | bytes 100000 | tf_op jit(solution)/shard_map/halo/pallas_call | solution.py:438
  1.9 3.3 %collective-permute-start = (f32[45,8,128]{2,1,0:T(8,128)S(1)}, f32[45,8,128]{2,1,0:T(8,128)S(1)}, u32[]{:S(2)}, u32[]{:S(2)}) collective-permute-start(f32[45,8,128]{2,1,0:T(8,128)S(1)} %get-tuple-element.15), channel_id=1, source_target_pairs={{0,4},{8,12},{16,20},{24,28},{32,36},{40,44},{48,52},{56,60},{64,6... | collective-permute-start | bytes 552968 | tf_op jit(solution)/shard_map/ppermute | solution.py:422
  5.2 0.0 collective-permute-start.1
  5.2 0.0 copy-done.5
  5.2 0.0 copy-done.6
  5.3 0.0 copy-done.7
  5.3 0.0 copy-start
  5.3 0.0 copy-start.1
  5.3 0.0 copy-start.2
  5.3 0.0 copy-start.3
  5.3 7.8 %send.1 = (f32[1856,128]{1,0:T(8,128)}, s32[1,4096]{1,0:T(1,128)S(1)}, f32[4,8,128]{2,1,0:T(8,128)S(1)}) custom-call(f32[18,4096]{1,0:T(8,128)} %kern_in.1, s32[1,4096]{1,0:T(1,128)S(1)} %bitcast.43, s32[1,4096]{1,0:T(1,128)S(1)} %bitcast.44, s32[1,4096]{1,0:T(1,128)S(1)} %bitcast.45, f32[36,8,128]{2,1,0:T(8,128)S(1)} %get-tuple-element.13.part_ref), custom_call_target="tpu_custom_call" | custom-call | flops 8999999488 | bytes 100000 | tf_op jit(solution)/shard_map/send/pallas_call | solution.py:452
  13.1 0.0 collective-permute-done.near_ref
  13.1 0.0 collective-permute-done.1.far_ref
  13.1 0.0 copy-done
  13.1 0.0 copy-done.1
  13.1 0.0 copy-done.2
  13.1 0.0 copy-done.3
  13.1 0.3 advect.1.x_ref.refs_0_
  13.4 3.0 %collective-permute-start.4 = (f32[40,8,128]{2,1,0:T(8,128)S(1)}, f32[40,8,128]{2,1,0:T(8,128)S(1)}, u32[]{:S(2)}, u32[]{:S(2)}) collective-permute-start(f32[40,8,128]{2,1,0:T(8,128)S(1)} %advect.1.x_ref.refs_0_), channel_id=1, source_target_pairs={{0,1},{1,2},{2,3},{3,0},{4,5},{5,6},{6,7},{7,4},{8,9},{9,10},{10,1... | collective-permute-start | bytes 491528 | tf_op jit(solution)/shard_map/ppermute | solution.py:431
  16.4 4.2 %collective-permute-start.3 = (f32[40,8,128]{2,1,0:T(8,128)S(1)}, f32[40,8,128]{2,1,0:T(8,128)S(1)}, u32[]{:S(2)}, u32[]{:S(2)}) collective-permute-start(f32[40,8,128]{2,1,0:T(8,128)S(1)} %advect.1.x_ref.refs_0_), channel_id=1, source_target_pairs={{0,2},{1,3},{2,0},{3,1},{4,6},{5,7},{6,4},{7,5},{8,10},{9,11},{10,... | collective-permute-start | bytes 491528 | tf_op jit(solution)/shard_map/ppermute | solution.py:431
  20.6 2.4 %collective-permute-start.2 = (f32[40,8,128]{2,1,0:T(8,128)S(1)}, f32[40,8,128]{2,1,0:T(8,128)S(1)}, u32[]{:S(2)}, u32[]{:S(2)}) collective-permute-start(f32[40,8,128]{2,1,0:T(8,128)S(1)} %advect.1.x_ref.refs_0_), channel_id=1, source_target_pairs={{0,3},{1,0},{2,1},{3,2},{4,7},{5,4},{6,5},{7,6},{8,11},{9,8},{10,9... | collective-permute-start | bytes 491528 | tf_op jit(solution)/shard_map/ppermute | solution.py:431
  23.6 0.0 copy-start.4
  23.6 10.0 %all-to-all-start = ((f32[64,1,3712]{2,1,0:T(1,128)}), f32[64,1,3712]{2,1,0:T(1,128)S(1)}, u32[]{:S(2)}, u32[]{:S(2)}) async-start(f32[64,1,3712]{2,1,0:T(1,128)} %bitcast.26), calls=%async_computation | async-start | bytes 1900544 | tf_op jit(solution)/shard_map/all_to_all | solution.py:468
  33.6 0.0 collective-permute-done.4.refs_3_
  33.6 0.0 collective-permute-done.3.refs_2_
  33.6 0.0 collective-permute-done.2.refs_1_
  33.6 0.0 copy-done.4
  33.6 1.3 %mix.1 = (f32[36,8,128]{2,1,0:T(8,128)}, f32[8,2,24,128]{3,2,1,0:T(8,128)S(1)}, f32[4,8,128]{2,1,0:T(8,128)S(1)}) custom-call(s32[1]{0:T(128)S(6)} %copy.24.count_ref, f32[72,72]{1,0:T(8,128)S(1)} %copy-done.4, f32[8,128]{1,0:T(8,128)S(1)} %mark.1.mark_ref, f32[40,8,128]{2,1,0:T(8,128)S(1)} %advect.1.x_ref.refs_0_, ...), custom_call_target="tpu_custom_call" | custom-call | flops 99999997952 | bytes 100000 | tf_op jit(solution)/shard_map/mix/pallas_call | solution.py:470
  35.0 16.9 %all-to-all-done = f32[64,1,3712]{2,1,0:T(1,128)S(1)} async-done(((f32[64,1,3712]{2,1,0:T(1,128)}), f32[64,1,3712]{2,1,0:T(1,128)S(1)}, u32[]{:S(2)}, u32[]{:S(2)}) %all-to-all-start) | async-done | bytes 950304 | tf_op jit(solution)/shard_map/all_to_all | solution.py:468
  51.8 3.5 %sample.1 = f32[192,128]{1,0:T(8,128)S(1)} custom-call(f32[1856,128]{1,0:T(8,128)S(1)} %bitcast.32, f32[8,2,24,128]{3,2,1,0:T(8,128)S(1)} %get-tuple-element.21.field_ref), custom_call_target="tpu_custom_call" | custom-call | flops 1000000 | bytes 100000 | tf_op jit(solution)/shard_map/sample/pallas_call | solution.py:477
  55.3 12.2 %all_to_all.10 = f32[64,1,384]{2,1,0:T(1,128)S(1)} all-to-all(f32[64,1,384]{2,1,0:T(1,128)S(1)} %bitcast.36), channel_id=1, replica_groups=mesh['tile'=64,'lev'=4] {'tile'}, dimensions={0} | all-to-all | bytes 196608 | tf_op jit(solution)/shard_map/all_to_all | solution.py:485
  67.5 1.1 %home.1.a_ref = f32[8,8,128]{2,1,0:T(8,128)S(1)} custom-call(f32[192,128]{1,0:T(8,128)S(1)} %bitcast.35, s32[1,4096]{1,0:T(1,128)S(1)} %get-tuple-element.22.place_ref), custom_call_target="tpu_custom_call" | custom-call | flops 1000000 | bytes 100000 | tf_op jit(solution)/shard_map/home/pallas_call | solution.py:487
  68.6 2.3 %collective-permute-start.7 = (f32[8,8,128]{2,1,0:T(8,128)S(1)}, f32[8,8,128]{2,1,0:T(8,128)S(1)}, u32[]{:S(2)}, u32[]{:S(2)}) collective-permute-start(f32[8,8,128]{2,1,0:T(8,128)S(1)} %home.1.a_ref), channel_id=1, source_target_pairs={{0,2},{1,3},{2,0},{3,1},{4,6},{5,7},{6,4},{7,5},{8,10},{9,11},{10,... | collective-permute-start | bytes 98312 | tf_op jit(solution)/shard_map/ppermute | solution.py:431
  70.9 2.6 %collective-permute-start.6 = (f32[8,8,128]{2,1,0:T(8,128)S(1)}, f32[8,8,128]{2,1,0:T(8,128)S(1)}, u32[]{:S(2)}, u32[]{:S(2)}) collective-permute-start(f32[8,8,128]{2,1,0:T(8,128)S(1)} %home.1.a_ref), channel_id=1, source_target_pairs={{0,1},{1,2},{2,3},{3,0},{4,5},{5,6},{6,7},{7,4},{8,9},{9,10},{10,1... | collective-permute-start | bytes 98312 | tf_op jit(solution)/shard_map/ppermute | solution.py:431
  73.5 1.0 %collective-permute-start.5 = (f32[8,8,128]{2,1,0:T(8,128)S(1)}, f32[8,8,128]{2,1,0:T(8,128)S(1)}, u32[]{:S(2)}, u32[]{:S(2)}) collective-permute-start(f32[8,8,128]{2,1,0:T(8,128)S(1)} %home.1.a_ref), channel_id=1, source_target_pairs={{0,3},{1,0},{2,1},{3,2},{4,7},{5,4},{6,5},{7,6},{8,11},{9,8},{10,9... | collective-permute-start | bytes 98312 | tf_op jit(solution)/shard_map/ppermute | solution.py:431
  74.5 0.9 %collective-permute-done.7.c_ref = f32[8,8,128]{2,1,0:T(8,128)S(1)} collective-permute-done((f32[8,8,128]{2,1,0:T(8,128)S(1)}, f32[8,8,128]{2,1,0:T(8,128)S(1)}, u32[]{:S(2)}, u32[]{:S(2)}) %collective-permute-start.7) | collective-permute-done | bytes 32800 | tf_op jit(solution)/shard_map/ppermute | solution.py:431
  75.4 1.3 %collective-permute-done.6.d_ref = f32[8,8,128]{2,1,0:T(8,128)S(1)} collective-permute-done((f32[8,8,128]{2,1,0:T(8,128)S(1)}, f32[8,8,128]{2,1,0:T(8,128)S(1)}, u32[]{:S(2)}, u32[]{:S(2)}) %collective-permute-start.6) | collective-permute-done | bytes 32800 | tf_op jit(solution)/shard_map/ppermute | solution.py:431
  76.7 1.0 %collective-permute-done.5.b_ref = f32[8,8,128]{2,1,0:T(8,128)S(1)} collective-permute-done((f32[8,8,128]{2,1,0:T(8,128)S(1)}, f32[8,8,128]{2,1,0:T(8,128)S(1)}, u32[]{:S(2)}, u32[]{:S(2)}) %collective-permute-start.5) | collective-permute-done | bytes 32800 | tf_op jit(solution)/shard_map/ppermute | solution.py:431
  77.6 0.6 last.1
  (1 shorter events, 0.0 us)
Async XLA Ops:
  0.6 4.6 %copy-start.5 = (s32[4096]{0:T(1024)S(1)}, s32[4096]{0:T(1024)}, u32[]{:S(2)}) copy-start(s32[4096]{0:T(1024)} %param.16) | copy-start | bytes 49156
  0.6 4.6 %copy-start.6 = (s32[4096]{0:T(1024)S(1)}, s32[4096]{0:T(1024)}, u32[]{:S(2)}) copy-start(s32[4096]{0:T(1024)} %param.17) | copy-start | bytes 49156
  0.7 4.6 %copy-start.7 = (s32[4096]{0:T(1024)S(1)}, s32[4096]{0:T(1024)}, u32[]{:S(2)}) copy-start(s32[4096]{0:T(1024)} %param.18) | copy-start | bytes 49156
  1.9 11.2 %collective-permute-start = (f32[45,8,128]{2,1,0:T(8,128)S(1)}, f32[45,8,128]{2,1,0:T(8,128)S(1)}, u32[]{:S(2)}, u32[]{:S(2)}) collective-permute-start(f32[45,8,128]{2,1,0:T(8,128)S(1)} %get-tuple-element.15), channel_id=1, source_target_pairs={{0,4},{8,12},{16,20},{24,28},{32,36},{40,44},{48,52},{56,60},{64,6... | collective-permute-start | bytes 552968 | tf_op jit(solution)/shard_map/ppermute | solution.py:422
  5.2 7.8 %collective-permute-start.1 = (f32[45,8,128]{2,1,0:T(8,128)S(1)}, f32[45,8,128]{2,1,0:T(8,128)S(1)}, u32[]{:S(2)}, u32[]{:S(2)}) collective-permute-start(f32[45,8,128]{2,1,0:T(8,128)S(1)} %get-tuple-element.16), channel_id=1, source_target_pairs={{4,8},{12,16},{20,24},{28,32},{36,40},{44,48},{52,56},{60,64},{68,... | collective-permute-start | bytes 552968 | tf_op jit(solution)/shard_map/ppermute | solution.py:422
  5.3 7.8 %copy-start = (f32[2,18,2,512]{3,2,1,0:T(2,128)S(1)}, f32[2,18,2,512]{3,2,1,0:T(2,128)}, u32[]{:S(2)}) copy-start(f32[2,18,2,512]{3,2,1,0:T(2,128)} %param.10) | copy-start | bytes 442372
  5.3 7.8 %copy-start.1 = (f32[18,2,512]{2,1,0:T(2,128)S(1)}, f32[18,2,512]{2,1,0:T(2,128)}, u32[]{:S(2)}) copy-start(f32[18,2,512]{2,1,0:T(2,128)} %param.11) | copy-start | bytes 221188
  5.3 7.8 %copy-start.2 = (f32[18,2,512]{2,1,0:T(2,128)S(1)}, f32[18,2,512]{2,1,0:T(2,128)}, u32[]{:S(2)}) copy-start(f32[18,2,512]{2,1,0:T(2,128)} %param.12) | copy-start | bytes 221188
  5.3 7.8 %copy-start.3 = (f32[2,2,512]{2,1,0:T(2,128)S(1)}, f32[2,2,512]{2,1,0:T(2,128)}, u32[]{:S(2)}) copy-start(f32[2,2,512]{2,1,0:T(2,128)} %param.13) | copy-start | bytes 24580
  13.4 20.2 %collective-permute-start.4 = (f32[40,8,128]{2,1,0:T(8,128)S(1)}, f32[40,8,128]{2,1,0:T(8,128)S(1)}, u32[]{:S(2)}, u32[]{:S(2)}) collective-permute-start(f32[40,8,128]{2,1,0:T(8,128)S(1)} %advect.1.x_ref.refs_0_), channel_id=1, source_target_pairs={{0,1},{1,2},{2,3},{3,0},{4,5},{5,6},{6,7},{7,4},{8,9},{9,10},{10,1... | collective-permute-start | bytes 491528 | tf_op jit(solution)/shard_map/ppermute | solution.py:431
  16.4 17.3 %collective-permute-start.3 = (f32[40,8,128]{2,1,0:T(8,128)S(1)}, f32[40,8,128]{2,1,0:T(8,128)S(1)}, u32[]{:S(2)}, u32[]{:S(2)}) collective-permute-start(f32[40,8,128]{2,1,0:T(8,128)S(1)} %advect.1.x_ref.refs_0_), channel_id=1, source_target_pairs={{0,2},{1,3},{2,0},{3,1},{4,6},{5,7},{6,4},{7,5},{8,10},{9,11},{10,... | collective-permute-start | bytes 491528 | tf_op jit(solution)/shard_map/ppermute | solution.py:431
  20.6 13.1 %collective-permute-start.2 = (f32[40,8,128]{2,1,0:T(8,128)S(1)}, f32[40,8,128]{2,1,0:T(8,128)S(1)}, u32[]{:S(2)}, u32[]{:S(2)}) collective-permute-start(f32[40,8,128]{2,1,0:T(8,128)S(1)} %advect.1.x_ref.refs_0_), channel_id=1, source_target_pairs={{0,3},{1,0},{2,1},{3,2},{4,7},{5,4},{6,5},{7,6},{8,11},{9,8},{10,9... | collective-permute-start | bytes 491528 | tf_op jit(solution)/shard_map/ppermute | solution.py:431
  23.6 10.0 %copy-start.4 = (f32[72,72]{1,0:T(8,128)S(1)}, f32[72,72]{1,0:T(8,128)}, u32[]{:S(2)}) copy-start(f32[72,72]{1,0:T(8,128)} %mix_ref.1) | copy-start | bytes 62212
  23.6 28.2 %all-to-all-start = ((f32[64,1,3712]{2,1,0:T(1,128)}), f32[64,1,3712]{2,1,0:T(1,128)S(1)}, u32[]{:S(2)}, u32[]{:S(2)}) async-start(f32[64,1,3712]{2,1,0:T(1,128)} %bitcast.26), calls=%async_computation | async-start | bytes 1900544 | tf_op jit(solution)/shard_map/all_to_all | solution.py:468
  68.6 6.8 %collective-permute-start.7 = (f32[8,8,128]{2,1,0:T(8,128)S(1)}, f32[8,8,128]{2,1,0:T(8,128)S(1)}, u32[]{:S(2)}, u32[]{:S(2)}) collective-permute-start(f32[8,8,128]{2,1,0:T(8,128)S(1)} %home.1.a_ref), channel_id=1, source_target_pairs={{0,2},{1,3},{2,0},{3,1},{4,6},{5,7},{6,4},{7,5},{8,10},{9,11},{10,... | collective-permute-start | bytes 98312 | tf_op jit(solution)/shard_map/ppermute | solution.py:431
  70.9 5.8 %collective-permute-start.6 = (f32[8,8,128]{2,1,0:T(8,128)S(1)}, f32[8,8,128]{2,1,0:T(8,128)S(1)}, u32[]{:S(2)}, u32[]{:S(2)}) collective-permute-start(f32[8,8,128]{2,1,0:T(8,128)S(1)} %home.1.a_ref), channel_id=1, source_target_pairs={{0,1},{1,2},{2,3},{3,0},{4,5},{5,6},{6,7},{7,4},{8,9},{9,10},{10,1... | collective-permute-start | bytes 98312 | tf_op jit(solution)/shard_map/ppermute | solution.py:431
  73.5 4.1 %collective-permute-start.5 = (f32[8,8,128]{2,1,0:T(8,128)S(1)}, f32[8,8,128]{2,1,0:T(8,128)S(1)}, u32[]{:S(2)}, u32[]{:S(2)}) collective-permute-start(f32[8,8,128]{2,1,0:T(8,128)S(1)} %home.1.a_ref), channel_id=1, source_target_pairs={{0,3},{1,0},{2,1},{3,2},{4,7},{5,4},{6,5},{7,6},{8,11},{9,8},{10,9... | collective-permute-start | bytes 98312 | tf_op jit(solution)/shard_map/ppermute | solution.py:431

commit v6 on v5

--- a/solution.py
+++ b/solution.py
@@ -116,6 +116,7 @@
 
 def mix_kernel(count_ref, mix_ref, mark_ref, *refs):
     *refs, out_ref, field_ref, scale_ref = refs
+    refs = [refs[i] for i in (0, 1, 3, 2)]
     size = 2 * HERE + 4
 
     def block(d, row, count, sub):
@@ -473,7 +474,7 @@
         [spec(SMEM)] + [spec()] * (5 + len(across)),
         flops=10**11,
         name="mix",
-    )(counts, mixing, mark, adv, up, *across, down)
+    )(counts, mixing, mark, adv, up, down, *across)
     sums = call(
         sample_kernel,
         arr((3 * TILES, LANES)),

time: 78.6 us -> 77.8 us (0.990)
  waiting for transfers between devices: 20 us -> 17.7 us
  starting transfers between devices: 28.7 us -> 30.2 us
    all_to_all x1, waiting for transfers between devices: 16.9 us -> 14.1 us  [body(): lax.all_to_all(send.reshape(TILES, 1, MESSAGE * LANES), 'tile', 0, 0, til...]
    ppermute x6, starting transfers between devices: 15.4 us -> 16.9 us  [shift(): lax.ppermute(x, axis, [(i, (i + distance) % size) for i in range(size)])]
  transfers between devices with their start and end apart: 9 -> 9, of which waited for: 4 -> 3; matrix products, arithmetic and copies ran while one was open for 0% -> 0% of each run, Pallas kernels for 2% -> 2%
where the time goes in v6:
time: 77.8 us; the launch traced here: 77.5 us
  starting transfers between devices  30.2 us (39%)
  waiting for transfers between devices  17.7 us (23%)
  Pallas kernels  15.7 us (20%)
  blocking collectives  12.3 us (16%)
  between operations  1.47 us (2%)
    ppermute x6, starting transfers between devices, shift(): lax.ppermute(x, axis, [(i, (i + distance) % size) for i in range(size)])  16.9 us
    all_to_all x1, waiting for transfers between devices, body(): lax.all_to_all(send.reshape(TILES, 1, MESSAGE * LANES), 'tile', 0, 0, til...  14.1 us
    all_to_all x1, blocking collectives, body(): lax.all_to_all(sums.reshape(TILES, 1, 3 * LANES), 'tile', 0, 0, tiled=True)  12.3 us
    all_to_all x1, starting transfers between devices, body(): lax.all_to_all(send.reshape(TILES, 1, MESSAGE * LANES), 'tile', 0, 0, til...  9.97 us
    pallas_call x1, Pallas kernels, body(): call(send_kernel, [arr((TILES * MESSAGE, LANES)), arr((1, SND), jnp.int32...  7.76 us
    ppermute x6, waiting for transfers between devices, shift(): lax.ppermute(x, axis, [(i, (i + distance) % size) for i in range(size)])  3.63 us
    pallas_call x1, Pallas kernels, body(): call(sample_kernel, arr((3 * TILES, LANES)), [spec()] * 2, [pltpu.VMEM((8...  3.45 us
    ppermute x2, starting transfers between devices, swapped(): return lax.ppermute(x, 'tile', pairs + [(b, a) for a, b in pairs])  3.33 us
  transfers between devices with their start and end apart: 9, of which 3 were waited for; matrix products, arithmetic and copies ran while one was open for 0% of the time, Pallas kernels for 2%

profile of v6, /device:TPU:1, one launch (start us, length us, event | category | flops | bytes accessed | tf_op | source)
XLA Modules:
  0.0 77.5 jit_solution(4522587398263871237)
XLA Ops:
  0.6 0.0 copy-start.5
  0.6 0.0 copy-start.6
  0.7 0.0 copy-start.7
  0.7 1.2 %halo.1 = (f32[45,8,128]{2,1,0:T(8,128)S(1)}, f32[45,8,128]{2,1,0:T(8,128)S(1)}, f32[36,8,128]{2,1,0:T(8,128)S(1)}) custom-call(f32[36,8,128]{2,1,0:T(8,128)} %bitcast.33, f32[18,8,128]{2,1,0:T(8,128)} %bitcast.37, f32[18,8,128]{2,1,0:T(8,128)} %bitcast.39, f32[2,8,128]{2,1,0:T(8,128)} %bitcast.41), custom_call_target="tpu_custom_call" | custom-call | flops 1000000 | bytes 100000 | tf_op jit(solution)/shard_map/halo/pallas_call | solution.py:439
  1.9 3.3 %collective-permute-start = (f32[45,8,128]{2,1,0:T(8,128)S(1)}, f32[45,8,128]{2,1,0:T(8,128)S(1)}, u32[]{:S(2)}, u32[]{:S(2)}) collective-permute-start(f32[45,8,128]{2,1,0:T(8,128)S(1)} %get-tuple-element.15), channel_id=1, source_target_pairs={{0,4},{8,12},{16,20},{24,28},{32,36},{40,44},{48,52},{56,60},{64,6... | collective-permute-start | bytes 552968 | tf_op jit(solution)/shard_map/ppermute | solution.py:423
  5.2 0.0 collective-permute-start.1
  5.2 0.0 copy-done.5
  5.2 0.0 copy-done.6
  5.3 0.0 copy-done.7
  5.3 0.0 copy-start
  5.3 0.0 copy-start.1
  5.3 0.0 copy-start.2
  5.3 0.0 copy-start.3
  5.3 7.8 %send.1 = (f32[1856,128]{1,0:T(8,128)}, s32[1,4096]{1,0:T(1,128)S(1)}, f32[4,8,128]{2,1,0:T(8,128)S(1)}) custom-call(f32[18,4096]{1,0:T(8,128)} %kern_in.1, s32[1,4096]{1,0:T(1,128)S(1)} %bitcast.43, s32[1,4096]{1,0:T(1,128)S(1)} %bitcast.44, s32[1,4096]{1,0:T(1,128)S(1)} %bitcast.45, f32[36,8,128]{2,1,0:T(8,128)S(1)} %get-tuple-element.13.part_ref), custom_call_target="tpu_custom_call" | custom-call | flops 8999999488 | bytes 100000 | tf_op jit(solution)/shard_map/send/pallas_call | solution.py:453
  13.1 0.0 collective-permute-done.near_ref
  13.1 0.0 collective-permute-done.1.far_ref
  13.1 0.0 copy-done
  13.1 0.0 copy-done.1
  13.1 0.0 copy-done.2
  13.1 0.0 copy-done.3
  13.1 0.3 advect.1.x_ref.refs_0_
  13.4 6.0 %collective-permute-start.4 = (f32[40,8,128]{2,1,0:T(8,128)S(1)}, f32[40,8,128]{2,1,0:T(8,128)S(1)}, u32[]{:S(2)}, u32[]{:S(2)}) collective-permute-start(f32[40,8,128]{2,1,0:T(8,128)S(1)} %advect.1.x_ref.refs_0_), channel_id=1, source_target_pairs={{0,2},{1,3},{2,0},{3,1},{4,6},{5,7},{6,4},{7,5},{8,10},{9,11},{10,... | collective-permute-start | bytes 491528 | tf_op jit(solution)/shard_map/ppermute | solution.py:432
  19.4 1.2 %collective-permute-start.3 = (f32[40,8,128]{2,1,0:T(8,128)S(1)}, f32[40,8,128]{2,1,0:T(8,128)S(1)}, u32[]{:S(2)}, u32[]{:S(2)}) collective-permute-start(f32[40,8,128]{2,1,0:T(8,128)S(1)} %advect.1.x_ref.refs_0_), channel_id=1, source_target_pairs={{0,1},{1,2},{2,3},{3,0},{4,5},{5,6},{6,7},{7,4},{8,9},{9,10},{10,1... | collective-permute-start | bytes 491528 | tf_op jit(solution)/shard_map/ppermute | solution.py:432
  20.6 2.4 %collective-permute-start.2 = (f32[40,8,128]{2,1,0:T(8,128)S(1)}, f32[40,8,128]{2,1,0:T(8,128)S(1)}, u32[]{:S(2)}, u32[]{:S(2)}) collective-permute-start(f32[40,8,128]{2,1,0:T(8,128)S(1)} %advect.1.x_ref.refs_0_), channel_id=1, source_target_pairs={{0,3},{1,0},{2,1},{3,2},{4,7},{5,4},{6,5},{7,6},{8,11},{9,8},{10,9... | collective-permute-start | bytes 491528 | tf_op jit(solution)/shard_map/ppermute | solution.py:432
  23.6 0.0 copy-start.4
  23.6 10.0 %all-to-all-start = ((f32[64,1,3712]{2,1,0:T(1,128)}), f32[64,1,3712]{2,1,0:T(1,128)S(1)}, u32[]{:S(2)}, u32[]{:S(2)}) async-start(f32[64,1,3712]{2,1,0:T(1,128)} %bitcast.26), calls=%async_computation | async-start | bytes 1900544 | tf_op jit(solution)/shard_map/all_to_all | solution.py:469
  33.6 0.0 collective-permute-done.4.refs_3_
  33.6 0.0 collective-permute-done.3.refs_2_
  33.6 2.0 %collective-permute-done.2.refs_1_ = f32[40,8,128]{2,1,0:T(8,128)S(1)} collective-permute-done((f32[40,8,128]{2,1,0:T(8,128)S(1)}, f32[40,8,128]{2,1,0:T(8,128)S(1)}, u32[]{:S(2)}, u32[]{:S(2)}) %collective-permute-start.2) | collective-permute-done | bytes 163872 | tf_op jit(solution)/shard_map/ppermute | solution.py:432
  35.6 0.0 copy-done.4
  35.6 1.3 %mix.1 = (f32[36,8,128]{2,1,0:T(8,128)}, f32[8,2,24,128]{3,2,1,0:T(8,128)S(1)}, f32[4,8,128]{2,1,0:T(8,128)S(1)}) custom-call(s32[1]{0:T(128)S(6)} %copy.24.count_ref, f32[72,72]{1,0:T(8,128)S(1)} %copy-done.4, f32[8,128]{1,0:T(8,128)S(1)} %mark.1.mark_ref, f32[40,8,128]{2,1,0:T(8,128)S(1)} %advect.1.x_ref.refs_0_, ...), custom_call_target="tpu_custom_call" | custom-call | flops 99999997952 | bytes 100000 | tf_op jit(solution)/shard_map/mix/pallas_call | solution.py:471
  36.9 14.1 %all-to-all-done = f32[64,1,3712]{2,1,0:T(1,128)S(1)} async-done(((f32[64,1,3712]{2,1,0:T(1,128)}), f32[64,1,3712]{2,1,0:T(1,128)S(1)}, u32[]{:S(2)}, u32[]{:S(2)}) %all-to-all-start) | async-done | bytes 950304 | tf_op jit(solution)/shard_map/all_to_all | solution.py:469
  51.0 3.5 %sample.1 = f32[192,128]{1,0:T(8,128)S(1)} custom-call(f32[1856,128]{1,0:T(8,128)S(1)} %bitcast.32, f32[8,2,24,128]{3,2,1,0:T(8,128)S(1)} %get-tuple-element.21.field_ref), custom_call_target="tpu_custom_call" | custom-call | flops 1000000 | bytes 100000 | tf_op jit(solution)/shard_map/sample/pallas_call | solution.py:478
  54.5 12.3 %all_to_all.10 = f32[64,1,384]{2,1,0:T(1,128)S(1)} all-to-all(f32[64,1,384]{2,1,0:T(1,128)S(1)} %bitcast.36), channel_id=1, replica_groups=mesh['tile'=64,'lev'=4] {'tile'}, dimensions={0} | all-to-all | bytes 196608 | tf_op jit(solution)/shard_map/all_to_all | solution.py:486
  66.8 1.1 %home.1.a_ref = f32[8,8,128]{2,1,0:T(8,128)S(1)} custom-call(f32[192,128]{1,0:T(8,128)S(1)} %bitcast.35, s32[1,4096]{1,0:T(1,128)S(1)} %get-tuple-element.22.place_ref), custom_call_target="tpu_custom_call" | custom-call | flops 1000000 | bytes 100000 | tf_op jit(solution)/shard_map/home/pallas_call | solution.py:488
  67.9 3.8 %collective-permute-start.7 = (f32[8,8,128]{2,1,0:T(8,128)S(1)}, f32[8,8,128]{2,1,0:T(8,128)S(1)}, u32[]{:S(2)}, u32[]{:S(2)}) collective-permute-start(f32[8,8,128]{2,1,0:T(8,128)S(1)} %home.1.a_ref), channel_id=1, source_target_pairs={{0,2},{1,3},{2,0},{3,1},{4,6},{5,7},{6,4},{7,5},{8,10},{9,11},{10,... | collective-permute-start | bytes 98312 | tf_op jit(solution)/shard_map/ppermute | solution.py:432
  71.6 1.0 %collective-permute-start.6 = (f32[8,8,128]{2,1,0:T(8,128)S(1)}, f32[8,8,128]{2,1,0:T(8,128)S(1)}, u32[]{:S(2)}, u32[]{:S(2)}) collective-permute-start(f32[8,8,128]{2,1,0:T(8,128)S(1)} %home.1.a_ref), channel_id=1, source_target_pairs={{0,1},{1,2},{2,3},{3,0},{4,5},{5,6},{6,7},{7,4},{8,9},{9,10},{10,1... | collective-permute-start | bytes 98312 | tf_op jit(solution)/shard_map/ppermute | solution.py:432
  72.6 2.6 %collective-permute-start.5 = (f32[8,8,128]{2,1,0:T(8,128)S(1)}, f32[8,8,128]{2,1,0:T(8,128)S(1)}, u32[]{:S(2)}, u32[]{:S(2)}) collective-permute-start(f32[8,8,128]{2,1,0:T(8,128)S(1)} %home.1.a_ref), channel_id=1, source_target_pairs={{0,3},{1,0},{2,1},{3,2},{4,7},{5,4},{6,5},{7,6},{8,11},{9,8},{10,9... | collective-permute-start | bytes 98312 | tf_op jit(solution)/shard_map/ppermute | solution.py:432
  75.2 0.0 collective-permute-done.7.c_ref
  75.2 1.6 %collective-permute-done.6.d_ref = f32[8,8,128]{2,1,0:T(8,128)S(1)} collective-permute-done((f32[8,8,128]{2,1,0:T(8,128)S(1)}, f32[8,8,128]{2,1,0:T(8,128)S(1)}, u32[]{:S(2)}, u32[]{:S(2)}) %collective-permute-start.6) | collective-permute-done | bytes 32800 | tf_op jit(solution)/shard_map/ppermute | solution.py:432
  76.8 0.0 collective-permute-done.5.b_ref
  76.8 0.6 last.1
  (1 shorter events, 0.0 us)
Async XLA Ops:
  0.6 4.6 %copy-start.5 = (s32[4096]{0:T(1024)S(1)}, s32[4096]{0:T(1024)}, u32[]{:S(2)}) copy-start(s32[4096]{0:T(1024)} %param.16) | copy-start | bytes 49156
  0.6 4.6 %copy-start.6 = (s32[4096]{0:T(1024)S(1)}, s32[4096]{0:T(1024)}, u32[]{:S(2)}) copy-start(s32[4096]{0:T(1024)} %param.17) | copy-start | bytes 49156
  0.7 4.6 %copy-start.7 = (s32[4096]{0:T(1024)S(1)}, s32[4096]{0:T(1024)}, u32[]{:S(2)}) copy-start(s32[4096]{0:T(1024)} %param.18) | copy-start | bytes 49156
  1.9 11.2 %collective-permute-start = (f32[45,8,128]{2,1,0:T(8,128)S(1)}, f32[45,8,128]{2,1,0:T(8,128)S(1)}, u32[]{:S(2)}, u32[]{:S(2)}) collective-permute-start(f32[45,8,128]{2,1,0:T(8,128)S(1)} %get-tuple-element.15), channel_id=1, source_target_pairs={{0,4},{8,12},{16,20},{24,28},{32,36},{40,44},{48,52},{56,60},{64,6... | collective-permute-start | bytes 552968 | tf_op jit(solution)/shard_map/ppermute | solution.py:423
  5.2 7.8 %collective-permute-start.1 = (f32[45,8,128]{2,1,0:T(8,128)S(1)}, f32[45,8,128]{2,1,0:T(8,128)S(1)}, u32[]{:S(2)}, u32[]{:S(2)}) collective-permute-start(f32[45,8,128]{2,1,0:T(8,128)S(1)} %get-tuple-element.16), channel_id=1, source_target_pairs={{4,8},{12,16},{20,24},{28,32},{36,40},{44,48},{52,56},{60,64},{68,... | collective-permute-start | bytes 552968 | tf_op jit(solution)/shard_map/ppermute | solution.py:423
  5.3 7.8 %copy-start = (f32[2,18,2,512]{3,2,1,0:T(2,128)S(1)}, f32[2,18,2,512]{3,2,1,0:T(2,128)}, u32[]{:S(2)}) copy-start(f32[2,18,2,512]{3,2,1,0:T(2,128)} %param.10) | copy-start | bytes 442372
  5.3 7.8 %copy-start.1 = (f32[18,2,512]{2,1,0:T(2,128)S(1)}, f32[18,2,512]{2,1,0:T(2,128)}, u32[]{:S(2)}) copy-start(f32[18,2,512]{2,1,0:T(2,128)} %param.11) | copy-start | bytes 221188
  5.3 7.8 %copy-start.2 = (f32[18,2,512]{2,1,0:T(2,128)S(1)}, f32[18,2,512]{2,1,0:T(2,128)}, u32[]{:S(2)}) copy-start(f32[18,2,512]{2,1,0:T(2,128)} %param.12) | copy-start | bytes 221188
  5.3 7.8 %copy-start.3 = (f32[2,2,512]{2,1,0:T(2,128)S(1)}, f32[2,2,512]{2,1,0:T(2,128)}, u32[]{:S(2)}) copy-start(f32[2,2,512]{2,1,0:T(2,128)} %param.13) | copy-start | bytes 24580
  13.4 20.2 %collective-permute-start.4 = (f32[40,8,128]{2,1,0:T(8,128)S(1)}, f32[40,8,128]{2,1,0:T(8,128)S(1)}, u32[]{:S(2)}, u32[]{:S(2)}) collective-permute-start(f32[40,8,128]{2,1,0:T(8,128)S(1)} %advect.1.x_ref.refs_0_), channel_id=1, source_target_pairs={{0,2},{1,3},{2,0},{3,1},{4,6},{5,7},{6,4},{7,5},{8,10},{9,11},{10,... | collective-permute-start | bytes 491528 | tf_op jit(solution)/shard_map/ppermute | solution.py:432
  19.4 14.2 %collective-permute-start.3 = (f32[40,8,128]{2,1,0:T(8,128)S(1)}, f32[40,8,128]{2,1,0:T(8,128)S(1)}, u32[]{:S(2)}, u32[]{:S(2)}) collective-permute-start(f32[40,8,128]{2,1,0:T(8,128)S(1)} %advect.1.x_ref.refs_0_), channel_id=1, source_target_pairs={{0,1},{1,2},{2,3},{3,0},{4,5},{5,6},{6,7},{7,4},{8,9},{9,10},{10,1... | collective-permute-start | bytes 491528 | tf_op jit(solution)/shard_map/ppermute | solution.py:432
  20.6 15.1 %collective-permute-start.2 = (f32[40,8,128]{2,1,0:T(8,128)S(1)}, f32[40,8,128]{2,1,0:T(8,128)S(1)}, u32[]{:S(2)}, u32[]{:S(2)}) collective-permute-start(f32[40,8,128]{2,1,0:T(8,128)S(1)} %advect.1.x_ref.refs_0_), channel_id=1, source_target_pairs={{0,3},{1,0},{2,1},{3,2},{4,7},{5,4},{6,5},{7,6},{8,11},{9,8},{10,9... | collective-permute-start | bytes 491528 | tf_op jit(solution)/shard_map/ppermute | solution.py:432
  23.6 12.0 %copy-start.4 = (f32[72,72]{1,0:T(8,128)S(1)}, f32[72,72]{1,0:T(8,128)}, u32[]{:S(2)}) copy-start(f32[72,72]{1,0:T(8,128)} %mix_ref.1) | copy-start | bytes 62212
  23.6 27.4 %all-to-all-start = ((f32[64,1,3712]{2,1,0:T(1,128)}), f32[64,1,3712]{2,1,0:T(1,128)S(1)}, u32[]{:S(2)}, u32[]{:S(2)}) async-start(f32[64,1,3712]{2,1,0:T(1,128)} %bitcast.26), calls=%async_computation | async-start | bytes 1900544 | tf_op jit(solution)/shard_map/all_to_all | solution.py:469
  67.9 7.3 %collective-permute-start.7 = (f32[8,8,128]{2,1,0:T(8,128)S(1)}, f32[8,8,128]{2,1,0:T(8,128)S(1)}, u32[]{:S(2)}, u32[]{:S(2)}) collective-permute-start(f32[8,8,128]{2,1,0:T(8,128)S(1)} %home.1.a_ref), channel_id=1, source_target_pairs={{0,2},{1,3},{2,0},{3,1},{4,6},{5,7},{6,4},{7,5},{8,10},{9,11},{10,... | collective-permute-start | bytes 98312 | tf_op jit(solution)/shard_map/ppermute | solution.py:432
  71.6 5.2 %collective-permute-start.6 = (f32[8,8,128]{2,1,0:T(8,128)S(1)}, f32[8,8,128]{2,1,0:T(8,128)S(1)}, u32[]{:S(2)}, u32[]{:S(2)}) collective-permute-start(f32[8,8,128]{2,1,0:T(8,128)S(1)} %home.1.a_ref), channel_id=1, source_target_pairs={{0,1},{1,2},{2,3},{3,0},{4,5},{5,6},{6,7},{7,4},{8,9},{9,10},{10,1... | collective-permute-start | bytes 98312 | tf_op jit(solution)/shard_map/ppermute | solution.py:432
  72.6 4.2 %collective-permute-start.5 = (f32[8,8,128]{2,1,0:T(8,128)S(1)}, f32[8,8,128]{2,1,0:T(8,128)S(1)}, u32[]{:S(2)}, u32[]{:S(2)}) collective-permute-start(f32[8,8,128]{2,1,0:T(8,128)S(1)} %home.1.a_ref), channel_id=1, source_target_pairs={{0,3},{1,0},{2,1},{3,2},{4,7},{5,4},{6,5},{7,6},{8,11},{9,8},{10,9... | collective-permute-start | bytes 98312 | tf_op jit(solution)/shard_map/ppermute | solution.py:432

commit v7 on v6

--- a/solution.py
+++ b/solution.py
@@ -230,7 +230,7 @@
     w_ref[37:38, :] = (col & 3).astype(F32)
     w_ref[38:40, :] = jnp.zeros((2, SND), F32)
 
-    quads, chunk = 16, 512
+    quads, chunk = 16, 1024
     sub, left = iota((SUBS, LANES), 0), iota((SUBS, LANES), 1) < 64
 
     def some(i):

time: 77.8 us -> 77.8 us (level)
  no operation moved by 1% of the time
where the time goes in v7:
time: 77.8 us; the launch traced here: 77.5 us
  starting transfers between devices  30.2 us (39%)
  waiting for transfers between devices  17.7 us (23%)
  Pallas kernels  15.7 us (20%)
  blocking collectives  12.3 us (16%)
  between operations  1.47 us (2%)
    ppermute x6, starting transfers between devices, shift(): lax.ppermute(x, axis, [(i, (i + distance) % size) for i in range(size)])  16.9 us
    all_to_all x1, waiting for transfers between devices, body(): lax.all_to_all(send.reshape(TILES, 1, MESSAGE * LANES), 'tile', 0, 0, til...  14.1 us
    all_to_all x1, blocking collectives, body(): lax.all_to_all(sums.reshape(TILES, 1, 3 * LANES), 'tile', 0, 0, tiled=True)  12.3 us
    all_to_all x1, starting transfers between devices, body(): lax.all_to_all(send.reshape(TILES, 1, MESSAGE * LANES), 'tile', 0, 0, til...  9.97 us
    pallas_call x1, Pallas kernels, body(): call(send_kernel, [arr((TILES * MESSAGE, LANES)), arr((1, SND), jnp.int32...  7.76 us
    ppermute x6, waiting for transfers between devices, shift(): lax.ppermute(x, axis, [(i, (i + distance) % size) for i in range(size)])  3.63 us
    pallas_call x1, Pallas kernels, body(): call(sample_kernel, arr((3 * TILES, LANES)), [spec()] * 2, [pltpu.VMEM((8...  3.45 us
    ppermute x2, starting transfers between devices, swapped(): return lax.ppermute(x, 'tile', pairs + [(b, a) for a, b in pairs])  3.33 us
  transfers between devices with their start and end apart: 9, of which 3 were waited for; matrix products, arithmetic and copies ran while one was open for 0% of the time, Pallas kernels for 2%

profile of v7, /device:TPU:1, one launch (start us, length us, event | category | flops | bytes accessed | tf_op | source)
XLA Modules:
  0.0 77.5 jit_solution(13117237572444232359)
XLA Ops:
  0.6 0.0 copy-start.5
  0.6 0.0 copy-start.6
  0.7 0.0 copy-start.7
  0.7 1.2 %halo.1 = (f32[45,8,128]{2,1,0:T(8,128)S(1)}, f32[45,8,128]{2,1,0:T(8,128)S(1)}, f32[36,8,128]{2,1,0:T(8,128)S(1)}) custom-call(f32[36,8,128]{2,1,0:T(8,128)} %bitcast.33, f32[18,8,128]{2,1,0:T(8,128)} %bitcast.37, f32[18,8,128]{2,1,0:T(8,128)} %bitcast.39, f32[2,8,128]{2,1,0:T(8,128)} %bitcast.41), custom_call_target="tpu_custom_call" | custom-call | flops 1000000 | bytes 100000 | tf_op jit(solution)/shard_map/halo/pallas_call | solution.py:439
  1.9 3.3 %collective-permute-start = (f32[45,8,128]{2,1,0:T(8,128)S(1)}, f32[45,8,128]{2,1,0:T(8,128)S(1)}, u32[]{:S(2)}, u32[]{:S(2)}) collective-permute-start(f32[45,8,128]{2,1,0:T(8,128)S(1)} %get-tuple-element.15), channel_id=1, source_target_pairs={{0,4},{8,12},{16,20},{24,28},{32,36},{40,44},{48,52},{56,60},{64,6... | collective-permute-start | bytes 552968 | tf_op jit(solution)/shard_map/ppermute | solution.py:423
  5.2 0.0 collective-permute-start.1
  5.2 0.0 copy-done.5
  5.2 0.0 copy-done.6
  5.3 0.0 copy-done.7
  5.3 0.0 copy-start
  5.3 0.0 copy-start.1
  5.3 0.0 copy-start.2
  5.3 0.0 copy-start.3
  5.3 7.8 %send.1 = (f32[1856,128]{1,0:T(8,128)}, s32[1,4096]{1,0:T(1,128)S(1)}, f32[4,8,128]{2,1,0:T(8,128)S(1)}) custom-call(f32[18,4096]{1,0:T(8,128)} %kern_in.1, s32[1,4096]{1,0:T(1,128)S(1)} %bitcast.43, s32[1,4096]{1,0:T(1,128)S(1)} %bitcast.44, s32[1,4096]{1,0:T(1,128)S(1)} %bitcast.45, f32[36,8,128]{2,1,0:T(8,128)S(1)} %get-tuple-element.13.part_ref), custom_call_target="tpu_custom_call" | custom-call | flops 8999999488 | bytes 100000 | tf_op jit(solution)/shard_map/send/pallas_call | solution.py:453
  13.1 0.0 collective-permute-done.near_ref
  13.1 0.0 collective-permute-done.1.far_ref
  13.1 0.0 copy-done
  13.1 0.0 copy-done.1
  13.1 0.0 copy-done.2
  13.1 0.0 copy-done.3
  13.1 0.3 advect.1.x_ref.refs_0_
  13.4 6.0 %collective-permute-start.4 = (f32[40,8,128]{2,1,0:T(8,128)S(1)}, f32[40,8,128]{2,1,0:T(8,128)S(1)}, u32[]{:S(2)}, u32[]{:S(2)}) collective-permute-start(f32[40,8,128]{2,1,0:T(8,128)S(1)} %advect.1.x_ref.refs_0_), channel_id=1, source_target_pairs={{0,2},{1,3},{2,0},{3,1},{4,6},{5,7},{6,4},{7,5},{8,10},{9,11},{10,... | collective-permute-start | bytes 491528 | tf_op jit(solution)/shard_map/ppermute | solution.py:432
  19.4 1.2 %collective-permute-start.3 = (f32[40,8,128]{2,1,0:T(8,128)S(1)}, f32[40,8,128]{2,1,0:T(8,128)S(1)}, u32[]{:S(2)}, u32[]{:S(2)}) collective-permute-start(f32[40,8,128]{2,1,0:T(8,128)S(1)} %advect.1.x_ref.refs_0_), channel_id=1, source_target_pairs={{0,1},{1,2},{2,3},{3,0},{4,5},{5,6},{6,7},{7,4},{8,9},{9,10},{10,1... | collective-permute-start | bytes 491528 | tf_op jit(solution)/shard_map/ppermute | solution.py:432
  20.6 2.4 %collective-permute-start.2 = (f32[40,8,128]{2,1,0:T(8,128)S(1)}, f32[40,8,128]{2,1,0:T(8,128)S(1)}, u32[]{:S(2)}, u32[]{:S(2)}) collective-permute-start(f32[40,8,128]{2,1,0:T(8,128)S(1)} %advect.1.x_ref.refs_0_), channel_id=1, source_target_pairs={{0,3},{1,0},{2,1},{3,2},{4,7},{5,4},{6,5},{7,6},{8,11},{9,8},{10,9... | collective-permute-start | bytes 491528 | tf_op jit(solution)/shard_map/ppermute | solution.py:432
  23.6 0.0 copy-start.4
  23.6 10.0 %all-to-all-start = ((f32[64,1,3712]{2,1,0:T(1,128)}), f32[64,1,3712]{2,1,0:T(1,128)S(1)}, u32[]{:S(2)}, u32[]{:S(2)}) async-start(f32[64,1,3712]{2,1,0:T(1,128)} %bitcast.26), calls=%async_computation | async-start | bytes 1900544 | tf_op jit(solution)/shard_map/all_to_all | solution.py:469
  33.6 0.0 collective-permute-done.4.refs_3_
  33.6 0.0 collective-permute-done.3.refs_2_
  33.6 2.0 %collective-permute-done.2.refs_1_ = f32[40,8,128]{2,1,0:T(8,128)S(1)} collective-permute-done((f32[40,8,128]{2,1,0:T(8,128)S(1)}, f32[40,8,128]{2,1,0:T(8,128)S(1)}, u32[]{:S(2)}, u32[]{:S(2)}) %collective-permute-start.2) | collective-permute-done | bytes 163872 | tf_op jit(solution)/shard_map/ppermute | solution.py:432
  35.6 0.0 copy-done.4
  35.6 1.3 %mix.1 = (f32[36,8,128]{2,1,0:T(8,128)}, f32[8,2,24,128]{3,2,1,0:T(8,128)S(1)}, f32[4,8,128]{2,1,0:T(8,128)S(1)}) custom-call(s32[1]{0:T(128)S(6)} %copy.24.count_ref, f32[72,72]{1,0:T(8,128)S(1)} %copy-done.4, f32[8,128]{1,0:T(8,128)S(1)} %mark.1.mark_ref, f32[40,8,128]{2,1,0:T(8,128)S(1)} %advect.1.x_ref.refs_0_, ...), custom_call_target="tpu_custom_call" | custom-call | flops 99999997952 | bytes 100000 | tf_op jit(solution)/shard_map/mix/pallas_call | solution.py:471
  36.9 14.1 %all-to-all-done = f32[64,1,3712]{2,1,0:T(1,128)S(1)} async-done(((f32[64,1,3712]{2,1,0:T(1,128)}), f32[64,1,3712]{2,1,0:T(1,128)S(1)}, u32[]{:S(2)}, u32[]{:S(2)}) %all-to-all-start) | async-done | bytes 950304 | tf_op jit(solution)/shard_map/all_to_all | solution.py:469
  51.0 3.5 %sample.1 = f32[192,128]{1,0:T(8,128)S(1)} custom-call(f32[1856,128]{1,0:T(8,128)S(1)} %bitcast.32, f32[8,2,24,128]{3,2,1,0:T(8,128)S(1)} %get-tuple-element.21.field_ref), custom_call_target="tpu_custom_call" | custom-call | flops 1000000 | bytes 100000 | tf_op jit(solution)/shard_map/sample/pallas_call | solution.py:478
  54.5 12.3 %all_to_all.10 = f32[64,1,384]{2,1,0:T(1,128)S(1)} all-to-all(f32[64,1,384]{2,1,0:T(1,128)S(1)} %bitcast.36), channel_id=1, replica_groups=mesh['tile'=64,'lev'=4] {'tile'}, dimensions={0} | all-to-all | bytes 196608 | tf_op jit(solution)/shard_map/all_to_all | solution.py:486
  66.8 1.1 %home.1.a_ref = f32[8,8,128]{2,1,0:T(8,128)S(1)} custom-call(f32[192,128]{1,0:T(8,128)S(1)} %bitcast.35, s32[1,4096]{1,0:T(1,128)S(1)} %get-tuple-element.22.place_ref), custom_call_target="tpu_custom_call" | custom-call | flops 1000000 | bytes 100000 | tf_op jit(solution)/shard_map/home/pallas_call | solution.py:488
  67.9 3.8 %collective-permute-start.7 = (f32[8,8,128]{2,1,0:T(8,128)S(1)}, f32[8,8,128]{2,1,0:T(8,128)S(1)}, u32[]{:S(2)}, u32[]{:S(2)}) collective-permute-start(f32[8,8,128]{2,1,0:T(8,128)S(1)} %home.1.a_ref), channel_id=1, source_target_pairs={{0,2},{1,3},{2,0},{3,1},{4,6},{5,7},{6,4},{7,5},{8,10},{9,11},{10,... | collective-permute-start | bytes 98312 | tf_op jit(solution)/shard_map/ppermute | solution.py:432
  71.6 1.0 %collective-permute-start.6 = (f32[8,8,128]{2,1,0:T(8,128)S(1)}, f32[8,8,128]{2,1,0:T(8,128)S(1)}, u32[]{:S(2)}, u32[]{:S(2)}) collective-permute-start(f32[8,8,128]{2,1,0:T(8,128)S(1)} %home.1.a_ref), channel_id=1, source_target_pairs={{0,1},{1,2},{2,3},{3,0},{4,5},{5,6},{6,7},{7,4},{8,9},{9,10},{10,1... | collective-permute-start | bytes 98312 | tf_op jit(solution)/shard_map/ppermute | solution.py:432
  72.6 2.6 %collective-permute-start.5 = (f32[8,8,128]{2,1,0:T(8,128)S(1)}, f32[8,8,128]{2,1,0:T(8,128)S(1)}, u32[]{:S(2)}, u32[]{:S(2)}) collective-permute-start(f32[8,8,128]{2,1,0:T(8,128)S(1)} %home.1.a_ref), channel_id=1, source_target_pairs={{0,3},{1,0},{2,1},{3,2},{4,7},{5,4},{6,5},{7,6},{8,11},{9,8},{10,9... | collective-permute-start | bytes 98312 | tf_op jit(solution)/shard_map/ppermute | solution.py:432
  75.2 0.0 collective-permute-done.7.c_ref
  75.2 1.6 %collective-permute-done.6.d_ref = f32[8,8,128]{2,1,0:T(8,128)S(1)} collective-permute-done((f32[8,8,128]{2,1,0:T(8,128)S(1)}, f32[8,8,128]{2,1,0:T(8,128)S(1)}, u32[]{:S(2)}, u32[]{:S(2)}) %collective-permute-start.6) | collective-permute-done | bytes 32800 | tf_op jit(solution)/shard_map/ppermute | solution.py:432
  76.8 0.0 collective-permute-done.5.b_ref
  76.8 0.6 last.1
  (1 shorter events, 0.0 us)
Async XLA Ops:
  0.6 4.6 %copy-start.5 = (s32[4096]{0:T(1024)S(1)}, s32[4096]{0:T(1024)}, u32[]{:S(2)}) copy-start(s32[4096]{0:T(1024)} %param.16) | copy-start | bytes 49156
  0.6 4.6 %copy-start.6 = (s32[4096]{0:T(1024)S(1)}, s32[4096]{0:T(1024)}, u32[]{:S(2)}) copy-start(s32[4096]{0:T(1024)} %param.17) | copy-start | bytes 49156
  0.7 4.6 %copy-start.7 = (s32[4096]{0:T(1024)S(1)}, s32[4096]{0:T(1024)}, u32[]{:S(2)}) copy-start(s32[4096]{0:T(1024)} %param.18) | copy-start | bytes 49156
  1.9 11.2 %collective-permute-start = (f32[45,8,128]{2,1,0:T(8,128)S(1)}, f32[45,8,128]{2,1,0:T(8,128)S(1)}, u32[]{:S(2)}, u32[]{:S(2)}) collective-permute-start(f32[45,8,128]{2,1,0:T(8,128)S(1)} %get-tuple-element.15), channel_id=1, source_target_pairs={{0,4},{8,12},{16,20},{24,28},{32,36},{40,44},{48,52},{56,60},{64,6... | collective-permute-start | bytes 552968 | tf_op jit(solution)/shard_map/ppermute | solution.py:423
  5.2 7.8 %collective-permute-start.1 = (f32[45,8,128]{2,1,0:T(8,128)S(1)}, f32[45,8,128]{2,1,0:T(8,128)S(1)}, u32[]{:S(2)}, u32[]{:S(2)}) collective-permute-start(f32[45,8,128]{2,1,0:T(8,128)S(1)} %get-tuple-element.16), channel_id=1, source_target_pairs={{4,8},{12,16},{20,24},{28,32},{36,40},{44,48},{52,56},{60,64},{68,... | collective-permute-start | bytes 552968 | tf_op jit(solution)/shard_map/ppermute | solution.py:423
  5.3 7.8 %copy-start = (f32[2,18,2,512]{3,2,1,0:T(2,128)S(1)}, f32[2,18,2,512]{3,2,1,0:T(2,128)}, u32[]{:S(2)}) copy-start(f32[2,18,2,512]{3,2,1,0:T(2,128)} %param.10) | copy-start | bytes 442372
  5.3 7.8 %copy-start.1 = (f32[18,2,512]{2,1,0:T(2,128)S(1)}, f32[18,2,512]{2,1,0:T(2,128)}, u32[]{:S(2)}) copy-start(f32[18,2,512]{2,1,0:T(2,128)} %param.11) | copy-start | bytes 221188
  5.3 7.8 %copy-start.2 = (f32[18,2,512]{2,1,0:T(2,128)S(1)}, f32[18,2,512]{2,1,0:T(2,128)}, u32[]{:S(2)}) copy-start(f32[18,2,512]{2,1,0:T(2,128)} %param.12) | copy-start | bytes 221188
  5.3 7.8 %copy-start.3 = (f32[2,2,512]{2,1,0:T(2,128)S(1)}, f32[2,2,512]{2,1,0:T(2,128)}, u32[]{:S(2)}) copy-start(f32[2,2,512]{2,1,0:T(2,128)} %param.13) | copy-start | bytes 24580
  13.4 20.2 %collective-permute-start.4 = (f32[40,8,128]{2,1,0:T(8,128)S(1)}, f32[40,8,128]{2,1,0:T(8,128)S(1)}, u32[]{:S(2)}, u32[]{:S(2)}) collective-permute-start(f32[40,8,128]{2,1,0:T(8,128)S(1)} %advect.1.x_ref.refs_0_), channel_id=1, source_target_pairs={{0,2},{1,3},{2,0},{3,1},{4,6},{5,7},{6,4},{7,5},{8,10},{9,11},{10,... | collective-permute-start | bytes 491528 | tf_op jit(solution)/shard_map/ppermute | solution.py:432
  19.4 14.2 %collective-permute-start.3 = (f32[40,8,128]{2,1,0:T(8,128)S(1)}, f32[40,8,128]{2,1,0:T(8,128)S(1)}, u32[]{:S(2)}, u32[]{:S(2)}) collective-permute-start(f32[40,8,128]{2,1,0:T(8,128)S(1)} %advect.1.x_ref.refs_0_), channel_id=1, source_target_pairs={{0,1},{1,2},{2,3},{3,0},{4,5},{5,6},{6,7},{7,4},{8,9},{9,10},{10,1... | collective-permute-start | bytes 491528 | tf_op jit(solution)/shard_map/ppermute | solution.py:432
  20.6 15.1 %collective-permute-start.2 = (f32[40,8,128]{2,1,0:T(8,128)S(1)}, f32[40,8,128]{2,1,0:T(8,128)S(1)}, u32[]{:S(2)}, u32[]{:S(2)}) collective-permute-start(f32[40,8,128]{2,1,0:T(8,128)S(1)} %advect.1.x_ref.refs_0_), channel_id=1, source_target_pairs={{0,3},{1,0},{2,1},{3,2},{4,7},{5,4},{6,5},{7,6},{8,11},{9,8},{10,9... | collective-permute-start | bytes 491528 | tf_op jit(solution)/shard_map/ppermute | solution.py:432
  23.6 12.0 %copy-start.4 = (f32[72,72]{1,0:T(8,128)S(1)}, f32[72,72]{1,0:T(8,128)}, u32[]{:S(2)}) copy-start(f32[72,72]{1,0:T(8,128)} %mix_ref.1) | copy-start | bytes 62212
  23.6 27.4 %all-to-all-start = ((f32[64,1,3712]{2,1,0:T(1,128)}), f32[64,1,3712]{2,1,0:T(1,128)S(1)}, u32[]{:S(2)}, u32[]{:S(2)}) async-start(f32[64,1,3712]{2,1,0:T(1,128)} %bitcast.26), calls=%async_computation | async-start | bytes 1900544 | tf_op jit(solution)/shard_map/all_to_all | solution.py:469
  67.9 7.3 %collective-permute-start.7 = (f32[8,8,128]{2,1,0:T(8,128)S(1)}, f32[8,8,128]{2,1,0:T(8,128)S(1)}, u32[]{:S(2)}, u32[]{:S(2)}) collective-permute-start(f32[8,8,128]{2,1,0:T(8,128)S(1)} %home.1.a_ref), channel_id=1, source_target_pairs={{0,2},{1,3},{2,0},{3,1},{4,6},{5,7},{6,4},{7,5},{8,10},{9,11},{10,... | collective-permute-start | bytes 98312 | tf_op jit(solution)/shard_map/ppermute | solution.py:432
  71.6 5.2 %collective-permute-start.6 = (f32[8,8,128]{2,1,0:T(8,128)S(1)}, f32[8,8,128]{2,1,0:T(8,128)S(1)}, u32[]{:S(2)}, u32[]{:S(2)}) collective-permute-start(f32[8,8,128]{2,1,0:T(8,128)S(1)} %home.1.a_ref), channel_id=1, source_target_pairs={{0,1},{1,2},{2,3},{3,0},{4,5},{5,6},{6,7},{7,4},{8,9},{9,10},{10,1... | collective-permute-start | bytes 98312 | tf_op jit(solution)/shard_map/ppermute | solution.py:432
  72.6 4.2 %collective-permute-start.5 = (f32[8,8,128]{2,1,0:T(8,128)S(1)}, f32[8,8,128]{2,1,0:T(8,128)S(1)}, u32[]{:S(2)}, u32[]{:S(2)}) collective-permute-start(f32[8,8,128]{2,1,0:T(8,128)S(1)} %home.1.a_ref), channel_id=1, source_target_pairs={{0,3},{1,0},{2,1},{3,2},{4,7},{5,4},{6,5},{7,6},{8,11},{9,8},{10,9... | collective-permute-start | bytes 98312 | tf_op jit(solution)/shard_map/ppermute | solution.py:432
